TPU v7x, 128 devices: a whole 4x4x4 slice. The times are simulated.
128 devices in a mesh: gx: 16 (over x, z), gy: 8 (over y, core).
Axes of the slice: x: 4, y: 4, z: 4, core: 2. Of those that a mesh axis runs over, the one named last changes fastest.
Arguments:
- test_vectors: float32 [48, 64, 128, 128], P(None, 'gx', 'gy'), may hold values from -6 to 6
- coef_x: float32 [64, 128, 128], P('gx', 'gy'), may hold values from 0.3 to 3
- coef_y: float32 [64, 128, 128], P('gx', 'gy'), may hold values from 0.3 to 3
- coef_z: float32 [64, 128, 128], P('gx', 'gy'), may hold values from 0.05 to 0.5
- shift: float32 [64, 128, 128], P('gx', 'gy'), may hold values from 0.1 to 1
- cf_split: int32 [64, 128, 1], P('gx', 'gy'), may hold values from 0 to 1, as said below
- nbr_count: int32 [64, 128, 1], P('gx', 'gy'), may hold values from 1 to 4, as said below
- nbr_owner: int32 [64, 128, 1, 4], P('gx', 'gy'), may hold values from 0 to 127, as said below
- nbr_block: int32 [64, 128, 1, 4], P('gx', 'gy'), may hold values from 0 to 63, as said below
Outputs:
- smoothed: float32 [48, 64, 128, 128], P(None, 'gx', 'gy')
- interp_weights: float32 [4, 64, 128, 128], P(None, 'gx', 'gy')
Inputs may be any that keep to these rules, and one draw needn't show every extreme that they name: `cf_split`: each device holds exactly 16 C blocks. Only the first nbr_count slots of an F block are live; the other slots, and all slots of C blocks, are filler. `nbr_owner`: owner ids are i * 8 + j for the mesh position (i, j). Among the live slots of one device's blocks at most 2 name the same owner, and in every draw some owner is named by exactly 2 live slots of every device. `nbr_block`: A live slot names a C block of its owner.
All inputs are finite; a program needn't handle non-finite values.
Results may differ from a plain program's by a relative error of at most 0.0039.
Values may be sent and summed in bfloat16 or wider, within the bound.
A program may use at most 64 MiB of HBM per device.

v0:
```python
import jax
import jax.numpy as jnp
from jax import lax
from jax.sharding import PartitionSpec as P

SLOTS = 4
SWEEPS = 3
BLOCK_ROWS = 128


OMEGA = 0.8
RIDGE = 0.05


def extended(value, sides, width):
    for axis, dim in sides:
        size, length = (lax.axis_size(axis), value.shape[dim])
        up = [(i, (i + 1) % size) for i in range(size - 1)]
        down = [(j, i) for i, j in up]
        last = lax.slice_in_dim(value, length - width, length, axis=dim)
        leading = lax.slice_in_dim(value, 0, width, axis=dim)
        before = lax.ppermute(last, axis, up)
        after = lax.ppermute(leading, axis, down)
        value = jnp.concatenate([before, value, after], axis=dim)
    return value


def couple(padded, weight_x, weight_y, weight_z):
    along_x = padded[:, 2:, 1:-1, 1:-1] + padded[:, :-2, 1:-1, 1:-1]
    along_y = padded[:, 1:-1, 2:, 1:-1] + padded[:, 1:-1, :-2, 1:-1]
    along_z = padded[:, 1:-1, 1:-1, 2:] + padded[:, 1:-1, 1:-1, :-2]
    return weight_x * along_x + weight_y * along_y + weight_z * along_z


def relax_step(values, summed, diagonal):
    return (1.0 - OMEGA) * values + OMEGA * (summed / diagonal)


def solve_small(gram_rows, right_side):
    extent = len(right_side)
    factor = [[None] * extent for unused in range(extent)]
    for row_at in range(extent):
        for col_at in range(row_at + 1):
            residual_sum = gram_rows[row_at][col_at]
            for mid_at in range(col_at):
                residual_sum = residual_sum - factor[row_at][mid_at] * factor[col_at][mid_at]
            if row_at == col_at:
                factor[row_at][row_at] = jnp.sqrt(residual_sum)
            else:
                factor[row_at][col_at] = residual_sum / factor[col_at][col_at]
    forward = []
    for row_at in range(extent):
        residual_sum = right_side[row_at]
        for mid_at in range(row_at):
            residual_sum = residual_sum - factor[row_at][mid_at] * forward[mid_at]
        forward.append(residual_sum / factor[row_at][row_at])
    result = [None] * extent
    for row_at in reversed(range(extent)):
        residual_sum = forward[row_at]
        for mid_at in range(row_at + 1, extent):
            residual_sum = residual_sum - factor[mid_at][row_at] * result[mid_at]
        result[row_at] = residual_sum / factor[row_at][row_at]
    return result


def vector_sum(first_part, second_part):
    return jnp.sum(first_part.astype(jnp.float32) * second_part.astype(jnp.float32), axis=0)


def per_device(
    test_vectors, coef_x, coef_y, coef_z, shift, cf_split, nbr_count, nbr_owner, nbr_block
):
    vector_count = test_vectors.shape[0]
    cells_x = test_vectors.shape[1]
    cells_y = test_vectors.shape[2]
    depth_dev = test_vectors.shape[3]
    diagonal = 2.0 * (coef_x + coef_y + coef_z) + shift
    vectors = test_vectors
    for repeat in range(SWEEPS):
        padded = extended(vectors, (("gx", 1), ("gy", 2)), 1)
        padded = jnp.pad(padded, ((0, 0), (0, 0), (0, 0), (1, 1)))
        vectors = relax_step(vectors, couple(padded, coef_x, coef_y, coef_z), diagonal)
    rounded = vectors.astype(jnp.bfloat16)
    zblocks = depth_dev // BLOCK_ROWS
    blocks_dev = cells_x * cells_y * zblocks
    fine_leading = rounded.reshape(vector_count, blocks_dev, BLOCK_ROWS)
    local_blocks = jnp.transpose(fine_leading, (1, 0, 2))
    grid_x_dev = lax.axis_size("gx")
    grid_y_dev = lax.axis_size("gy")
    devices = grid_x_dev * grid_y_dev
    capacity = max(2, blocks_dev * SLOTS // devices)
    entries = blocks_dev * SLOTS
    slot_ids = jnp.arange(SLOTS)
    is_live = ((cf_split == 0)[..., None] & (slot_ids < nbr_count[..., None])).reshape(entries)
    owner_ids = nbr_owner.reshape(entries)
    local_ids = nbr_block.reshape(entries)
    member = ((owner_ids[:, None] == jnp.arange(devices)[None, :]) & is_live[:, None]).astype(
        jnp.bfloat16
    )
    earlier = (jnp.arange(entries)[:, None] >= jnp.arange(entries)[None, :]).astype(jnp.bfloat16)
    running = jnp.dot(earlier, member, preferred_element_type=jnp.float32)
    position = (jnp.sum(running * member, axis=1) - 1.0).astype(jnp.int32)
    target = jnp.where(is_live, owner_ids * capacity + position, devices * capacity)
    request_table = (
        jnp.zeros((devices * capacity,), jnp.int32).at[target].set(local_ids, mode="drop")
    )
    found_rows = local_blocks[
        lax.all_to_all(
            request_table.reshape(devices, capacity),
            ("gx", "gy"),
            split_axis=0,
            concat_axis=0,
            tiled=True,
        )
    ]
    replies = lax.all_to_all(found_rows, ("gx", "gy"), split_axis=0, concat_axis=0, tiled=True)
    replies = replies.reshape(devices * capacity, vector_count, BLOCK_ROWS)
    coarse = replies[jnp.minimum(target, devices * capacity - 1)]
    coarse = jnp.where(is_live[:, None, None], coarse, jnp.zeros((), jnp.bfloat16))
    coarse_leading = jnp.transpose(
        coarse.reshape(blocks_dev, SLOTS, vector_count, BLOCK_ROWS), (2, 1, 0, 3)
    )
    pair_sums = {}
    for first in range(SLOTS):
        for second in range(first + 1):
            pair_sums[first, second] = (
                vector_sum(coarse_leading[:, first], coarse_leading[:, second]) / vector_count
            )
    gram_rows = [
        [
            pair_sums[max(first, second), min(first, second)] + (RIDGE if first == second else 0.0)
            for second in range(SLOTS)
        ]
        for first in range(SLOTS)
    ]
    rhs_rows = [
        vector_sum(coarse_leading[:, first], fine_leading) / vector_count for first in range(SLOTS)
    ]
    weights = solve_small(gram_rows, rhs_rows)
    interp_weights = jnp.stack(weights, 0).reshape(SLOTS, cells_x, cells_y, depth_dev)
    return (vectors, interp_weights)


def solution(mesh):
    in_specs = (
        P(None, "gx", "gy", None),
        P("gx", "gy", None),
        P("gx", "gy", None),
        P("gx", "gy", None),
        P("gx", "gy", None),
        P("gx", "gy", None),
        P("gx", "gy", None),
        P("gx", "gy", None, None),
        P("gx", "gy", None, None),
    )
    out_specs = (P(None, "gx", "gy", None), P(None, "gx", "gy", None))
    return jax.shard_map(
        per_device, mesh=mesh, in_specs=in_specs, out_specs=out_specs, check_vma=False
    )
```

profile of v0, /device:TPU:1, one launch (start us, length us, event | category | flops | bytes accessed | tf_op | source)
XLA Modules:
  0.0 164.6 jit_solution(4212923767895226337)
XLA Ops:
  0.6 2.3 %copy.16 = f32[48,4,16,128]{3,0,2,1:T(8,128)S(1)} copy(f32[48,4,16,128]{3,2,1,0:T(8,128)} %param.9) | data formatting | bytes 3145728 | tf_op args[0]
  3.0 0.1 fusion.62
  3.0 4.5 %collective-permute-start.1 = (f32[48,1,16,128]{3,0,2,1:T(8,128)S(1)}, f32[48,1,16,128]{3,0,2,1:T(8,128)S(1)}, u32[]{:S(2)}, u32[]{:S(2)}) collective-permute-start(f32[48,1,16,128]{3,0,2,1:T(8,128)S(1)} %get-tuple-element.39), channel_id=1, source_target_pairs={{0,8},{8,16},{16,24},{24,32},{32,40},{40,48},{48,56},{56,64},{64,7... | collective-permute-start | bytes 1179656 | tf_op jit(solution)/shard_map/ppermute | solution.py:22
  7.6 1.3 collective-permute-start
  8.9 6.4 %collective-permute-done.1 = f32[48,1,16,128]{3,0,2,1:T(8,128)S(1)} collective-permute-done((f32[48,1,16,128]{3,0,2,1:T(8,128)S(1)}, f32[48,1,16,128]{3,0,2,1:T(8,128)S(1)}, u32[]{:S(2)}, u32[]{:S(2)}) %collective-permute-start.1) | collective-permute-done | bytes 393248 | tf_op jit(solution)/shard_map/ppermute | solution.py:22
  15.4 0.0 copy-start.8
  15.4 0.0 copy-start.11
  15.4 0.9 constant_dynamic-update-slice_fusion.1
  16.3 3.2 %collective-permute-done = f32[48,1,16,128]{3,0,2,1:T(8,128)S(1)} collective-permute-done((f32[48,1,16,128]{3,0,2,1:T(8,128)S(1)}, f32[48,1,16,128]{3,0,2,1:T(8,128)S(1)}, u32[]{:S(2)}, u32[]{:S(2)}) %collective-permute-start) | collective-permute-done | bytes 393248 | tf_op jit(solution)/shard_map/ppermute | solution.py:23
  19.5 3.6 %collective-permute-start.2 = (f32[48,6,1,128]{3,0,2,1:T(8,128)S(1)}, f32[48,6,1,128]{3,0,2,1:T(8,128)S(1)}, u32[]{:S(2)}, u32[]{:S(2)}) collective-permute-start(f32[48,6,1,128]{3,0,2,1:T(8,128)S(1)} %get-tuple-element.33), channel_id=1, source_target_pairs={{1,0},{2,1},{3,2},{4,3},{5,4},{6,5},{7,6},{9,8},{10,9},{11,10},{12... | collective-permute-start | bytes 442376 | tf_op jit(solution)/shard_map/ppermute | solution.py:23
  23.1 3.1 %collective-permute-start.3 = (f32[48,6,1,128]{3,0,2,1:T(8,128)S(1)}, f32[48,6,1,128]{3,0,2,1:T(8,128)S(1)}, u32[]{:S(2)}, u32[]{:S(2)}) collective-permute-start(f32[48,6,1,128]{3,0,2,1:T(8,128)S(1)} %get-tuple-element.32), channel_id=1, source_target_pairs={{0,1},{1,2},{2,3},{3,4},{4,5},{5,6},{6,7},{8,9},{9,10},{10,11},{11... | collective-permute-start | bytes 442376 | tf_op jit(solution)/shard_map/ppermute | solution.py:22
  26.3 0.8 collective-permute-done.2
  27.1 1.2 collective-permute-done.3
  28.3 2.2 %select_maximum_fusion.8 = f32[48,6,18,130]{3,0,2,1:T(8,128)S(1)} fusion(f32[48,6,1,128]{3,0,2,1:T(8,128)S(1)} %collective-permute-done.2, f32[48,6,16,128]{3,0,2,1:T(8,128)S(1)} %constant_dynamic-update-slice_fusion, f32[48,6,1,128]{3,0,2,1:T(8,128)S(1)} %collective-permute-done.3), kind=kLoop, calls=%fused_computation.13 | loop fusion | flops 5391360 | bytes 5349888 | tf_op jit(solution)/shard_map/concatenate | solution.py:24
  30.5 1.6 fusion.40
  32.2 0.0 copy-start.21
  32.2 0.1 fusion.61
  32.3 0.0 copy-start.20
  32.3 1.3 collective-permute-start.4
  33.6 4.0 %collective-permute-start.5 = (f32[48,1,16,128]{3,0,2,1:T(8,128)S(1)}, f32[48,1,16,128]{3,0,2,1:T(8,128)S(1)}, u32[]{:S(2)}, u32[]{:S(2)}) collective-permute-start(f32[48,1,16,128]{3,0,2,1:T(8,128)S(1)} %get-tuple-element.36), channel_id=1, source_target_pairs={{0,8},{8,16},{16,24},{24,32},{32,40},{40,48},{48,56},{56,64},{64,7... | collective-permute-start | bytes 1179656 | tf_op jit(solution)/shard_map/ppermute | solution.py:22
  37.6 0.6 fusion.56
  38.2 5.5 %collective-permute-done.4 = f32[48,1,16,128]{3,0,2,1:T(8,128)S(1)} collective-permute-done((f32[48,1,16,128]{3,0,2,1:T(8,128)S(1)}, f32[48,1,16,128]{3,0,2,1:T(8,128)S(1)}, u32[]{:S(2)}, u32[]{:S(2)}) %collective-permute-start.4) | collective-permute-done | bytes 393248 | tf_op jit(solution)/shard_map/ppermute | solution.py:23
  43.7 1.8 %collective-permute-done.5 = f32[48,1,16,128]{3,0,2,1:T(8,128)S(1)} collective-permute-done((f32[48,1,16,128]{3,0,2,1:T(8,128)S(1)}, f32[48,1,16,128]{3,0,2,1:T(8,128)S(1)}, u32[]{:S(2)}, u32[]{:S(2)}) %collective-permute-start.5) | collective-permute-done | bytes 393248 | tf_op jit(solution)/shard_map/ppermute | solution.py:22
  45.5 1.9 %collective-permute-start.6 = (f32[48,6,1,128]{3,0,2,1:T(8,128)S(1)}, f32[48,6,1,128]{3,0,2,1:T(8,128)S(1)}, u32[]{:S(2)}, u32[]{:S(2)}) collective-permute-start(f32[48,6,1,128]{3,0,2,1:T(8,128)S(1)} %get-tuple-element.31), channel_id=1, source_target_pairs={{1,0},{2,1},{3,2},{4,3},{5,4},{6,5},{7,6},{9,8},{10,9},{11,10},{12... | collective-permute-start | bytes 442376 | tf_op jit(solution)/shard_map/ppermute | solution.py:23
  47.4 4.5 %collective-permute-start.7 = (f32[48,6,1,128]{3,0,2,1:T(8,128)S(1)}, f32[48,6,1,128]{3,0,2,1:T(8,128)S(1)}, u32[]{:S(2)}, u32[]{:S(2)}) collective-permute-start(f32[48,6,1,128]{3,0,2,1:T(8,128)S(1)} %get-tuple-element.30), channel_id=1, source_target_pairs={{0,1},{1,2},{2,3},{3,4},{4,5},{5,6},{6,7},{8,9},{9,10},{10,11},{11... | collective-permute-start | bytes 442376 | tf_op jit(solution)/shard_map/ppermute | solution.py:22
  52.0 0.1 fusion.52
  52.0 0.1 copy.23
  52.1 0.1 and.58
  52.3 0.1 and.57
  52.4 0.1 eq.23
  52.5 0.1 copy.22
  52.6 0.1 mul.673
  52.7 0.1 copy.24
  52.8 0.1 reshape.849
  52.9 0.2 fusion.46
  53.2 0.8 collective-permute-done.7
  54.0 0.6 copy-done.4
  54.7 2.9 %select_maximum_fusion.4 = f32[48,6,18,130]{3,0,2,1:T(8,128)S(1)} fusion(f32[48,6,1,128]{3,0,2,1:T(8,128)S(1)} %collective-permute-done.6, f32[48,6,1,128]{3,0,2,1:T(8,128)S(1)} %collective-permute-done.7, f32[48,1,16,128]{3,0,2,1:T(8,128)S(1)} %collective-permute-done.4, f32[48,4,16,128]{3,0,2,1:T(8,128)S(1)} %fusion.40, ...), kind=kLoop, calls=%fused_computation.9 | loop fusion | flops 8087040 | bytes 5349888 | tf_op jit(solution)/shard_map/concatenate | solution.py:24
  57.6 2.4 %fusion.30 = f32[48,4,16,128]{3,0,2,1:T(8,128)S(1)} fusion(f32[48,6,18,130]{3,0,2,1:T(8,128)S(1)} %select_maximum_fusion.4, f32[48,6,1,128]{3,0,2,1:T(8,128)} %copy-done.4, f32[48,1,16,128]{3,0,2,1:T(8,128)S(1)} %collective-permute-done.4, f32[48,4,16,128]{3,0,2,1:T(8,128)S(1)} %fusion.40, f32[48,1,16,128]{3,0,2,1:T(8,128)} %copy-done.2, ...), kind=kLoop, calls=%fused_computation.70 | loop fusion | flops 7864320 | bytes 7503872 | tf_op jit(solution)/shard_map/add | solution.py:36
  60.1 0.1 fusion.60
  60.2 1.3 collective-permute-start.8
  61.5 4.8 %collective-permute-start.9 = (f32[48,1,16,128]{3,0,2,1:T(8,128)S(1)}, f32[48,1,16,128]{3,0,2,1:T(8,128)S(1)}, u32[]{:S(2)}, u32[]{:S(2)}) collective-permute-start(f32[48,1,16,128]{3,0,2,1:T(8,128)S(1)} %get-tuple-element.34), channel_id=1, source_target_pairs={{0,8},{8,16},{16,24},{24,32},{32,40},{40,48},{48,56},{56,64},{64,7... | collective-permute-start | bytes 1179656 | tf_op jit(solution)/shard_map/ppermute | solution.py:22
  66.3 1.4 scatter_custom_fusion
  67.7 0.8 all_to_all.11
  68.4 15.8 %all-to-all-start = ((s32[128,1,2]{2,1,0:T(1,128)}), s32[128,1,2]{2,1,0:T(1,128)S(1)}, u32[]{:S(2)}, u32[]{:S(2)}) async-start(s32[128,1,2]{2,1,0:T(1,128)} %bitcast.5), calls=%async_computation | async-start | bytes 131072 | tf_op jit(solution)/shard_map/all_to_all | solution.py:108
  84.2 3.0 %collective-permute-start.10 = (f32[48,6,1,128]{3,0,2,1:T(8,128)S(1)}, f32[48,6,1,128]{3,0,2,1:T(8,128)S(1)}, u32[]{:S(2)}, u32[]{:S(2)}) collective-permute-start(f32[48,6,1,128]{3,0,2,1:T(8,128)S(1)} %get-tuple-element.29), channel_id=1, source_target_pairs={{1,0},{2,1},{3,2},{4,3},{5,4},{6,5},{7,6},{9,8},{10,9},{11,10},{12... | collective-permute-start | bytes 442376 | tf_op jit(solution)/shard_map/ppermute | solution.py:23
  87.2 2.6 %collective-permute-start.11 = (f32[48,6,1,128]{3,0,2,1:T(8,128)S(1)}, f32[48,6,1,128]{3,0,2,1:T(8,128)S(1)}, u32[]{:S(2)}, u32[]{:S(2)}) collective-permute-start(f32[48,6,1,128]{3,0,2,1:T(8,128)S(1)} %get-tuple-element.28), channel_id=1, source_target_pairs={{0,1},{1,2},{2,3},{3,4},{4,5},{5,6},{6,7},{8,9},{9,10},{10,11},{11... | collective-permute-start | bytes 442376 | tf_op jit(solution)/shard_map/ppermute | solution.py:22
  89.8 3.8 %all-to-all-done = s32[128,1,2]{2,1,0:T(1,128)S(1)} async-done(((s32[128,1,2]{2,1,0:T(1,128)}), s32[128,1,2]{2,1,0:T(1,128)S(1)}, u32[]{:S(2)}, u32[]{:S(2)}) %all-to-all-start) | async-done | bytes 1056 | tf_op jit(solution)/shard_map/all_to_all | solution.py:108
  93.6 0.1 reshape.831
  93.9 2.9 %select_maximum_fusion = f32[48,6,18,130]{3,0,2,1:T(8,128)S(1)} fusion(f32[48,6,1,128]{3,0,2,1:T(8,128)S(1)} %collective-permute-done.10, f32[48,6,1,128]{3,0,2,1:T(8,128)S(1)} %collective-permute-done.11, f32[48,1,16,128]{3,0,2,1:T(8,128)S(1)} %collective-permute-done.8, f32[48,4,16,128]{3,0,2,1:T(8,128)S(1)} %fusion.30, ...), kind=kLoop, calls=%fused_computation.5 | loop fusion | flops 8087040 | bytes 5349888 | tf_op jit(solution)/shard_map/concatenate | solution.py:24
  96.8 2.5 %fusion.57 = (bf16[48,4,16,128]{3,0,2,1:T(8,128)(2,1)S(1)}, f32[48,4,16,128]{3,0,2,1:T(8,128)}) fusion(f32[4,16,128]{2,1,0:T(8,128)S(1)} %copy-done.16, f32[48,6,18,130]{3,0,2,1:T(8,128)S(1)} %select_maximum_fusion, f32[4,16,128]{2,1,0:T(8,128)S(1)} %copy-done.7, f32[48,1,16,128]{3,0,2,1:T(8,128)S(1)} %collective-permute-done.8, ...), kind=kLoop, calls=%fused_computation.164 | loop fusion | flops 8257536 | bytes 8290304 | tf_op jit(solution)/shard_map/convert_element_type | solution.py:83
  99.3 2.6 %gather_fusion = bf16[256,48,128]{2,1,0:T(8,128)(2,1)} fusion(bf16[64,48,128]{2,1,0:T(8,128)(2,1)S(1)} %bitcast.110, s32[1024]{0:T(1024)S(1)} %pad_clamp_fusion.1), kind=kCustom, calls=%fused_computation | custom fusion | bytes 6292480 | tf_op jit(solution)/shard_map/gather | solution.py:107
  102.0 9.2 %all-to-all-start.1 = ((bf16[128,2,48,128]{3,2,1,0:T(8,128)(2,1)}), bf16[128,2,48,128]{3,2,1,0:T(8,128)(2,1)}, u32[]{:S(2)}, u32[]{:S(2)}) async-start(bf16[128,2,48,128]{3,2,1,0:T(8,128)(2,1)} %bitcast.111), calls=%async_computation.1 | async-start | bytes 6291456 | tf_op jit(solution)/shard_map/all_to_all | solution.py:116
  111.2 0.1 and.51
  111.3 0.5 broadcast.689
  111.8 0.7 reduce.5
  112.5 0.1 lt.80
  112.6 1.6 copy.27
  114.2 38.4 %all-to-all-done.1 = bf16[128,2,48,128]{3,2,1,0:T(8,128)(2,1)} async-done(((bf16[128,2,48,128]{3,2,1,0:T(8,128)(2,1)}), bf16[128,2,48,128]{3,2,1,0:T(8,128)(2,1)}, u32[]{:S(2)}, u32[]{:S(2)}) %all-to-all-start.1) | async-done | bytes 3145760 | tf_op jit(solution)/shard_map/all_to_all | solution.py:116
  152.6 4.5 %gather_fusion.1 = bf16[256,48,128]{2,1,0:T(8,128)(2,1)} fusion(bf16[256,48,128]{2,1,0:T(8,128)(2,1)} %bitcast.8, s32[1024]{0:T(1024)S(1)} %pad_clamp_fusion), kind=kCustom, calls=%fused_computation.1 | custom fusion | bytes 6292480 | tf_op jit(solution)/shard_map/gather | solution.py:118
  157.1 2.1 %fusion.1 = bf16[48,4,64,128]{3,0,2,1:T(8,128)(2,1)S(1)} fusion(bf16[64,4,48,128]{3,2,1,0:T(8,128)(2,1)} %bitcast.112, pred[64,4]{0,1:T(4,128)(4,1)S(1)} %fusion.53), kind=kLoop, calls=%fused_computation.31 | loop fusion | flops 1572864 | bytes 6291712 | tf_op jit(solution)/shard_map/transpose | solution.py:120
  159.3 4.3 %fusion.13 = (f32[64,128]{1,0:T(8,128)S(1)}, f32[64,128]{1,0:T(8,128)S(1)}, f32[64,128]{1,0:T(8,128)S(1)}, f32[64,128]{1,0:T(8,128)S(1)}, f32[64,128]{1,0:T(8,12...) fusion(bf16[48,4,64,128]{3,0,2,1:T(8,128)(2,1)S(1)} %fusion.1, ...), kind=kLoop, calls=%fused_computation.43 | loop fusion | flops 12861440 | bytes 4390912 | tf_op jit(solution)/shard_map/reduce_sum | solution.py:67
  163.8 0.1 subtract_divide_fusion
  163.9 0.7 pad_maximum_fusion.26
  (68 shorter events, 0.4 us)
Async XLA Ops:
  3.0 12.4 %copy-start = (f32[48,4,16,128]{3,2,1,0:T(8,128)S(1)}, f32[48,4,16,128]{3,2,1,0:T(8,128)}, u32[]{:S(2)}) copy-start(f32[48,4,16,128]{3,2,1,0:T(8,128)} %param.9) | copy-start | bytes 4718596
  3.0 12.3 %collective-permute-start.1 = (f32[48,1,16,128]{3,0,2,1:T(8,128)S(1)}, f32[48,1,16,128]{3,0,2,1:T(8,128)S(1)}, u32[]{:S(2)}, u32[]{:S(2)}) collective-permute-start(f32[48,1,16,128]{3,0,2,1:T(8,128)S(1)} %get-tuple-element.39), channel_id=1, source_target_pairs={{0,8},{8,16},{16,24},{24,32},{32,40},{40,48},{48,56},{56,64},{64,7... | collective-permute-start | bytes 1179656 | tf_op jit(solution)/shard_map/ppermute | solution.py:22
  7.6 11.9 %collective-permute-start = (f32[48,1,16,128]{3,0,2,1:T(8,128)S(1)}, f32[48,1,16,128]{3,0,2,1:T(8,128)S(1)}, u32[]{:S(2)}, u32[]{:S(2)}) collective-permute-start(f32[48,1,16,128]{3,0,2,1:T(8,128)S(1)} %get-tuple-element.38), channel_id=1, source_target_pairs={{8,0},{16,8},{24,16},{32,24},{40,32},{48,40},{56,48},{64,56},{72,6... | collective-permute-start | bytes 1179656 | tf_op jit(solution)/shard_map/ppermute | solution.py:23
  15.3 10.9 %copy-start.5 = (f32[4,16,128]{2,1,0:T(8,128)S(1)}, f32[4,16,128]{2,1,0:T(8,128)}, u32[]{:S(2)}) copy-start(f32[4,16,128]{2,1,0:T(8,128)} %param.12) | copy-start | bytes 98308
  15.4 10.9 %copy-start.8 = (f32[4,16,128]{2,1,0:T(8,128)S(1)}, f32[4,16,128]{2,1,0:T(8,128)}, u32[]{:S(2)}) copy-start(f32[4,16,128]{2,1,0:T(8,128)} %param.10) | copy-start | bytes 98308
  15.4 10.9 %copy-start.11 = (f32[4,16,128]{2,1,0:T(8,128)S(1)}, f32[4,16,128]{2,1,0:T(8,128)}, u32[]{:S(2)}) copy-start(f32[4,16,128]{2,1,0:T(8,128)} %param.11) | copy-start | bytes 98308
  15.4 10.9 %copy-start.17 = (f32[4,16,128]{2,1,0:T(8,128)S(1)}, f32[4,16,128]{2,1,0:T(8,128)}, u32[]{:S(2)}) copy-start(f32[4,16,128]{2,1,0:T(8,128)} %param.13) | copy-start | bytes 98308
  19.5 7.6 %collective-permute-start.2 = (f32[48,6,1,128]{3,0,2,1:T(8,128)S(1)}, f32[48,6,1,128]{3,0,2,1:T(8,128)S(1)}, u32[]{:S(2)}, u32[]{:S(2)}) collective-permute-start(f32[48,6,1,128]{3,0,2,1:T(8,128)S(1)} %get-tuple-element.33), channel_id=1, source_target_pairs={{1,0},{2,1},{3,2},{4,3},{5,4},{6,5},{7,6},{9,8},{10,9},{11,10},{12... | collective-permute-start | bytes 442376 | tf_op jit(solution)/shard_map/ppermute | solution.py:23
  23.1 5.2 %collective-permute-start.3 = (f32[48,6,1,128]{3,0,2,1:T(8,128)S(1)}, f32[48,6,1,128]{3,0,2,1:T(8,128)S(1)}, u32[]{:S(2)}, u32[]{:S(2)}) collective-permute-start(f32[48,6,1,128]{3,0,2,1:T(8,128)S(1)} %get-tuple-element.32), channel_id=1, source_target_pairs={{0,1},{1,2},{2,3},{3,4},{4,5},{5,6},{6,7},{8,9},{9,10},{10,11},{11... | collective-permute-start | bytes 442376 | tf_op jit(solution)/shard_map/ppermute | solution.py:22
  26.3 4.2 %copy-start.14 = (f32[4,16,128]{2,1,0:T(8,128)}, f32[4,16,128]{2,1,0:T(8,128)S(1)}, u32[]{:S(2)}) copy-start(f32[4,16,128]{2,1,0:T(8,128)S(1)} %multiply_add_fusion.3) | copy-start | bytes 98308
  32.2 5.4 %copy-start.21 = (s32[4,16,1]{1,2,0:T(1,128)S(1)}, s32[4,16,1]{1,2,0:T(1,128)}, u32[]{:S(2)}) copy-start(s32[4,16,1]{1,2,0:T(1,128)} %param.14) | copy-start | bytes 772
  32.2 6.0 %copy-start.18 = (s32[4,16,1,4]{1,3,2,0:T(4,128)S(1)}, s32[4,16,1,4]{1,3,2,0:T(4,128)}, u32[]{:S(2)}) copy-start(s32[4,16,1,4]{1,3,2,0:T(4,128)} %param.16) | copy-start | bytes 3076
  32.3 19.7 %copy-start.20 = (s32[4,16,1]{1,2,0:T(1,128)S(1)}, s32[4,16,1]{1,2,0:T(1,128)}, u32[]{:S(2)}) copy-start(s32[4,16,1]{1,2,0:T(1,128)} %param.15) | copy-start | bytes 772
  32.3 20.4 %copy-start.19 = (s32[4,16,1,4]{1,3,2,0:T(4,128)S(1)}, s32[4,16,1,4]{1,3,2,0:T(4,128)}, u32[]{:S(2)}) copy-start(s32[4,16,1,4]{1,3,2,0:T(4,128)} %param.17) | copy-start | bytes 3076
  32.3 11.4 %collective-permute-start.4 = (f32[48,1,16,128]{3,0,2,1:T(8,128)S(1)}, f32[48,1,16,128]{3,0,2,1:T(8,128)S(1)}, u32[]{:S(2)}, u32[]{:S(2)}) collective-permute-start(f32[48,1,16,128]{3,0,2,1:T(8,128)S(1)} %get-tuple-element.37), channel_id=1, source_target_pairs={{8,0},{16,8},{24,16},{32,24},{40,32},{48,40},{56,48},{64,56},{72,6... | collective-permute-start | bytes 1179656 | tf_op jit(solution)/shard_map/ppermute | solution.py:23
  33.6 11.9 %collective-permute-start.5 = (f32[48,1,16,128]{3,0,2,1:T(8,128)S(1)}, f32[48,1,16,128]{3,0,2,1:T(8,128)S(1)}, u32[]{:S(2)}, u32[]{:S(2)}) collective-permute-start(f32[48,1,16,128]{3,0,2,1:T(8,128)S(1)} %get-tuple-element.36), channel_id=1, source_target_pairs={{0,8},{8,16},{16,24},{24,32},{32,40},{40,48},{48,56},{56,64},{64,7... | collective-permute-start | bytes 1179656 | tf_op jit(solution)/shard_map/ppermute | solution.py:22
  45.5 8.6 %copy-start.2 = (f32[48,1,16,128]{3,0,2,1:T(8,128)}, f32[48,1,16,128]{3,0,2,1:T(8,128)S(1)}, u32[]{:S(2)}) copy-start(f32[48,1,16,128]{3,0,2,1:T(8,128)S(1)} %collective-permute-done.5) | copy-start | bytes 1179652
  45.5 7.7 %collective-permute-start.6 = (f32[48,6,1,128]{3,0,2,1:T(8,128)S(1)}, f32[48,6,1,128]{3,0,2,1:T(8,128)S(1)}, u32[]{:S(2)}, u32[]{:S(2)}) collective-permute-start(f32[48,6,1,128]{3,0,2,1:T(8,128)S(1)} %get-tuple-element.31), channel_id=1, source_target_pairs={{1,0},{2,1},{3,2},{4,3},{5,4},{6,5},{7,6},{9,8},{10,9},{11,10},{12... | collective-permute-start | bytes 442376 | tf_op jit(solution)/shard_map/ppermute | solution.py:23
  47.4 6.6 %collective-permute-start.7 = (f32[48,6,1,128]{3,0,2,1:T(8,128)S(1)}, f32[48,6,1,128]{3,0,2,1:T(8,128)S(1)}, u32[]{:S(2)}, u32[]{:S(2)}) collective-permute-start(f32[48,6,1,128]{3,0,2,1:T(8,128)S(1)} %get-tuple-element.30), channel_id=1, source_target_pairs={{0,1},{1,2},{2,3},{3,4},{4,5},{5,6},{6,7},{8,9},{9,10},{10,11},{11... | collective-permute-start | bytes 442376 | tf_op jit(solution)/shard_map/ppermute | solution.py:22
  53.2 4.5 %copy-start.6 = (f32[4,16,128]{2,1,0:T(8,128)S(1)}, f32[4,16,128]{2,1,0:T(8,128)}, u32[]{:S(2)}) copy-start(f32[4,16,128]{2,1,0:T(8,128)} %param.12) | copy-start | bytes 98308
  53.2 4.5 %copy-start.9 = (f32[4,16,128]{2,1,0:T(8,128)S(1)}, f32[4,16,128]{2,1,0:T(8,128)}, u32[]{:S(2)}) copy-start(f32[4,16,128]{2,1,0:T(8,128)} %param.10) | copy-start | bytes 98308
  53.2 4.5 %copy-start.12 = (f32[4,16,128]{2,1,0:T(8,128)S(1)}, f32[4,16,128]{2,1,0:T(8,128)}, u32[]{:S(2)}) copy-start(f32[4,16,128]{2,1,0:T(8,128)} %param.11) | copy-start | bytes 98308
  53.2 4.5 %copy-start.15 = (f32[4,16,128]{2,1,0:T(8,128)S(1)}, f32[4,16,128]{2,1,0:T(8,128)}, u32[]{:S(2)}) copy-start(f32[4,16,128]{2,1,0:T(8,128)} %copy-done.14) | copy-start | bytes 98308
  53.2 0.8 copy-start.3
  54.0 0.7 copy-start.4
  60.2 24.0 %collective-permute-start.8 = (f32[48,1,16,128]{3,0,2,1:T(8,128)S(1)}, f32[48,1,16,128]{3,0,2,1:T(8,128)S(1)}, u32[]{:S(2)}, u32[]{:S(2)}) collective-permute-start(f32[48,1,16,128]{3,0,2,1:T(8,128)S(1)} %get-tuple-element.35), channel_id=1, source_target_pairs={{8,0},{16,8},{24,16},{32,24},{40,32},{48,40},{56,48},{64,56},{72,6... | collective-permute-start | bytes 1179656 | tf_op jit(solution)/shard_map/ppermute | solution.py:23
  61.5 22.8 %collective-permute-start.9 = (f32[48,1,16,128]{3,0,2,1:T(8,128)S(1)}, f32[48,1,16,128]{3,0,2,1:T(8,128)S(1)}, u32[]{:S(2)}, u32[]{:S(2)}) collective-permute-start(f32[48,1,16,128]{3,0,2,1:T(8,128)S(1)} %get-tuple-element.34), channel_id=1, source_target_pairs={{0,8},{8,16},{16,24},{24,32},{32,40},{40,48},{48,56},{56,64},{64,7... | collective-permute-start | bytes 1179656 | tf_op jit(solution)/shard_map/ppermute | solution.py:22
  68.4 25.2 %all-to-all-start = ((s32[128,1,2]{2,1,0:T(1,128)}), s32[128,1,2]{2,1,0:T(1,128)S(1)}, u32[]{:S(2)}, u32[]{:S(2)}) async-start(s32[128,1,2]{2,1,0:T(1,128)} %bitcast.5), calls=%async_computation | async-start | bytes 131072 | tf_op jit(solution)/shard_map/all_to_all | solution.py:108
  84.2 9.6 %collective-permute-start.10 = (f32[48,6,1,128]{3,0,2,1:T(8,128)S(1)}, f32[48,6,1,128]{3,0,2,1:T(8,128)S(1)}, u32[]{:S(2)}, u32[]{:S(2)}) collective-permute-start(f32[48,6,1,128]{3,0,2,1:T(8,128)S(1)} %get-tuple-element.29), channel_id=1, source_target_pairs={{1,0},{2,1},{3,2},{4,3},{5,4},{6,5},{7,6},{9,8},{10,9},{11,10},{12... | collective-permute-start | bytes 442376 | tf_op jit(solution)/shard_map/ppermute | solution.py:23
  87.2 6.6 %collective-permute-start.11 = (f32[48,6,1,128]{3,0,2,1:T(8,128)S(1)}, f32[48,6,1,128]{3,0,2,1:T(8,128)S(1)}, u32[]{:S(2)}, u32[]{:S(2)}) collective-permute-start(f32[48,6,1,128]{3,0,2,1:T(8,128)S(1)} %get-tuple-element.28), channel_id=1, source_target_pairs={{0,1},{1,2},{2,3},{3,4},{4,5},{5,6},{6,7},{8,9},{9,10},{10,11},{11... | collective-permute-start | bytes 442376 | tf_op jit(solution)/shard_map/ppermute | solution.py:22
  93.8 3.0 %copy-start.7 = (f32[4,16,128]{2,1,0:T(8,128)S(1)}, f32[4,16,128]{2,1,0:T(8,128)}, u32[]{:S(2)}) copy-start(f32[4,16,128]{2,1,0:T(8,128)} %param.12) | copy-start | bytes 98308
  93.8 3.0 %copy-start.10 = (f32[4,16,128]{2,1,0:T(8,128)S(1)}, f32[4,16,128]{2,1,0:T(8,128)}, u32[]{:S(2)}) copy-start(f32[4,16,128]{2,1,0:T(8,128)} %param.10) | copy-start | bytes 98308
  93.8 3.0 %copy-start.13 = (f32[4,16,128]{2,1,0:T(8,128)S(1)}, f32[4,16,128]{2,1,0:T(8,128)}, u32[]{:S(2)}) copy-start(f32[4,16,128]{2,1,0:T(8,128)} %param.11) | copy-start | bytes 98308
  93.8 3.0 %copy-start.16 = (f32[4,16,128]{2,1,0:T(8,128)S(1)}, f32[4,16,128]{2,1,0:T(8,128)}, u32[]{:S(2)}) copy-start(f32[4,16,128]{2,1,0:T(8,128)} %copy-done.14) | copy-start | bytes 98308
  102.0 9.2 %copy-start.22 = (pred[4,16]{1,0:T(4,128)(4,1)S(1)}, pred[4,16]{1,0:T(4,128)(4,1)}, u32[]{:S(2)}) copy-start(pred[4,16]{1,0:T(4,128)(4,1)} %get-tuple-element.46) | copy-start | bytes 196
  102.0 10.6 %copy-start.1 = (f32[48,4,16,128]{3,0,2,1:T(8,128)S(1)}, f32[48,4,16,128]{3,0,2,1:T(8,128)}, u32[]{:S(2)}) copy-start(f32[48,4,16,128]{3,0,2,1:T(8,128)} %get-tuple-element.26) | copy-start | bytes 4718596
  102.0 50.6 %all-to-all-start.1 = ((bf16[128,2,48,128]{3,2,1,0:T(8,128)(2,1)}), bf16[128,2,48,128]{3,2,1,0:T(8,128)(2,1)}, u32[]{:S(2)}, u32[]{:S(2)}) async-start(bf16[128,2,48,128]{3,2,1,0:T(8,128)(2,1)} %bitcast.111), calls=%async_computation.1 | async-start | bytes 6291456 | tf_op jit(solution)/shard_map/all_to_all | solution.py:116
where the time goes:
time: 165 us
  waiting for transfers between devices  61.8 us (37%)
  starting transfers between devices  60.9 us (37%)
  other arithmetic  23.4 us (14%)
  local copies, waits for them, and re-layouts  16.9 us (10%)
    all_to_all x1, waiting for transfers between devices, per_device(): lax.all_to_all(found_rows, ('gx', 'gy'), split_axis=0, concat_axis=0, til...  38.4 us
    ppermute x6, starting transfers between devices, extended(): before = lax.ppermute(last, axis, up)  23.5 us
    all_to_all x1, starting transfers between devices, per_device(): lax.all_to_all(request_table.reshape(devices, capacity), ('gx', 'gy'), sp...  15.8 us
    ppermute x6, starting transfers between devices, extended(): after = lax.ppermute(leading, axis, down)  12.4 us
    ppermute x6, waiting for transfers between devices, extended(): before = lax.ppermute(last, axis, up)  10.2 us
    ppermute x6, waiting for transfers between devices, extended(): after = lax.ppermute(leading, axis, down)  9.46 us
    all_to_all x1, starting transfers between devices, per_device(): lax.all_to_all(found_rows, ('gx', 'gy'), split_axis=0, concat_axis=0, til...  9.23 us
    concatenate x5, other arithmetic, extended(): value = jnp.concatenate([before, value, after], axis=dim)  8.11 us
  transfers between devices with their start and end apart: 14, of which 9 were waited for; matrix products, arithmetic and copies ran while one was open for 4% of the time, Pallas kernels for 0%

commit v1 on v0

v1 whole, which is shorter than its diff:
```python
import jax
import jax.numpy as jnp
from jax import lax
from jax.experimental import pallas as pl
from jax.experimental.pallas import tpu as pltpu
from jax.sharding import PartitionSpec as P

SLOTS = 4
SWEEPS = 3
ROWS = 128
OMEGA = 0.8
RIDGE = 0.05
VECS = 48
CHUNKS = 3
KV = VECS // CHUNKS
NX = 4
NY = 16
SITES = NX * NY
XROW = (NY + 2) * KV
EXT = (NX + 2) * XROW
GX = 16
GY = 8
MESH = pl.DeviceIdType.MESH
F32 = jnp.float32
BF16 = jnp.bfloat16


def site_row(x, y):
    return (x + 1) * XROW + (y + 1) * KV


def smooth_kernel(
    tv, cx, cy, cz, sh, sm_out, blk, stage, wa, wb, ka, kb, km, kp, fxs, fxr, fys, fyr,
    in_sem, out_sem, send_sem, recv_sem
):
    i = lax.axis_index("gx")
    j = lax.axis_index("gy")
    peers = (
        (lax.rem(i + GX - 1, GX), j),
        (lax.rem(i + 1, GX), j),
        (i, lax.rem(j + GY - 1, GY)),
        (i, lax.rem(j + 1, GY)),
    )
    loads = []
    for c in range(CHUNKS):
        part = pl.ds(c * KV, KV)
        load = pltpu.make_async_copy(tv.at[part], stage.at[part], in_sem.at[c])
        load.start()
        loads.append(load)
    barrier = pltpu.get_barrier_semaphore()
    for peer in peers:
        pl.semaphore_signal(barrier, inc=1, device_id=peer, device_id_type=MESH)

    ax, ay, az = cx[...], cy[...], cz[...]
    scale = OMEGA / (2.0 * (ax + ay + az) + sh[...])
    ka[...] = ax * scale
    kb[...] = ay * scale
    az = az * scale
    lane = lax.broadcasted_iota(jnp.int32, az.shape, 2)
    km[...] = jnp.where(lane == 0, 0.0, az)
    kp[...] = jnp.where(lane == ROWS - 1, 0.0, az)
    keep = (
        (i > 0).astype(F32),
        (i < GX - 1).astype(F32),
        (j > 0).astype(F32),
        (j < GY - 1).astype(F32),
    )

    def copies(s, c):
        out = []
        for d in range(4):
            src, dst = (fxs, fxr) if d < 2 else (fys, fyr)
            out.append(
                pltpu.make_async_remote_copy(
                    src_ref=src.at[s, c, d % 2],
                    dst_ref=dst.at[s, c, 1 - d % 2],
                    send_sem=send_sem.at[s, c, d],
                    recv_sem=recv_sem.at[s, c, d],
                    device_id=peers[d],
                    device_id_type=MESH,
                )
            )
        return out

    def send_faces(s, c, w):
        for side in range(2):
            x = side * (NX - 1)
            fxs[s, c, side] = w[c, pl.ds(site_row(x, 0), NY * KV)].astype(BF16)
            y = side * (NY - 1)
            for x in range(NX):
                fys[s, c, side, pl.ds(x * KV, KV)] = w[c, pl.ds(site_row(x, y), KV)].astype(BF16)
        for copy in copies(s, c):
            copy.start()

    def fill_halo(s, c, w):
        for copy in copies(s, c):
            copy.wait_recv()
        for side in range(2):
            x = -1 if side == 0 else NX
            w[c, pl.ds(site_row(x, 0), NY * KV)] = fxr[s, c, side].astype(F32) * keep[side]
            y = -1 if side == 0 else NY
            for x in range(NX):
                w[c, pl.ds(site_row(x, y), KV)] = (
                    fyr[s, c, side, pl.ds(x * KV, KV)].astype(F32) * keep[2 + side]
                )

    def sweep(c, src, dst, last):
        def plane(x, carry):
            base = pl.multiple_of(x * XROW, 16)

            def cell(dx, y):
                return src[c, pl.ds(base + site_row(dx, y), KV)]

            below, here = cell(0, -1), cell(0, 0)
            for y in range(NY):
                above = cell(0, y + 1)
                row = slice(y, y + 1)
                new = (
                    ka[x, row] * (cell(-1, y) + cell(1, y))
                    + kb[x, row] * (below + above)
                    + km[x, row] * pltpu.roll(here, 1, 1)
                    + kp[x, row] * pltpu.roll(here, ROWS - 1, 1)
                    + (1.0 - OMEGA) * here
                )
                dst[c, pl.ds(base + site_row(0, y), KV)] = new
                if last:
                    blk[x * NY + y, pl.ds(c * KV, KV)] = new.astype(BF16)
                below, here = here, above
            return carry

        lax.fori_loop(0, NX, plane, 0)

    buffers = (wa, wb)
    for c in range(CHUNKS):
        loads[c].wait()
        for x in range(NX):
            for half in range(NY // 8):
                for k in range(KV):
                    wa[c, pl.ds(site_row(x, half * 8) + k, 8, stride=KV), :] = stage[
                        c * KV + k, x, pl.ds(half * 8, 8), :
                    ]
        if c == 0:
            pl.semaphore_wait(barrier, 4)
        send_faces(0, c, wa)
    stores = []
    for s in range(SWEEPS):
        src, dst = buffers[s % 2], buffers[(s + 1) % 2]
        for c in range(CHUNKS):
            fill_halo(s, c, src)
            sweep(c, src, dst, s == SWEEPS - 1)
            if s < SWEEPS - 1:
                send_faces(s + 1, c, dst)
            else:
                for x in range(NX):
                    for half in range(NY // 8):
                        for k in range(KV):
                            stage[c * KV + k, x, pl.ds(half * 8, 8), :] = dst[
                                c, pl.ds(site_row(x, half * 8) + k, 8, stride=KV), :
                            ]
                part = pl.ds(c * KV, KV)
                store = pltpu.make_async_copy(stage.at[part], sm_out.at[part], out_sem.at[c])
                store.start()
                stores.append(store)
    for s in range(SWEEPS):
        for c in range(CHUNKS):
            for copy in copies(s, c):
                copy.wait_send()
    for store in stores:
        store.wait()


def smooth(test_vectors, coef_x, coef_y, coef_z, shift):
    vmem = pl.BlockSpec(memory_space=pltpu.VMEM)
    anywhere = pl.BlockSpec(memory_space=pl.ANY)
    return pl.pallas_call(
        smooth_kernel,
        out_shape=(
            jax.ShapeDtypeStruct((VECS, NX, NY, ROWS), F32),
            jax.ShapeDtypeStruct((SITES, VECS, ROWS), BF16),
        ),
        in_specs=[anywhere, vmem, vmem, vmem, vmem],
        out_specs=(anywhere, vmem),
        scratch_shapes=[
            pltpu.VMEM((VECS, NX, NY, ROWS), F32),
            pltpu.VMEM((CHUNKS, EXT, ROWS), F32),
            pltpu.VMEM((CHUNKS, EXT, ROWS), F32),
            pltpu.VMEM((NX, NY, ROWS), F32),
            pltpu.VMEM((NX, NY, ROWS), F32),
            pltpu.VMEM((NX, NY, ROWS), F32),
            pltpu.VMEM((NX, NY, ROWS), F32),
            pltpu.VMEM((SWEEPS, CHUNKS, 2, NY * KV, ROWS), BF16),
            pltpu.VMEM((SWEEPS, CHUNKS, 2, NY * KV, ROWS), BF16),
            pltpu.VMEM((SWEEPS, CHUNKS, 2, NX * KV, ROWS), BF16),
            pltpu.VMEM((SWEEPS, CHUNKS, 2, NX * KV, ROWS), BF16),
            pltpu.SemaphoreType.DMA((CHUNKS,)),
            pltpu.SemaphoreType.DMA((CHUNKS,)),
            pltpu.SemaphoreType.DMA((SWEEPS, CHUNKS, 4)),
            pltpu.SemaphoreType.DMA((SWEEPS, CHUNKS, 4)),
        ],
        compiler_params=pltpu.CompilerParams(
            collective_id=0, has_side_effects=True, vmem_limit_bytes=48 * 1024 * 1024
        ),
        name="smooth",
    )(test_vectors, coef_x, coef_y, coef_z, shift)


def solve_rows(gram, rhs):
    low = [[None] * SLOTS for _ in range(SLOTS)]
    inv = []
    for r in range(SLOTS):
        scaled = []
        diag = gram[r, r]
        for c in range(r):
            rest = gram[r, c]
            for m in range(c):
                rest = rest - scaled[m] * low[c][m]
            scaled.append(rest)
            low[r][c] = rest * inv[c]
            diag = diag - rest * low[r][c]
        inv.append(1.0 / diag)
    fwd = []
    for r in range(SLOTS):
        rest = rhs[r]
        for m in range(r):
            rest = rest - low[r][m] * fwd[m]
        fwd.append(rest)
    out = [None] * SLOTS
    for r in reversed(range(SLOTS)):
        rest = fwd[r] * inv[r]
        for m in range(r + 1, SLOTS):
            rest = rest - low[m][r] * out[m]
        out[r] = rest
    return out


PAIRS = [(s, t) for s in range(SLOTS) for t in range(s + 1)] + [
    (s, SLOTS) for s in range(SLOTS)
]


def weights_kernel(target, replies, blk, sm_in, w_out, sm_out, sums, copy_sem):
    move = pltpu.make_async_copy(sm_in, sm_out, copy_sem)
    move.start()

    def block(b, carry):
        values = []
        for s in range(SLOTS):
            at = target[b * SLOTS + s]
            live = at >= 0
            found = replies[jnp.maximum(at, 0)].astype(F32)
            values.append(jnp.where(live, found, 0.0))
        values.append(blk[b].astype(F32))
        for n, (s, t) in enumerate(PAIRS):
            prod = values[s] * values[t]
            acc = prod[0:8]
            for h in range(1, VECS // 8):
                acc = acc + prod[8 * h : 8 * h + 8]
            sums[n, pl.ds(pl.multiple_of(b * 8, 8), 8), :] = acc
        return carry

    lax.fori_loop(0, SITES, block, 0)
    for g in range(SITES // 8):
        total = {}
        for n, pair in enumerate(PAIRS):
            acc = sums[n, pl.ds(g * 64, 8, stride=8), :]
            for h in range(1, 8):
                acc = acc + sums[n, pl.ds(g * 64 + h, 8, stride=8), :]
            acc = acc * (1.0 / VECS)
            if pair[0] == pair[1]:
                acc = acc + RIDGE
            total[pair] = acc
        out = solve_rows(total, [total[s, SLOTS] for s in range(SLOTS)])
        for s in range(SLOTS):
            w_out[s, g // 2, pl.ds((g % 2) * 8, 8), :] = out[s]
    move.wait()


def fit(target, replies, blk, sm):
    vmem = pl.BlockSpec(memory_space=pltpu.VMEM)
    anywhere = pl.BlockSpec(memory_space=pl.ANY)
    return pl.pallas_call(
        weights_kernel,
        out_shape=(
            jax.ShapeDtypeStruct((SLOTS, NX, NY, ROWS), F32),
            jax.ShapeDtypeStruct((VECS, NX, NY, ROWS), F32),
        ),
        in_specs=[pl.BlockSpec(memory_space=pltpu.SMEM), vmem, vmem, anywhere],
        out_specs=(vmem, anywhere),
        scratch_shapes=[
            pltpu.VMEM((len(PAIRS), SITES * 8, ROWS), F32),
            pltpu.SemaphoreType.DMA,
        ],
        compiler_params=pltpu.CompilerParams(vmem_limit_bytes=48 * 1024 * 1024),
        name="fit",
    )(target, replies, blk, sm)


def per_device(
    test_vectors, coef_x, coef_y, coef_z, shift, cf_split, nbr_count, nbr_owner, nbr_block
):
    devices = GX * GY
    entries = SITES * SLOTS
    capacity = 2
    live = ((cf_split == 0)[..., None] & (jnp.arange(SLOTS) < nbr_count[..., None])).reshape(entries)
    owner = nbr_owner.reshape(entries)
    local = nbr_block.reshape(entries)
    member = (owner[:, None] == jnp.arange(devices)[None, :]) & live[:, None]
    key = jnp.arange(entries) * SITES + local
    first = jnp.min(jnp.where(member, key[:, None], entries * SITES), axis=0)
    second = jnp.max(jnp.where(member, key[:, None], -1), axis=0)
    table = jnp.stack([first % SITES, jnp.maximum(second, 0) % SITES], axis=1)
    first_here = jnp.sum(jnp.where(member, first[None, :], 0), axis=1)
    target = jnp.where(live, owner * capacity + (key != first_here), -1)
    sm, blk = smooth(test_vectors, coef_x, coef_y, coef_z, shift)
    wanted = lax.all_to_all(table, ("gx", "gy"), split_axis=0, concat_axis=0, tiled=True)
    found = blk[wanted.reshape(-1)].reshape(devices, capacity, VECS, ROWS)
    replies = lax.all_to_all(found, ("gx", "gy"), split_axis=0, concat_axis=0, tiled=True)
    replies = replies.reshape(devices * capacity, VECS, ROWS)
    weights, smoothed = fit(target, replies, blk, sm)
    return (smoothed, weights)


def solution(mesh):
    cells = P("gx", "gy", None)
    lists = P("gx", "gy", None, None)
    vectors = P(None, "gx", "gy", None)
    return jax.shard_map(
        per_device,
        mesh=mesh,
        in_specs=(vectors, cells, cells, cells, cells, cells, cells, lists, lists),
        out_specs=(vectors, vectors),
        check_vma=False,
    )
```

time: 165 us -> 106 us (0.64)
  starting transfers between devices: 60.9 us -> 20.5 us
  Pallas kernels: 0 us -> 30.2 us
  other arithmetic: 23.4 us -> 2.69 us
  waiting for transfers between devices: 61.8 us -> 41.2 us
  local copies, waits for them, and re-layouts: 16.9 us -> 10.4 us
    ppermute x12 -> x0, starting transfers between devices: 35.9 us -> none  [the longest x6 23.5 us: extended(): before = lax.ppermute(last, axis, up)]
    pallas_call x0 -> x2, Pallas kernels: none -> 30.2 us  [the longest x1 24.6 us: smooth(): pl.pallas_call(smooth_kernel, out_shape=(jax.ShapeDtypeStruct((VECS, NX,...]
    ppermute x12 -> x0, waiting for transfers between devices: 19.7 us -> none  [the longest x6 10.2 us: extended(): before = lax.ppermute(last, axis, up)]
    concatenate x5 -> x0, other arithmetic: 8.11 us -> none  [extended(): value = jnp.concatenate([before, value, after], axis=dim)]
    all_to_all x2, starting transfers between devices: 25 us -> 20.5 us  [the longest x1 11.5 us: per_device(): lax.all_to_all(table, ('gx', 'gy'), split_axis=0, concat_axis=0, tiled=True)]
    gather x2 -> x1, local copies, waits for them, and re-layouts: 7.17 us -> 2.65 us  [per_device(): found = blk[wanted.reshape(-1)].reshape(devices, capacity, VECS, ROWS)]
    reduce_sum x1, other arithmetic: 4.32 us -> 0.21 us  [per_device(): first_here = jnp.sum(jnp.where(member, first[None, :], 0), axis=1)]
    add x5 -> x1, other arithmetic: 4.11 us -> 0.01 us  [per_device(): key = jnp.arange(entries) * SITES + local]
  transfers between devices with their start and end apart: 14 -> 2, of which waited for: 9 -> 1; matrix products, arithmetic and copies ran while one was open for 4% -> 0% of each run, Pallas kernels for 0% -> 23%
where the time goes in v1:
time: 106 us
  waiting for transfers between devices  41.2 us (39%)
  Pallas kernels  30.2 us (28%)
  starting transfers between devices  20.5 us (19%)
  local copies, waits for them, and re-layouts  10.4 us (10%)
  other arithmetic  2.69 us (3%)
    all_to_all x1, waiting for transfers between devices, per_device(): lax.all_to_all(found, ('gx', 'gy'), split_axis=0, concat_axis=0, tiled=True)  41.2 us
    pallas_call x1, Pallas kernels, smooth(): pl.pallas_call(smooth_kernel, out_shape=(jax.ShapeDtypeStruct((VECS, NX,...  24.6 us
    all_to_all x1, starting transfers between devices, per_device(): lax.all_to_all(table, ('gx', 'gy'), split_axis=0, concat_axis=0, tiled=True)  11.5 us
    all_to_all x1, starting transfers between devices, per_device(): lax.all_to_all(found, ('gx', 'gy'), split_axis=0, concat_axis=0, tiled=True)  8.98 us
    unnamed x13, local copies, waits for them, and re-layouts  6.03 us
    pallas_call x1, Pallas kernels, fit(): pl.pallas_call(weights_kernel, out_shape=(jax.ShapeDtypeStruct((SLOTS, NX...  5.63 us
    gather x1, local copies, waits for them, and re-layouts, per_device(): found = blk[wanted.reshape(-1)].reshape(devices, capacity, VECS, ROWS)  2.65 us
  transfers between devices with their start and end apart: 2, of which 1 were waited for; matrix products, arithmetic and copies ran while one was open for 0% of the time, Pallas kernels for 23%

profile of v1, /device:TPU:1, one launch (start us, length us, event | category | flops | bytes accessed | tf_op | source)
XLA Modules:
  0.0 105.6 jit_solution(16734382928166599623)
XLA Ops:
  0.6 0.7 broadcast_compare_fusion
  1.3 0.8 fusion.1
  2.1 0.1 and.67
  2.2 0.8 copy.17
  3.0 0.1 reshape.162
  3.1 0.8 copy.18
  3.9 0.1 reshape.163
  4.0 0.2 select_reduce_fusion
  4.2 0.7 copy.19
  5.0 11.5 %all-to-all-start = ((s32[128,1,2]{2,1,0:T(1,128)}), s32[128,1,2]{2,1,0:T(1,128)S(1)}, u32[]{:S(2)}, u32[]{:S(2)}) async-start(s32[128,1,2]{2,1,0:T(1,128)} %copy.19), calls=%async_computation | async-start | bytes 131072 | tf_op jit(solution)/shard_map/all_to_all | solution.py:315
  16.5 0.0 copy-start
  16.5 1.4 %copy-done = f32[48,4,16,128]{3,2,1,0:T(8,128)S(1)} copy-done((f32[48,4,16,128]{3,2,1,0:T(8,128)S(1)}, f32[48,4,16,128]{3,2,1,0:T(8,128)}, u32[]{:S(2)}) %copy-start) | copy-done | bytes 1572888
  17.9 0.0 copy-start.1
  17.9 0.8 copy-done.1
  18.7 0.0 copy-start.2
  18.7 0.8 copy-done.2
  19.4 0.0 copy-start.3
  19.4 0.8 copy-done.3
  20.2 0.0 copy-start.4
  20.2 0.8 copy-done.4
  20.9 24.6 %smooth.1 = (f32[48,4,16,128]{3,2,1,0:T(8,128)S(1)}, bf16[64,48,128]{2,1,0:T(8,128)(2,1)S(1)}) custom-call(f32[48,4,16,128]{3,2,1,0:T(8,128)S(1)} %copy-done, f32[4,16,128]{2,1,0:T(8,128)S(1)} %copy-done.1, f32[4,16,128]{2,1,0:T(8,128)S(1)} %copy-done.2, f32[4,16,128]{2,1,0:T(8,128)S(1)} %copy-done.3, f32[4,16,128]{2,1,0:T(8,128)S(1)} %copy-done.4), custom_call_target="tpu_custom_call" | custom-call | tf_op jit(solution)/shard_map/smooth/pallas_call | solution.py:175
  45.5 0.0 all-to-all-done
  45.5 0.5 broadcast.145
  46.0 0.8 reduce.3
  46.8 0.1 reshape.164
  47.0 2.7 %gather_fusion = bf16[256,48,128]{2,1,0:T(8,128)(2,1)} fusion(bf16[64,48,128]{2,1,0:T(8,128)(2,1)S(1)} %get-tuple-element.6.blk, s32[1024]{0:T(1024)S(1)} %pad_clamp_fusion), kind=kCustom, calls=%fused_computation | custom fusion | bytes 6292480 | tf_op jit(solution)/shard_map/gather | solution.py:316
  49.6 9.0 %all-to-all-start.1 = ((bf16[128,2,48,128]{3,2,1,0:T(8,128)(2,1)}), bf16[128,2,48,128]{3,2,1,0:T(8,128)(2,1)}, u32[]{:S(2)}, u32[]{:S(2)}) async-start(bf16[128,2,48,128]{3,2,1,0:T(8,128)(2,1)} %bitcast.25), calls=%async_computation.1 | async-start | bytes 6291456 | tf_op jit(solution)/shard_map/all_to_all | solution.py:317
  58.6 0.2 select_reduce_fusion.1
  58.9 41.2 %all-to-all-done.1 = bf16[128,2,48,128]{3,2,1,0:T(8,128)(2,1)} async-done(((bf16[128,2,48,128]{3,2,1,0:T(8,128)(2,1)}), bf16[128,2,48,128]{3,2,1,0:T(8,128)(2,1)}, u32[]{:S(2)}, u32[]{:S(2)}) %all-to-all-start.1) | async-done | bytes 3145760 | tf_op jit(solution)/shard_map/all_to_all | solution.py:317
  100.0 5.6 %fit.1 = (f32[4,4,16,128]{3,2,1,0:T(8,128)}, f32[48,4,16,128]{3,2,1,0:T(8,128)}) custom-call(s32[256]{0:T(256)S(1)} %fusion.3.target, bf16[256,48,128]{2,1,0:T(8,128)(2,1)} %bitcast.6.replies, bf16[64,48,128]{2,1,0:T(8,128)(2,1)S(1)} %get-tuple-element.6.blk, f32[48,4,16,128]{3,2,1,0:T(8,128)S(1)} %get-tuple-element.7.sm_in), custom_call_target="tpu_custom_call" | custom-call | tf_op jit(solution)/shard_map/fit/pallas_call | solution.py:281
  (7 shorter events, 0.1 us)
Async XLA Ops:
  5.0 40.5 %all-to-all-start = ((s32[128,1,2]{2,1,0:T(1,128)}), s32[128,1,2]{2,1,0:T(1,128)S(1)}, u32[]{:S(2)}, u32[]{:S(2)}) async-start(s32[128,1,2]{2,1,0:T(1,128)} %copy.19), calls=%async_computation | async-start | bytes 131072 | tf_op jit(solution)/shard_map/all_to_all | solution.py:315
  16.5 1.4 %copy-start = (f32[48,4,16,128]{3,2,1,0:T(8,128)S(1)}, f32[48,4,16,128]{3,2,1,0:T(8,128)}, u32[]{:S(2)}) copy-start(f32[48,4,16,128]{3,2,1,0:T(8,128)} %tv.1) | copy-start | bytes 4718596
  17.9 0.8 copy-start.1
  18.7 0.8 copy-start.2
  19.4 0.8 copy-start.3
  20.2 0.8 copy-start.4
  49.6 50.4 %all-to-all-start.1 = ((bf16[128,2,48,128]{3,2,1,0:T(8,128)(2,1)}), bf16[128,2,48,128]{3,2,1,0:T(8,128)(2,1)}, u32[]{:S(2)}, u32[]{:S(2)}) async-start(bf16[128,2,48,128]{3,2,1,0:T(8,128)(2,1)} %bitcast.25), calls=%async_computation.1 | async-start | bytes 6291456 | tf_op jit(solution)/shard_map/all_to_all | solution.py:317

commit v2 on v1

--- a/solution.py
+++ b/solution.py
@@ -29,30 +29,115 @@
     return (x + 1) * XROW + (y + 1) * KV
 
 
+AXES = "xyz"
+LINE = 4
+CORES = 2
+COARSE = 16
+PLANE = LINE * LINE
+ROUTES = (("x", "z", "y"), ("y", "z", "x"), ("z", "x", "y"))
+
+
+def lists_of(meta):
+    lane = lax.broadcasted_iota(jnp.int32, (ROWS, ROWS), 1)
+    sub = lax.broadcasted_iota(jnp.int32, (ROWS, ROWS), 0)
+    diag = lane == sub
+    none = 1 << 20
+
+    def column(row):
+        return jnp.sum(jnp.where(diag, row, 0), axis=1, keepdims=True)
+
+    def line(col):
+        return jnp.sum(jnp.where(diag, col, 0), axis=0, keepdims=True)
+
+    members, keys, owners = [], [], []
+    for h in range(2):
+        entry = meta[h : h + 1]
+        owner = entry >> 6
+        key = (lane[:1] + h * ROWS) * SITES + (entry & (SITES - 1))
+        owners.append(owner)
+        keys.append(key)
+        members.append(owner == sub)
+    first = jnp.minimum(*[jnp.where(m, k, none) for m, k in zip(members, keys)])
+    first = jnp.min(first, axis=1, keepdims=True)
+    first = jnp.where(first >= none, 0, first)
+    second = jnp.maximum(*[jnp.where(m, k, 0) for m, k in zip(members, keys)])
+    second = jnp.max(second, axis=1, keepdims=True)
+    wanted = [line(v) & (SITES - 1) for v in (first, second)]
+    targets = [[] for _ in ROUTES]
+    for h in range(2):
+        own = owners[h]
+        at_first = jnp.sum(jnp.where(members[h], first, 0), axis=0, keepdims=True)
+        place = jnp.where(keys[h] == at_first, 0, 1)
+        at = {"x": (own >> 5) & 3, "z": (own >> 3) & 3, "y": (own >> 1) & 3}
+        for c, (a, u, v) in enumerate(ROUTES):
+            slot = ((at[a] * CORES + (own & 1)) * PLANE + at[v] * LINE + at[u]) * 2 + place
+            targets[c].append(jnp.where(own < 0, -1, slot))
+    coarse = meta[2:3]
+    rank = jnp.sum(jnp.where(sub < lane, column(coarse), 0), axis=0, keepdims=True)
+    hit = (rank == sub[:COARSE]) & (coarse > 0)
+    ids = jnp.sum(jnp.where(hit, lane[:COARSE], 0), axis=1, keepdims=True)
+    ids = jnp.broadcast_to(ids, (COARSE, ROWS))
+    rank = jnp.minimum(rank, COARSE - 1)
+    return wanted, targets, rank, ids
+
+
 def smooth_kernel(
-    tv, cx, cy, cz, sh, sm_out, blk, stage, wa, wb, ka, kb, km, kp, fxs, fxr, fys, fyr,
-    in_sem, out_sem, send_sem, recv_sem
+    tv, cx, cy, cz, sh, meta, sm_out, blk, rb, tgt,
+    stage, coef, wa, wb, ka, kb, km, kp, fxs, fxr, fys, fyr,
+    want, wants, ranks, idv, want_s, rank_s, id_s, pg0, pg1, pg2, sb,
+    in_sem, coef_sem, out_sem, send_sem, recv_sem, want_send, want_recv, rank_send, rank_recv,
+    cast_send, cast_recv, ans_send, ans_recv, own_sem, smem_sem,
 ):
+    pg = (pg0, pg1, pg2)
     i = lax.axis_index("gx")
     j = lax.axis_index("gy")
+    core = lax.rem(j, CORES)
+    at = {"x": i // LINE, "z": lax.rem(i, LINE), "y": j // CORES}
     peers = (
         (lax.rem(i + GX - 1, GX), j),
         (lax.rem(i + 1, GX), j),
         (i, lax.rem(j + GY - 1, GY)),
         (i, lax.rem(j + 1, GY)),
     )
+
+    def device(axis, d, e):
+        moved = dict(at)
+        moved[axis] = lax.rem(at[axis] + d, LINE)
+        return (moved["x"] * LINE + moved["z"], moved["y"] * CORES + lax.rem(core + e, CORES))
+
+    def remote(src, dst, send, recv, peer):
+        return pltpu.make_async_remote_copy(
+            src_ref=src, dst_ref=dst, send_sem=send, recv_sem=recv,
+            device_id=peer, device_id_type=MESH,
+        )
+
     loads = []
+    for n, part in enumerate((cx, cy, cz, sh)):
+        load = pltpu.make_async_copy(part, coef.at[n], coef_sem.at[n])
+        load.start()
+        loads.append(load)
+    coef_loads, loads = loads, []
     for c in range(CHUNKS):
         part = pl.ds(c * KV, KV)
         load = pltpu.make_async_copy(tv.at[part], stage.at[part], in_sem.at[c])
         load.start()
         loads.append(load)
     barrier = pltpu.get_barrier_semaphore()
-    for peer in peers:
+    for peer in peers[:2]:
         pl.semaphore_signal(barrier, inc=1, device_id=peer, device_id_type=MESH)
-
-    ax, ay, az = cx[...], cy[...], cz[...]
-    scale = OMEGA / (2.0 * (ax + ay + az) + sh[...])
+    pl.semaphore_signal(barrier, inc=1, device_id=device("x", 0, 1), device_id_type=MESH)
+    for axis in AXES:
+        for d in range(1, LINE):
+            for e in range(CORES):
+                pl.semaphore_signal(
+                    barrier, inc=1, device_id=device(axis, d, e), device_id_type=MESH
+                )
+    greeted = 3 + len(AXES) * (LINE - 1) * CORES
+
+    for load in coef_loads:
+        load.wait()
+    ax, ay, az = coef[0], coef[1], coef[2]
+    scale = OMEGA / (2.0 * (ax + ay + az) + coef[3])
     ka[...] = ax * scale
     kb[...] = ay * scale
     az = az * scale
@@ -71,13 +156,9 @@
         for d in range(4):
             src, dst = (fxs, fxr) if d < 2 else (fys, fyr)
             out.append(
-                pltpu.make_async_remote_copy(
-                    src_ref=src.at[s, c, d % 2],
-                    dst_ref=dst.at[s, c, 1 - d % 2],
-                    send_sem=send_sem.at[s, c, d],
-                    recv_sem=recv_sem.at[s, c, d],
-                    device_id=peers[d],
-                    device_id_type=MESH,
+                remote(
+                    src.at[s, c, d % 2], dst.at[s, c, 1 - d % 2],
+                    send_sem.at[s, c, d], recv_sem.at[s, c, d], peers[d],
                 )
             )
         return out
@@ -124,14 +205,96 @@
                 )
                 dst[c, pl.ds(base + site_row(0, y), KV)] = new
                 if last:
-                    blk[x * NY + y, pl.ds(c * KV, KV)] = new.astype(BF16)
+                    blk[c, x * NY + y] = new.astype(BF16)
                 below, here = here, above
             return carry
 
         lax.fori_loop(0, NX, plane, 0)
 
-    buffers = (wa, wb)
-    for c in range(CHUNKS):
+    def want_copies():
+        out = []
+        for n, axis in enumerate(AXES):
+            for d in range(LINE):
+                for e in range(CORES):
+                    if d or e:
+                        out.append(
+                            remote(
+                                want, wants.at[n, at[axis] * CORES + core],
+                                want_send.at[n, d, e], want_recv.at[n, d, e], device(axis, d, e),
+                            )
+                        )
+        return out
+
+    def rank_copies(c, step):
+        a, u, v = ROUTES[c]
+        out = []
+        for d in range(1, LINE):
+            if step == 0:
+                ref, peer = ranks.at[c, at[v], at[u]], device(u, d, 0)
+            else:
+                ref, peer = ranks.at[c, at[v]], device(v, d, 0)
+            out.append(
+                remote(ref, ref, rank_send.at[c, step, d], rank_recv.at[c, step, d], peer)
+            )
+        return out
+
+    def cast_copies(c, step):
+        a, u, v = ROUTES[c]
+        out = []
+        for d in (2, 1, 3):
+            if step == 0:
+                ref, peer = pg[c].at[at[v], at[u]], device(u, d, 0)
+            else:
+                ref, peer = pg[c].at[at[v]], device(v, d, 0)
+            out.append(
+                remote(ref, ref, cast_send.at[c, step, d], cast_recv.at[c, step, d], peer)
+            )
+        return out
+
+    def answer(c, d, e):
+        a = ROUTES[c][0]
+        slot = lax.rem(at[a] + d, LINE) * CORES + lax.rem(core + e, CORES)
+        here = at[a] * CORES + core
+        if d == 0 and e == 0:
+            return pltpu.make_async_copy(sb.at[c, slot], rb.at[c, here], own_sem.at[c])
+        return remote(
+            sb.at[c, slot], rb.at[c, here],
+            ans_send.at[c, d, e], ans_recv.at[c, d, e], device(a, d, e),
+        )
+
+    order = [(d, e) for d in (2, 1, 3, 0) for e in range(CORES)]
+
+    def spread(c):
+        a, u, v = ROUTES[c]
+        for r in range(COARSE):
+            pg[c][at[v], at[u], r] = blk[c, id_s[r, 0] & (SITES - 1)]
+        for copy in cast_copies(c, 0):
+            copy.start()
+
+    def spread_more(c):
+        for copy in cast_copies(c, 0):
+            copy.wait_recv()
+        for copy in cast_copies(c, 1):
+            copy.start()
+
+    def reply(c):
+        a, u, v = ROUTES[c]
+        n = AXES.index(a)
+        for copy in cast_copies(c, 1):
+            copy.wait_recv()
+        for d, e in order:
+            slot = lax.rem(at[a] + d, LINE) * CORES + lax.rem(core + e, CORES)
+            for vv in range(LINE):
+                for uu in range(LINE):
+                    whose = {a: at[a], u: uu, v: vv}
+                    owner = whose["x"] * 32 + whose["z"] * 8 + whose["y"] * 2 + core
+                    for p in range(2):
+                        block = want_s[n, slot, p, owner] & (SITES - 1)
+                        rank = rank_s[c, vv, uu, 0, block] & (COARSE - 1)
+                        sb[c, slot, (vv * LINE + uu) * 2 + p] = pg[c][vv, uu, rank]
+            answer(c, d, e).start()
+
+    def transpose_in(c):
         loads[c].wait()
         for x in range(NX):
             for half in range(NY // 8):
@@ -139,69 +302,160 @@
                     wa[c, pl.ds(site_row(x, half * 8) + k, 8, stride=KV), :] = stage[
                         c * KV + k, x, pl.ds(half * 8, 8), :
                     ]
-        if c == 0:
-            pl.semaphore_wait(barrier, 4)
+
+    stores = []
+
+    def transpose_out(c, w):
+        for x in range(NX):
+            for half in range(NY // 8):
+                for k in range(KV):
+                    stage[c * KV + k, x, pl.ds(half * 8, 8), :] = w[
+                        c, pl.ds(site_row(x, half * 8) + k, 8, stride=KV), :
+                    ]
+        part = pl.ds(c * KV, KV)
+        store = pltpu.make_async_copy(stage.at[part], sm_out.at[part], out_sem.at[c])
+        store.start()
+        stores.append(store)
+
+    transpose_in(0)
+    pl.semaphore_wait(barrier, greeted)
+    send_faces(0, 0, wa)
+    for c in range(1, CHUNKS):
+        transpose_in(c)
         send_faces(0, c, wa)
-    stores = []
-    for s in range(SWEEPS):
-        src, dst = buffers[s % 2], buffers[(s + 1) % 2]
-        for c in range(CHUNKS):
-            fill_halo(s, c, src)
-            sweep(c, src, dst, s == SWEEPS - 1)
-            if s < SWEEPS - 1:
-                send_faces(s + 1, c, dst)
-            else:
-                for x in range(NX):
-                    for half in range(NY // 8):
-                        for k in range(KV):
-                            stage[c * KV + k, x, pl.ds(half * 8, 8), :] = dst[
-                                c, pl.ds(site_row(x, half * 8) + k, 8, stride=KV), :
-                            ]
-                part = pl.ds(c * KV, KV)
-                store = pltpu.make_async_copy(stage.at[part], sm_out.at[part], out_sem.at[c])
-                store.start()
-                stores.append(store)
+
+    wanted, targets, rank, ids = lists_of(meta[...])
+    idv[...] = ids
+    id_copy = pltpu.make_async_copy(idv, id_s, smem_sem.at[0])
+    id_copy.start()
+    for p in range(2):
+        want[p : p + 1] = wanted[p]
+        for n, axis in enumerate(AXES):
+            wants[n, at[axis] * CORES + core, p : p + 1] = wanted[p]
+    tgt[...] = jnp.zeros_like(tgt)
+    for c in range(CHUNKS):
+        a, u, v = ROUTES[c]
+        ranks[c, at[v], at[u]] = rank
+        for h in range(2):
+            tgt[2 * c + h : 2 * c + h + 1] = targets[c][h]
+        for copy in rank_copies(c, 0):
+            copy.start()
+    for copy in want_copies():
+        copy.start()
+
+    for c in range(CHUNKS):
+        fill_halo(0, c, wa)
+        sweep(c, wa, wb, False)
+        send_faces(1, c, wb)
+    for c in range(CHUNKS):
+        for copy in rank_copies(c, 0):
+            copy.wait_recv()
+        for copy in rank_copies(c, 1):
+            copy.start()
+    for c in range(CHUNKS):
+        fill_halo(1, c, wb)
+        sweep(c, wb, wa, False)
+        send_faces(2, c, wa)
+    for copy in want_copies():
+        copy.wait_recv()
+    want_copy = pltpu.make_async_copy(wants, want_s, smem_sem.at[1])
+    want_copy.start()
+    for c in range(CHUNKS):
+        for copy in rank_copies(c, 1):
+            copy.wait_recv()
+    rank_copy = pltpu.make_async_copy(ranks, rank_s, smem_sem.at[2])
+    rank_copy.start()
+    id_copy.wait()
+    for c in range(CHUNKS):
+        fill_halo(2, c, wa)
+        sweep(c, wa, wb, True)
+        spread(c)
+        if c > 0:
+            spread_more(c - 1)
+    want_copy.wait()
+    rank_copy.wait()
+    spread_more(CHUNKS - 1)
+    for c in range(CHUNKS):
+        reply(c)
+        transpose_out(c, wb)
+
     for s in range(SWEEPS):
         for c in range(CHUNKS):
             for copy in copies(s, c):
                 copy.wait_send()
+    for copy in want_copies():
+        copy.wait_send()
+    for c in range(CHUNKS):
+        for step in range(2):
+            for copy in rank_copies(c, step) + cast_copies(c, step):
+                copy.wait_send()
+        for d, e in order:
+            copy = answer(c, d, e)
+            if d or e:
+                copy.wait_send()
+                copy.wait_recv()
+            else:
+                copy.wait()
     for store in stores:
         store.wait()
 
 
-def smooth(test_vectors, coef_x, coef_y, coef_z, shift):
+def smooth(test_vectors, coef_x, coef_y, coef_z, shift, meta):
     vmem = pl.BlockSpec(memory_space=pltpu.VMEM)
     anywhere = pl.BlockSpec(memory_space=pl.ANY)
+    cells = pltpu.VMEM((NX, NY, ROWS), F32)
+    plane = pltpu.VMEM((LINE, LINE, COARSE, KV, ROWS), BF16)
+    dma = pltpu.SemaphoreType.DMA
     return pl.pallas_call(
         smooth_kernel,
         out_shape=(
             jax.ShapeDtypeStruct((VECS, NX, NY, ROWS), F32),
-            jax.ShapeDtypeStruct((SITES, VECS, ROWS), BF16),
+            jax.ShapeDtypeStruct((CHUNKS, SITES, KV, ROWS), BF16),
+            jax.ShapeDtypeStruct((CHUNKS, LINE * CORES, 2 * PLANE, KV, ROWS), BF16),
+            jax.ShapeDtypeStruct((8, ROWS), jnp.int32),
         ),
-        in_specs=[anywhere, vmem, vmem, vmem, vmem],
-        out_specs=(anywhere, vmem),
+        in_specs=[anywhere] * 5 + [vmem],
+        out_specs=(anywhere, vmem, anywhere, vmem),
         scratch_shapes=[
             pltpu.VMEM((VECS, NX, NY, ROWS), F32),
+            pltpu.VMEM((4, NX, NY, ROWS), F32),
             pltpu.VMEM((CHUNKS, EXT, ROWS), F32),
             pltpu.VMEM((CHUNKS, EXT, ROWS), F32),
-            pltpu.VMEM((NX, NY, ROWS), F32),
-            pltpu.VMEM((NX, NY, ROWS), F32),
-            pltpu.VMEM((NX, NY, ROWS), F32),
-            pltpu.VMEM((NX, NY, ROWS), F32),
+            cells, cells, cells, cells,
             pltpu.VMEM((SWEEPS, CHUNKS, 2, NY * KV, ROWS), BF16),
             pltpu.VMEM((SWEEPS, CHUNKS, 2, NY * KV, ROWS), BF16),
             pltpu.VMEM((SWEEPS, CHUNKS, 2, NX * KV, ROWS), BF16),
             pltpu.VMEM((SWEEPS, CHUNKS, 2, NX * KV, ROWS), BF16),
-            pltpu.SemaphoreType.DMA((CHUNKS,)),
-            pltpu.SemaphoreType.DMA((CHUNKS,)),
-            pltpu.SemaphoreType.DMA((SWEEPS, CHUNKS, 4)),
-            pltpu.SemaphoreType.DMA((SWEEPS, CHUNKS, 4)),
+            pltpu.VMEM((2, ROWS), jnp.int32),
+            pltpu.VMEM((len(AXES), LINE * CORES, 2, ROWS), jnp.int32),
+            pltpu.VMEM((CHUNKS, LINE, LINE, 1, ROWS), jnp.int32),
+            pltpu.VMEM((COARSE, ROWS), jnp.int32),
+            pltpu.SMEM((len(AXES), LINE * CORES, 2, ROWS), jnp.int32),
+            pltpu.SMEM((CHUNKS, LINE, LINE, 1, ROWS), jnp.int32),
+            pltpu.SMEM((COARSE, ROWS), jnp.int32),
+            plane, plane, plane,
+            pltpu.VMEM((CHUNKS, LINE * CORES, 2 * PLANE, KV, ROWS), BF16),
+            dma((CHUNKS,)),
+            dma((4,)),
+            dma((CHUNKS,)),
+            dma((SWEEPS, CHUNKS, 4)),
+            dma((SWEEPS, CHUNKS, 4)),
+            dma((len(AXES), LINE, CORES)),
+            dma((len(AXES), LINE, CORES)),
+            dma((CHUNKS, 2, LINE)),
+            dma((CHUNKS, 2, LINE)),
+            dma((CHUNKS, 2, LINE)),
+            dma((CHUNKS, 2, LINE)),
+            dma((CHUNKS, LINE, CORES)),
+            dma((CHUNKS, LINE, CORES)),
+            dma((CHUNKS,)),
+            dma((3,)),
         ],
         compiler_params=pltpu.CompilerParams(
             collective_id=0, has_side_effects=True, vmem_limit_bytes=48 * 1024 * 1024
         ),
         name="smooth",
-    )(test_vectors, coef_x, coef_y, coef_z, shift)
+    )(test_vectors, coef_x, coef_y, coef_z, shift, meta)
 
 
 def solve_rows(gram, rhs):
@@ -243,18 +497,19 @@
     move.start()
 
     def block(b, carry):
-        values = []
-        for s in range(SLOTS):
-            at = target[b * SLOTS + s]
-            live = at >= 0
-            found = replies[jnp.maximum(at, 0)].astype(F32)
-            values.append(jnp.where(live, found, 0.0))
-        values.append(blk[b].astype(F32))
-        for n, (s, t) in enumerate(PAIRS):
-            prod = values[s] * values[t]
-            acc = prod[0:8]
-            for h in range(1, VECS // 8):
-                acc = acc + prod[8 * h : 8 * h + 8]
+        accs = [None] * len(PAIRS)
+        for c in range(CHUNKS):
+            values = []
+            for s in range(SLOTS):
+                at = target[2 * c + b // 32, lax.rem(b, 32) * SLOTS + s]
+                found = replies[c, jnp.maximum(at, 0)].astype(F32)
+                values.append(jnp.where(at >= 0, found, 0.0))
+            values.append(blk[c, b].astype(F32))
+            for n, (s, t) in enumerate(PAIRS):
+                prod = values[s] * values[t]
+                part = prod[0:8] + prod[8:16]
+                accs[n] = part if c == 0 else accs[n] + part
+        for n, acc in enumerate(accs):
             sums[n, pl.ds(pl.multiple_of(b * 8, 8), 8), :] = acc
         return carry
 
@@ -298,24 +553,13 @@
 def per_device(
     test_vectors, coef_x, coef_y, coef_z, shift, cf_split, nbr_count, nbr_owner, nbr_block
 ):
-    devices = GX * GY
     entries = SITES * SLOTS
-    capacity = 2
-    live = ((cf_split == 0)[..., None] & (jnp.arange(SLOTS) < nbr_count[..., None])).reshape(entries)
-    owner = nbr_owner.reshape(entries)
-    local = nbr_block.reshape(entries)
-    member = (owner[:, None] == jnp.arange(devices)[None, :]) & live[:, None]
-    key = jnp.arange(entries) * SITES + local
-    first = jnp.min(jnp.where(member, key[:, None], entries * SITES), axis=0)
-    second = jnp.max(jnp.where(member, key[:, None], -1), axis=0)
-    table = jnp.stack([first % SITES, jnp.maximum(second, 0) % SITES], axis=1)
-    first_here = jnp.sum(jnp.where(member, first[None, :], 0), axis=1)
-    target = jnp.where(live, owner * capacity + (key != first_here), -1)
-    sm, blk = smooth(test_vectors, coef_x, coef_y, coef_z, shift)
-    wanted = lax.all_to_all(table, ("gx", "gy"), split_axis=0, concat_axis=0, tiled=True)
-    found = blk[wanted.reshape(-1)].reshape(devices, capacity, VECS, ROWS)
-    replies = lax.all_to_all(found, ("gx", "gy"), split_axis=0, concat_axis=0, tiled=True)
-    replies = replies.reshape(devices * capacity, VECS, ROWS)
+    live = (cf_split == 0)[..., None] & (jnp.arange(SLOTS) < nbr_count[..., None])
+    listed = jnp.where(live, nbr_owner * SITES + nbr_block, -1).reshape(entries // ROWS, ROWS)
+    coarse = jnp.pad(cf_split.reshape(1, SITES), ((0, 5), (0, ROWS - SITES)))
+    meta = jnp.concatenate([listed, coarse], axis=0)
+    sm, blk, replies, target = smooth(test_vectors, coef_x, coef_y, coef_z, shift, meta)
+    replies = replies.reshape(CHUNKS, LINE * CORES * 2 * PLANE, KV, ROWS)
     weights, smoothed = fit(target, replies, blk, sm)
     return (smoothed, weights)
 

time: 106 us -> 86.7 us (0.82)
  Pallas kernels: 30.2 us -> 75.3 us
  waiting for transfers between devices: 41.2 us -> 0 us
  starting transfers between devices: 20.5 us -> 0 us
  local copies, waits for them, and re-layouts: 10.4 us -> 7.13 us
    pallas_call x1, Pallas kernels: 24.6 us -> 69.8 us  [smooth(): pl.pallas_call(smooth_kernel, out_shape=(jax.ShapeDtypeStruct((VECS, NX,...]
    all_to_all x2 -> x0, waiting for transfers between devices: 41.2 us -> none  [the longest x1 41.2 us: per_device(): lax.all_to_all(found, ('gx', 'gy'), split_axis=0, concat_axis=0, tiled=True)]
    all_to_all x2 -> x0, starting transfers between devices: 20.5 us -> none  [the longest x1 11.5 us: per_device(): lax.all_to_all(table, ('gx', 'gy'), split_axis=0, concat_axis=0, tiled=True)]
    gather x1 -> x0, local copies, waits for them, and re-layouts: 2.65 us -> none  [per_device(): found = blk[wanted.reshape(-1)].reshape(devices, capacity, VECS, ROWS)]
    unnamed x0 -> x1, other arithmetic: none -> 1.34 us
    all_to_all x2 -> x0, local copies, waits for them, and re-layouts: 1.25 us -> none  [per_device(): lax.all_to_all(table, ('gx', 'gy'), split_axis=0, concat_axis=0, tiled=True)]
    unnamed x13 -> x14, local copies, waits for them, and re-layouts: 6.03 us -> 6.84 us
  transfers between devices with their start and end apart: 2 -> 0, of which waited for: 1 -> 0; matrix products, arithmetic and copies ran while one was open for 0% -> 0% of each run, Pallas kernels for 23% -> 0%
where the time goes in v2:
time: 86.7 us; the launch traced here: 85.9 us
  Pallas kernels  75.3 us (87%)
  local copies, waits for them, and re-layouts  7.13 us (8%)
  other arithmetic  2.76 us (3%)
    pallas_call x1, Pallas kernels, smooth(): pl.pallas_call(smooth_kernel, out_shape=(jax.ShapeDtypeStruct((VECS, NX,...  69.8 us
    unnamed x14, local copies, waits for them, and re-layouts  6.84 us
    pallas_call x1, Pallas kernels, fit(): pl.pallas_call(weights_kernel, out_shape=(jax.ShapeDtypeStruct((SLOTS, NX...  5.54 us

profile of v2, /device:TPU:1, one launch (start us, length us, event | category | flops | bytes accessed | tf_op | source)
XLA Modules:
  0.0 85.9 jit_solution(9387636900656720389)
XLA Ops:
  0.6 0.5 broadcast.26
  1.1 1.3 %reduce.3 = s32[4,16]{1,0:T(4,128)S(1)} reduce(s32[4,16,1]{1,2,0:T(1,128)} %param.14, s32[]{:T(128)} %broadcast.26), dimensions={2}, to_apply=%param.14.reduce_sub_computation.3 | reduce | bytes 516 | tf_op args[5]
  2.5 0.1 reshape.32
  2.6 0.7 broadcast_compare_fusion
  3.3 0.7 add_select_fusion
  4.0 0.1 copy.12
  4.1 0.1 reshape.31
  4.2 0.0 copy-start.1
  4.2 1.4 %copy-done.1 = f32[48,4,16,128]{3,2,1,0:T(8,128)S(1)} copy-done((f32[48,4,16,128]{3,2,1,0:T(8,128)S(1)}, f32[48,4,16,128]{3,2,1,0:T(8,128)}, u32[]{:S(2)}) %copy-start.1) | copy-done | bytes 1572888
  5.6 0.0 copy-start.2
  5.6 0.8 copy-done.2
  6.4 0.0 copy-start.3
  6.4 0.8 copy-done.3
  7.1 0.0 copy-start.4
  7.1 0.8 copy-done.4
  7.9 0.0 copy-start.5
  7.9 0.8 copy-done.5
  8.7 69.8 %smooth.1 = (f32[48,4,16,128]{3,2,1,0:T(8,128)S(1)}, bf16[3,64,16,128]{3,2,1,0:T(8,128)(2,1)S(1)}, bf16[3,8,32,16,128]{4,3,2,1,0:T(8,128)(2,1)}, s32[8,128]{1,0:T(8,128)S(1)}) custom-call(f32[48,4,16,128]{3,2,1,0:T(8,128)S(1)} %copy-done.1, f32[4,16,128]{2,1,0:T(8,128)S(1)} %copy-done.2, f32[4,16,128]{2,1,0:T(8,128)S(1)} %copy-done.3, ...), custom_call_target="tpu_custom_call" | custom-call | tf_op jit(solution)/shard_map/smooth/pallas_call | solution.py:409
  78.5 0.0 copy-start
  78.5 1.9 %copy-done = bf16[3,8,32,16,128]{4,3,2,1,0:T(8,128)(2,1)S(1)} copy-done((bf16[3,8,32,16,128]{4,3,2,1,0:T(8,128)(2,1)S(1)}, bf16[3,8,32,16,128]{4,3,2,1,0:T(8,128)(2,1)}, u32[]{:S(2)}) %copy-start) | copy-done | bytes 3145752
  80.4 5.5 %fit.1 = (f32[4,4,16,128]{3,2,1,0:T(8,128)}, f32[48,4,16,128]{3,2,1,0:T(8,128)}) custom-call(s32[8,128]{1,0:T(8,128)S(1)} %get-tuple-element.8.target, bf16[3,256,16,128]{3,2,1,0:T(8,128)(2,1)S(1)} %bitcast.10, bf16[3,64,16,128]{3,2,1,0:T(8,128)(2,1)S(1)} %get-tuple-element.10.blk, f32[48,4,16,128]{3,2,1,0:T(8,128)S(1)} %get-tuple-element.11.sm_in), custom_call_target="tpu_custom_call" | custom-call | tf_op jit(solution)/shard_map/fit/pallas_call | solution.py:536
  (2 shorter events, 0.0 us)
Async XLA Ops:
  4.2 1.4 %copy-start.1 = (f32[48,4,16,128]{3,2,1,0:T(8,128)S(1)}, f32[48,4,16,128]{3,2,1,0:T(8,128)}, u32[]{:S(2)}) copy-start(f32[48,4,16,128]{3,2,1,0:T(8,128)} %tv.1) | copy-start | bytes 4718596
  5.6 0.8 copy-start.2
  6.4 0.8 copy-start.3
  7.1 0.8 copy-start.4
  7.9 0.8 copy-start.5
  78.5 1.9 %copy-start = (bf16[3,8,32,16,128]{4,3,2,1,0:T(8,128)(2,1)S(1)}, bf16[3,8,32,16,128]{4,3,2,1,0:T(8,128)(2,1)}, u32[]{:S(2)}) copy-start(bf16[3,8,32,16,128]{4,3,2,1,0:T(8,128)(2,1)} %get-tuple-element.9) | copy-start | bytes 9437188

commit v3 on v2

--- a/solution.py
+++ b/solution.py
@@ -84,9 +84,9 @@
 def smooth_kernel(
     tv, cx, cy, cz, sh, meta, sm_out, blk, rb, tgt,
     stage, coef, wa, wb, ka, kb, km, kp, fxs, fxr, fys, fyr,
-    want, wants, ranks, idv, want_s, rank_s, id_s, pg0, pg1, pg2, sb,
+    want, wants, ranks, idv, want_s, rank_s, id_s, pg0, pg1, pg2, sb, fb,
     in_sem, coef_sem, out_sem, send_sem, recv_sem, want_send, want_recv, rank_send, rank_recv,
-    cast_send, cast_recv, ans_send, ans_recv, own_sem, smem_sem,
+    cast_send, cast_recv, ans_send, ans_recv, fwd_send, fwd_recv, own_sem, smem_sem,
 ):
     pg = (pg0, pg1, pg2)
     i = lax.axis_index("gx")
@@ -240,16 +240,22 @@
 
     def cast_copies(c, step):
         a, u, v = ROUTES[c]
-        out = []
-        for d in (2, 1, 3):
-            if step == 0:
-                ref, peer = pg[c].at[at[v], at[u]], device(u, d, 0)
-            else:
-                ref, peer = pg[c].at[at[v]], device(v, d, 0)
-            out.append(
-                remote(ref, ref, cast_send.at[c, step, d], cast_recv.at[c, step, d], peer)
+        axis = v if step else u
+
+        def part(back, half):
+            pos = lax.rem(at[axis] + LINE - back, LINE)
+            if step:
+                return pg[c].at[pos, pl.ds(half * (LINE // 2), LINE // 2)]
+            return pg[c].at[at[v], pos, pl.ds(half * (COARSE // 2), COARSE // 2)]
+
+        plan = ((0, 0, 1), (0, 1, 3), (0, 1, 1), (0, 0, 3), (1, 0, 1), (3, 1, 3))
+        return [
+            remote(
+                part(back, half), part(back, half),
+                cast_send.at[c, step, n], cast_recv.at[c, step, n], device(axis, d, 0),
             )
-        return out
+            for n, (back, half, d) in enumerate(plan)
+        ]
 
     def answer(c, d, e):
         a = ROUTES[c][0]
@@ -257,9 +263,17 @@
         here = at[a] * CORES + core
         if d == 0 and e == 0:
             return pltpu.make_async_copy(sb.at[c, slot], rb.at[c, here], own_sem.at[c])
+        dst, peer = rb.at[c, here], device(a, d, e)
+        if d == 2:
+            dst, peer = fb.at[c, e], device(a, 1 + 2 * e, 0)
+        return remote(sb.at[c, slot], dst, ans_send.at[c, d, e], ans_recv.at[c, d, e], peer)
+
+    def forward(c, e):
+        a = ROUTES[c][0]
+        origin = lax.rem(at[a] + 3 - 2 * e, LINE) * CORES + core
         return remote(
-            sb.at[c, slot], rb.at[c, here],
-            ans_send.at[c, d, e], ans_recv.at[c, d, e], device(a, d, e),
+            fb.at[c, e], rb.at[c, origin], fwd_send.at[c, e], fwd_recv.at[c, e],
+            device(a, 1 + 2 * e, e),
         )
 
     order = [(d, e) for d in (2, 1, 3, 0) for e in range(CORES)]
@@ -268,20 +282,28 @@
         a, u, v = ROUTES[c]
         for r in range(COARSE):
             pg[c][at[v], at[u], r] = blk[c, id_s[r, 0] & (SITES - 1)]
-        for copy in cast_copies(c, 0):
+        for copy in cast_copies(c, 0)[:4]:
             copy.start()
 
+    def pass_on(c, step):
+        all_copies = cast_copies(c, step)
+        for n in range(2):
+            all_copies[n].wait_recv()
+            all_copies[4 + n].start()
+
+    def gathered(c, step):
+        for copy in cast_copies(c, step)[2:]:
+            copy.wait_recv()
+
     def spread_more(c):
-        for copy in cast_copies(c, 0):
-            copy.wait_recv()
-        for copy in cast_copies(c, 1):
+        gathered(c, 0)
+        for copy in cast_copies(c, 1)[:4]:
             copy.start()
 
     def reply(c):
         a, u, v = ROUTES[c]
         n = AXES.index(a)
-        for copy in cast_copies(c, 1):
-            copy.wait_recv()
+        gathered(c, 1)
         for d, e in order:
             slot = lax.rem(at[a] + d, LINE) * CORES + lax.rem(core + e, CORES)
             for vv in range(LINE):
@@ -294,6 +316,11 @@
                         sb[c, slot, (vv * LINE + uu) * 2 + p] = pg[c][vv, uu, rank]
             answer(c, d, e).start()
 
+    def reply_on(c):
+        for e in range(2):
+            answer(c, 2, e).wait_recv()
+            forward(c, e).start()
+
     def transpose_in(c):
         loads[c].wait()
         for x in range(NX):
@@ -371,13 +398,26 @@
         sweep(c, wa, wb, True)
         spread(c)
         if c > 0:
-            spread_more(c - 1)
+            pass_on(c - 1, 0)
+        if c > 1:
+            spread_more(c - 2)
     want_copy.wait()
     rank_copy.wait()
-    spread_more(CHUNKS - 1)
-    for c in range(CHUNKS):
-        reply(c)
-        transpose_out(c, wb)
+    pass_on(2, 0)
+    spread_more(1)
+    transpose_out(0, wb)
+    pass_on(0, 1)
+    spread_more(2)
+    transpose_out(1, wb)
+    pass_on(1, 1)
+    reply(0)
+    pass_on(2, 1)
+    reply(1)
+    reply_on(0)
+    reply(2)
+    reply_on(1)
+    transpose_out(2, wb)
+    reply_on(2)
 
     for s in range(SWEEPS):
         for c in range(CHUNKS):
@@ -393,9 +433,13 @@
             copy = answer(c, d, e)
             if d or e:
                 copy.wait_send()
-                copy.wait_recv()
+                if d != 2:
+                    copy.wait_recv()
             else:
                 copy.wait()
+        for e in range(2):
+            forward(c, e).wait_send()
+            forward(c, e).wait_recv()
     for store in stores:
         store.wait()
 
@@ -435,6 +479,7 @@
             pltpu.SMEM((COARSE, ROWS), jnp.int32),
             plane, plane, plane,
             pltpu.VMEM((CHUNKS, LINE * CORES, 2 * PLANE, KV, ROWS), BF16),
+            pltpu.VMEM((CHUNKS, CORES, 2 * PLANE, KV, ROWS), BF16),
             dma((CHUNKS,)),
             dma((4,)),
             dma((CHUNKS,)),
@@ -444,15 +489,17 @@
             dma((len(AXES), LINE, CORES)),
             dma((CHUNKS, 2, LINE)),
             dma((CHUNKS, 2, LINE)),
-            dma((CHUNKS, 2, LINE)),
-            dma((CHUNKS, 2, LINE)),
+            dma((CHUNKS, 2, 6)),
+            dma((CHUNKS, 2, 6)),
             dma((CHUNKS, LINE, CORES)),
             dma((CHUNKS, LINE, CORES)),
+            dma((CHUNKS, CORES)),
+            dma((CHUNKS, CORES)),
             dma((CHUNKS,)),
             dma((3,)),
         ],
         compiler_params=pltpu.CompilerParams(
-            collective_id=0, has_side_effects=True, vmem_limit_bytes=48 * 1024 * 1024
+            collective_id=0, has_side_effects=True, vmem_limit_bytes=60 * 1024 * 1024
         ),
         name="smooth",
     )(test_vectors, coef_x, coef_y, coef_z, shift, meta)

time: 86.7 us -> 81.7 us (0.942)
  Pallas kernels: 75.3 us -> 71.4 us
  local copies, waits for them, and re-layouts: 7.13 us -> 5.91 us
    pallas_call x1, Pallas kernels: 69.8 us -> 65.8 us  [smooth(): pl.pallas_call(smooth_kernel, out_shape=(jax.ShapeDtypeStruct((VECS, NX,...]
    unnamed x14 -> x10, local copies, waits for them, and re-layouts: 6.84 us -> 5.62 us
where the time goes in v3:
time: 81.7 us; the launch traced here: 81.3 us
  Pallas kernels  71.4 us (87%)
  local copies, waits for them, and re-layouts  5.91 us (7%)
  other arithmetic  3.36 us (4%)
    pallas_call x1, Pallas kernels, smooth(): pl.pallas_call(smooth_kernel, out_shape=(jax.ShapeDtypeStruct((VECS, NX,...  65.8 us
    unnamed x10, local copies, waits for them, and re-layouts  5.62 us
    pallas_call x1, Pallas kernels, fit(): pl.pallas_call(weights_kernel, out_shape=(jax.ShapeDtypeStruct((SLOTS, NX...  5.54 us

profile of v3, /device:TPU:1, one launch (start us, length us, event | category | flops | bytes accessed | tf_op | source)
XLA Modules:
  0.0 81.3 jit_solution(3303603877430075565)
XLA Ops:
  0.6 0.5 broadcast.26
  1.1 1.3 %reduce.3 = s32[4,16]{1,0:T(4,128)S(1)} reduce(s32[4,16,1]{1,2,0:T(1,128)} %param.14, s32[]{:T(128)} %broadcast.26), dimensions={2}, to_apply=%param.14.reduce_sub_computation.3 | reduce | bytes 516 | tf_op args[5]
  2.5 0.1 reshape.32
  2.6 0.7 broadcast_compare_fusion
  3.3 0.7 add_select_fusion
  4.0 0.1 copy.12
  4.1 0.1 reshape.31
  4.2 0.6 pad_add_fusion.meta
  4.8 65.8 %smooth.1 = (f32[48,4,16,128]{3,2,1,0:T(8,128)}, bf16[3,64,16,128]{3,2,1,0:T(8,128)(2,1)}, bf16[3,8,32,16,128]{4,3,2,1,0:T(8,128)(2,1)}, s32[8,128]{1,0:T(8,128)}) custom-call(f32[48,4,16,128]{3,2,1,0:T(8,128)} %tv.1, f32[4,16,128]{2,1,0:T(8,128)} %cx.1, f32[4,16,128]{2,1,0:T(8,128)} %cy.1, f32[4,16,128]{2,1,0:T(8,128)} %cz.1, f32[4,16,128]{2,1,0:T(8,128)} %sh.1, ...), custom_call_target="tpu_custom_call" | custom-call | tf_op jit(solution)/shard_map/smooth/pallas_call | solution.py:453
  70.6 0.0 copy-start
  70.7 1.9 %copy-done = bf16[3,8,32,16,128]{4,3,2,1,0:T(8,128)(2,1)S(1)} copy-done((bf16[3,8,32,16,128]{4,3,2,1,0:T(8,128)(2,1)S(1)}, bf16[3,8,32,16,128]{4,3,2,1,0:T(8,128)(2,1)}, u32[]{:S(2)}) %copy-start) | copy-done | bytes 3145752
  72.5 0.0 copy-start.1
  72.5 1.4 %copy-done.1 = f32[48,4,16,128]{3,2,1,0:T(8,128)S(1)} copy-done((f32[48,4,16,128]{3,2,1,0:T(8,128)S(1)}, f32[48,4,16,128]{3,2,1,0:T(8,128)}, u32[]{:S(2)}) %copy-start.1) | copy-done | bytes 1572888
  73.9 0.0 copy-start.2
  73.9 1.1 %copy-done.2 = bf16[3,64,16,128]{3,2,1,0:T(8,128)(2,1)S(1)} copy-done((bf16[3,64,16,128]{3,2,1,0:T(8,128)(2,1)S(1)}, bf16[3,64,16,128]{3,2,1,0:T(8,128)(2,1)}, u32[]{:S(2)}) %copy-start.2) | copy-done | bytes 786456
  75.1 0.0 copy-start.3
  75.1 0.7 copy-done.3
  75.8 5.5 %fit.1 = (f32[4,4,16,128]{3,2,1,0:T(8,128)}, f32[48,4,16,128]{3,2,1,0:T(8,128)}) custom-call(s32[8,128]{1,0:T(8,128)S(1)} %copy-done.3, bf16[3,256,16,128]{3,2,1,0:T(8,128)(2,1)S(1)} %bitcast.10, bf16[3,64,16,128]{3,2,1,0:T(8,128)(2,1)S(1)} %copy-done.2, f32[48,4,16,128]{3,2,1,0:T(8,128)S(1)} %copy-done.1), custom_call_target="tpu_custom_call" | custom-call | tf_op jit(solution)/shard_map/fit/pallas_call | solution.py:583
  (1 shorter events, 0.0 us)
Async XLA Ops:
  70.6 1.9 %copy-start = (bf16[3,8,32,16,128]{4,3,2,1,0:T(8,128)(2,1)S(1)}, bf16[3,8,32,16,128]{4,3,2,1,0:T(8,128)(2,1)}, u32[]{:S(2)}) copy-start(bf16[3,8,32,16,128]{4,3,2,1,0:T(8,128)(2,1)} %get-tuple-element.9) | copy-start | bytes 9437188
  72.5 1.4 %copy-start.1 = (f32[48,4,16,128]{3,2,1,0:T(8,128)S(1)}, f32[48,4,16,128]{3,2,1,0:T(8,128)}, u32[]{:S(2)}) copy-start(f32[48,4,16,128]{3,2,1,0:T(8,128)} %get-tuple-element.11.sm_in) | copy-start | bytes 4718596
  73.9 1.1 %copy-start.2 = (bf16[3,64,16,128]{3,2,1,0:T(8,128)(2,1)S(1)}, bf16[3,64,16,128]{3,2,1,0:T(8,128)(2,1)}, u32[]{:S(2)}) copy-start(bf16[3,64,16,128]{3,2,1,0:T(8,128)(2,1)} %get-tuple-element.10.blk) | copy-start | bytes 2359300
  75.1 0.7 copy-start.3

commit v4 on v3

--- a/solution.py
+++ b/solution.py
@@ -34,7 +34,7 @@
 CORES = 2
 COARSE = 16
 PLANE = LINE * LINE
-ROUTES = (("x", "z", "y"), ("y", "z", "x"), ("z", "x", "y"))
+ROUTES = (("x", "z", "y"), ("y", "x", "z"), ("z", "y", "x"))
 
 
 def lists_of(meta):
@@ -592,7 +592,7 @@
             pltpu.VMEM((len(PAIRS), SITES * 8, ROWS), F32),
             pltpu.SemaphoreType.DMA,
         ],
-        compiler_params=pltpu.CompilerParams(vmem_limit_bytes=48 * 1024 * 1024),
+        compiler_params=pltpu.CompilerParams(vmem_limit_bytes=60 * 1024 * 1024),
         name="fit",
     )(target, replies, blk, sm)
 

time: 81.7 us -> 129 us (1.58)
  Pallas kernels: 71.4 us -> 123 us
  local copies, waits for them, and re-layouts: 5.91 us -> 0.81 us
    pallas_call x1, Pallas kernels: 5.54 us -> 51.5 us  [fit(): pl.pallas_call(weights_kernel, out_shape=(jax.ShapeDtypeStruct((SLOTS, NX...]
    pallas_call x1, Pallas kernels: 65.8 us -> 71.9 us  [smooth(): pl.pallas_call(smooth_kernel, out_shape=(jax.ShapeDtypeStruct((VECS, NX,...]
    unnamed x10 -> x2, local copies, waits for them, and re-layouts: 5.62 us -> 0.52 us
where the time goes in v4:
time: 129 us; the launch traced here: 128 us
  Pallas kernels  123 us (95%)
  other arithmetic  3.36 us (3%)
    pallas_call x1, Pallas kernels, smooth(): pl.pallas_call(smooth_kernel, out_shape=(jax.ShapeDtypeStruct((VECS, NX,...  71.9 us
    pallas_call x1, Pallas kernels, fit(): pl.pallas_call(weights_kernel, out_shape=(jax.ShapeDtypeStruct((SLOTS, NX...  51.5 us

profile of v4, /device:TPU:1, one launch (start us, length us, event | category | flops | bytes accessed | tf_op | source)
XLA Modules:
  0.0 128.2 jit_solution(4143635451995974463)
XLA Ops:
  0.6 0.5 broadcast.26
  1.1 1.3 %reduce.3 = s32[4,16]{1,0:T(4,128)S(1)} reduce(s32[4,16,1]{1,2,0:T(1,128)} %param.14, s32[]{:T(128)} %broadcast.26), dimensions={2}, to_apply=%param.14.reduce_sub_computation.3 | reduce | bytes 516 | tf_op args[5]
  2.5 0.1 reshape.32
  2.6 0.7 broadcast_compare_fusion
  3.3 0.7 add_select_fusion
  4.0 0.1 copy.12
  4.1 0.1 reshape.31
  4.2 0.6 pad_add_fusion.meta
  4.8 71.9 %smooth.1 = (f32[48,4,16,128]{3,2,1,0:T(8,128)}, bf16[3,64,16,128]{3,2,1,0:T(8,128)(2,1)}, bf16[3,8,32,16,128]{4,3,2,1,0:T(8,128)(2,1)}, s32[8,128]{1,0:T(8,128)}) custom-call(f32[48,4,16,128]{3,2,1,0:T(8,128)} %tv.1, f32[4,16,128]{2,1,0:T(8,128)} %cx.1, f32[4,16,128]{2,1,0:T(8,128)} %cy.1, f32[4,16,128]{2,1,0:T(8,128)} %cz.1, f32[4,16,128]{2,1,0:T(8,128)} %sh.1, ...), custom_call_target="tpu_custom_call" | custom-call | tf_op jit(solution)/shard_map/smooth/pallas_call | solution.py:453
  76.7 51.5 %fit.1 = (f32[4,4,16,128]{3,2,1,0:T(8,128)}, f32[48,4,16,128]{3,2,1,0:T(8,128)}) custom-call(s32[8,128]{1,0:T(8,128)} %get-tuple-element.8.target, bf16[3,256,16,128]{3,2,1,0:T(8,128)(2,1)} %bitcast.10, bf16[3,64,16,128]{3,2,1,0:T(8,128)(2,1)} %get-tuple-element.10.blk, f32[48,4,16,128]{3,2,1,0:T(8,128)} %get-tuple-element.11.sm_in), custom_call_target="tpu_custom_call" | custom-call | tf_op jit(solution)/shard_map/fit/pallas_call | solution.py:583
  (1 shorter events, 0.0 us)

commit v5 on v2

--- a/solution.py
+++ b/solution.py
@@ -34,10 +34,12 @@
 CORES = 2
 COARSE = 16
 PLANE = LINE * LINE
-ROUTES = (("x", "z", "y"), ("y", "z", "x"), ("z", "x", "y"))
-
-
-def lists_of(meta):
+ROUTES = (("x", "z", "y"), ("y", "x", "z"), ("z", "y", "x"))
+BACKS = (0, 1, 3, 2)
+PARTS = ((0, 1), (1, 2), (3, 1))
+
+
+def lists_of(meta, here):
     lane = lax.broadcasted_iota(jnp.int32, (ROWS, ROWS), 1)
     sub = lax.broadcasted_iota(jnp.int32, (ROWS, ROWS), 0)
     diag = lane == sub
@@ -70,7 +72,9 @@
         place = jnp.where(keys[h] == at_first, 0, 1)
         at = {"x": (own >> 5) & 3, "z": (own >> 3) & 3, "y": (own >> 1) & 3}
         for c, (a, u, v) in enumerate(ROUTES):
-            slot = ((at[a] * CORES + (own & 1)) * PLANE + at[v] * LINE + at[u]) * 2 + place
+            back = (at[v] - here[v]) & 3
+            spot = jnp.where(back == 2, 3, jnp.where(back == 3, 2, back))
+            slot = ((at[a] * CORES + (own & 1)) * PLANE + spot * LINE + at[u]) * 2 + place
             targets[c].append(jnp.where(own < 0, -1, slot))
     coarse = meta[2:3]
     rank = jnp.sum(jnp.where(sub < lane, column(coarse), 0), axis=0, keepdims=True)
@@ -84,11 +88,11 @@
 def smooth_kernel(
     tv, cx, cy, cz, sh, meta, sm_out, blk, rb, tgt,
     stage, coef, wa, wb, ka, kb, km, kp, fxs, fxr, fys, fyr,
-    want, wants, ranks, idv, want_s, rank_s, id_s, pg0, pg1, pg2, sb,
+    want, wants, ranks, idv, want_s, rank_s, id_s, p00, p01, p02, p03, p10, p11, p12, p13, p20, p21, p22, p23, sb, fb,
     in_sem, coef_sem, out_sem, send_sem, recv_sem, want_send, want_recv, rank_send, rank_recv,
-    cast_send, cast_recv, ans_send, ans_recv, own_sem, smem_sem,
+    near_send, near_recv, cast_send, cast_recv, ans_send, ans_recv, fwd_send, fwd_recv, own_sem, smem_sem,
 ):
-    pg = (pg0, pg1, pg2)
+    pg = ((p00, p01, p02, p03), (p10, p11, p12, p13), (p20, p21, p22, p23))
     i = lax.axis_index("gx")
     j = lax.axis_index("gy")
     core = lax.rem(j, CORES)
@@ -134,16 +138,6 @@
                 )
     greeted = 3 + len(AXES) * (LINE - 1) * CORES
 
-    for load in coef_loads:
-        load.wait()
-    ax, ay, az = coef[0], coef[1], coef[2]
-    scale = OMEGA / (2.0 * (ax + ay + az) + coef[3])
-    ka[...] = ax * scale
-    kb[...] = ay * scale
-    az = az * scale
-    lane = lax.broadcasted_iota(jnp.int32, az.shape, 2)
-    km[...] = jnp.where(lane == 0, 0.0, az)
-    kp[...] = jnp.where(lane == ROWS - 1, 0.0, az)
     keep = (
         (i > 0).astype(F32),
         (i < GX - 1).astype(F32),
@@ -238,28 +232,49 @@
             )
         return out
 
-    def cast_copies(c, step):
+    def spread_copies(c):
         a, u, v = ROUTES[c]
-        out = []
-        for d in (2, 1, 3):
-            if step == 0:
-                ref, peer = pg[c].at[at[v], at[u]], device(u, d, 0)
-            else:
-                ref, peer = pg[c].at[at[v]], device(v, d, 0)
-            out.append(
-                remote(ref, ref, cast_send.at[c, step, d], cast_recv.at[c, step, d], peer)
+        ref = pg[c][0].at[at[u]]
+        return [
+            remote(ref, ref, near_send.at[c, d], near_recv.at[c, d], device(u, d, 0))
+            for d in (2, 1, 3)
+        ]
+
+    def cast_copies(c):
+        a, u, v = ROUTES[c]
+        plan = ((0, 0, 3, 1), (0, 1, 1, 3), (0, 1, 3, 1), (0, 0, 1, 3), (3, 0, 2, 1), (1, 1, 2, 3))
+        return [
+            remote(
+                pg[c][src].at[pl.ds(half * 2, 2)], pg[c][dst].at[pl.ds(half * 2, 2)],
+                cast_send.at[c, n], cast_recv.at[c, n], device(v, d, 0),
             )
-        return out
-
-    def answer(c, d, e):
+            for n, (src, half, dst, d) in enumerate(plan)
+        ]
+
+    def piece(ref, part):
+        first, count = PARTS[part]
+        return ref.at[pl.ds(first, count)]
+
+    def answer(c, part, d, e):
         a = ROUTES[c][0]
         slot = lax.rem(at[a] + d, LINE) * CORES + lax.rem(core + e, CORES)
         here = at[a] * CORES + core
+        src = piece(sb.at[c, slot], part)
+        dst, peer = piece(rb.at[c, here], part), device(a, d, e)
         if d == 0 and e == 0:
-            return pltpu.make_async_copy(sb.at[c, slot], rb.at[c, here], own_sem.at[c])
+            return pltpu.make_async_copy(src, dst, own_sem.at[c, part])
+        if d == 2:
+            dst, peer = piece(fb.at[c, e], part), device(a, 1 + 2 * e, 0)
         return remote(
-            sb.at[c, slot], rb.at[c, here],
-            ans_send.at[c, d, e], ans_recv.at[c, d, e], device(a, d, e),
+            src, dst, ans_send.at[c, part, d, e], ans_recv.at[c, part, d, e], peer
+        )
+
+    def forward(c, part, e):
+        a = ROUTES[c][0]
+        origin = lax.rem(at[a] + 3 - 2 * e, LINE) * CORES + core
+        return remote(
+            piece(fb.at[c, e], part), piece(rb.at[c, origin], part),
+            fwd_send.at[c, part, e], fwd_recv.at[c, part, e], device(a, 1 + 2 * e, e),
         )
 
     order = [(d, e) for d in (2, 1, 3, 0) for e in range(CORES)]
@@ -267,32 +282,47 @@
     def spread(c):
         a, u, v = ROUTES[c]
         for r in range(COARSE):
-            pg[c][at[v], at[u], r] = blk[c, id_s[r, 0] & (SITES - 1)]
-        for copy in cast_copies(c, 0):
+            pg[c][0][at[u], r] = blk[c, id_s[r, 0] & (SITES - 1)]
+        for copy in spread_copies(c):
             copy.start()
 
-    def spread_more(c):
-        for copy in cast_copies(c, 0):
+    def cast(c):
+        for copy in spread_copies(c):
             copy.wait_recv()
-        for copy in cast_copies(c, 1):
+        for copy in cast_copies(c)[:4]:
             copy.start()
 
-    def reply(c):
+    def pass_on(c):
+        all_copies = cast_copies(c)
+        for n in range(2):
+            all_copies[n].wait_recv()
+            all_copies[4 + n].start()
+
+    def reply(c, part):
         a, u, v = ROUTES[c]
         n = AXES.index(a)
-        for copy in cast_copies(c, 1):
-            copy.wait_recv()
+        if part:
+            for copy in cast_copies(c)[2:4] if part == 1 else cast_copies(c)[4:]:
+                copy.wait_recv()
+        first, count = PARTS[part]
         for d, e in order:
             slot = lax.rem(at[a] + d, LINE) * CORES + lax.rem(core + e, CORES)
-            for vv in range(LINE):
+            for place in range(first, first + count):
+                back = BACKS[place]
+                vv = lax.rem(at[v] + back, LINE)
                 for uu in range(LINE):
                     whose = {a: at[a], u: uu, v: vv}
                     owner = whose["x"] * 32 + whose["z"] * 8 + whose["y"] * 2 + core
                     for p in range(2):
                         block = want_s[n, slot, p, owner] & (SITES - 1)
                         rank = rank_s[c, vv, uu, 0, block] & (COARSE - 1)
-                        sb[c, slot, (vv * LINE + uu) * 2 + p] = pg[c][vv, uu, rank]
-            answer(c, d, e).start()
+                        sb[c, slot, place, uu * 2 + p] = pg[c][back][uu, rank]
+            answer(c, part, d, e).start()
+
+    def reply_on(c, part):
+        for e in range(2):
+            answer(c, part, 2, e).wait_recv()
+            forward(c, part, e).start()
 
     def transpose_in(c):
         loads[c].wait()
@@ -317,14 +347,24 @@
         store.start()
         stores.append(store)
 
-    transpose_in(0)
-    pl.semaphore_wait(barrier, greeted)
-    send_faces(0, 0, wa)
-    for c in range(1, CHUNKS):
+    for c in range(CHUNKS):
         transpose_in(c)
+        if c == 0:
+            pl.semaphore_wait(barrier, greeted)
         send_faces(0, c, wa)
 
-    wanted, targets, rank, ids = lists_of(meta[...])
+    for load in coef_loads:
+        load.wait()
+    ax, ay, az = coef[0], coef[1], coef[2]
+    scale = OMEGA / (2.0 * (ax + ay + az) + coef[3])
+    ka[...] = ax * scale
+    kb[...] = ay * scale
+    az = az * scale
+    lane = lax.broadcasted_iota(jnp.int32, az.shape, 2)
+    km[...] = jnp.where(lane == 0, 0.0, az)
+    kp[...] = jnp.where(lane == ROWS - 1, 0.0, az)
+
+    wanted, targets, rank, ids = lists_of(meta[...], at)
     idv[...] = ids
     id_copy = pltpu.make_async_copy(idv, id_s, smem_sem.at[0])
     id_copy.start()
@@ -338,24 +378,30 @@
         ranks[c, at[v], at[u]] = rank
         for h in range(2):
             tgt[2 * c + h : 2 * c + h + 1] = targets[c][h]
+
+    for c in range(CHUNKS):
+        fill_halo(0, c, wa)
+        sweep(c, wa, wb, False)
+        send_faces(1, c, wb)
+    for c in range(CHUNKS):
         for copy in rank_copies(c, 0):
             copy.start()
     for copy in want_copies():
         copy.start()
-
-    for c in range(CHUNKS):
-        fill_halo(0, c, wa)
-        sweep(c, wa, wb, False)
-        send_faces(1, c, wb)
+    for c in range(CHUNKS):
+        fill_halo(1, c, wb)
+        sweep(c, wb, wa, False)
+        send_faces(2, c, wa)
     for c in range(CHUNKS):
         for copy in rank_copies(c, 0):
             copy.wait_recv()
         for copy in rank_copies(c, 1):
             copy.start()
-    for c in range(CHUNKS):
-        fill_halo(1, c, wb)
-        sweep(c, wb, wa, False)
-        send_faces(2, c, wa)
+    id_copy.wait()
+    for c in range(CHUNKS):
+        fill_halo(2, c, wa)
+        sweep(c, wa, wb, True)
+        spread(c)
     for copy in want_copies():
         copy.wait_recv()
     want_copy = pltpu.make_async_copy(wants, want_s, smem_sem.at[1])
@@ -365,19 +411,25 @@
             copy.wait_recv()
     rank_copy = pltpu.make_async_copy(ranks, rank_s, smem_sem.at[2])
     rank_copy.start()
-    id_copy.wait()
-    for c in range(CHUNKS):
-        fill_halo(2, c, wa)
-        sweep(c, wa, wb, True)
-        spread(c)
-        if c > 0:
-            spread_more(c - 1)
+    for c in range(CHUNKS):
+        cast(c)
     want_copy.wait()
     rank_copy.wait()
-    spread_more(CHUNKS - 1)
-    for c in range(CHUNKS):
-        reply(c)
-        transpose_out(c, wb)
+    transpose_out(0, wb)
+    for c in range(CHUNKS):
+        pass_on(c)
+    for c in range(CHUNKS):
+        reply(c, 0)
+    for c in range(CHUNKS):
+        reply(c, 1)
+        reply_on(c, 0)
+    for c in range(CHUNKS):
+        reply(c, 2)
+        reply_on(c, 1)
+    transpose_out(1, wb)
+    for c in range(CHUNKS):
+        reply_on(c, 2)
+    transpose_out(2, wb)
 
     for s in range(SWEEPS):
         for c in range(CHUNKS):
@@ -386,16 +438,20 @@
     for copy in want_copies():
         copy.wait_send()
     for c in range(CHUNKS):
-        for step in range(2):
-            for copy in rank_copies(c, step) + cast_copies(c, step):
-                copy.wait_send()
-        for d, e in order:
-            copy = answer(c, d, e)
-            if d or e:
-                copy.wait_send()
-                copy.wait_recv()
-            else:
-                copy.wait()
+        for copy in rank_copies(c, 0) + rank_copies(c, 1) + spread_copies(c) + cast_copies(c):
+            copy.wait_send()
+        for part in range(len(PARTS)):
+            for d, e in order:
+                copy = answer(c, part, d, e)
+                if d or e:
+                    copy.wait_send()
+                    if d != 2:
+                        copy.wait_recv()
+                else:
+                    copy.wait()
+            for e in range(2):
+                forward(c, part, e).wait_send()
+                forward(c, part, e).wait_recv()
     for store in stores:
         store.wait()
 
@@ -404,14 +460,14 @@
     vmem = pl.BlockSpec(memory_space=pltpu.VMEM)
     anywhere = pl.BlockSpec(memory_space=pl.ANY)
     cells = pltpu.VMEM((NX, NY, ROWS), F32)
-    plane = pltpu.VMEM((LINE, LINE, COARSE, KV, ROWS), BF16)
+    rows = pltpu.VMEM((LINE, COARSE, KV, ROWS), BF16)
     dma = pltpu.SemaphoreType.DMA
     return pl.pallas_call(
         smooth_kernel,
         out_shape=(
             jax.ShapeDtypeStruct((VECS, NX, NY, ROWS), F32),
             jax.ShapeDtypeStruct((CHUNKS, SITES, KV, ROWS), BF16),
-            jax.ShapeDtypeStruct((CHUNKS, LINE * CORES, 2 * PLANE, KV, ROWS), BF16),
+            jax.ShapeDtypeStruct((CHUNKS, LINE * CORES, LINE, 2 * LINE, KV, ROWS), BF16),
             jax.ShapeDtypeStruct((8, ROWS), jnp.int32),
         ),
         in_specs=[anywhere] * 5 + [vmem],
@@ -433,8 +489,9 @@
             pltpu.SMEM((len(AXES), LINE * CORES, 2, ROWS), jnp.int32),
             pltpu.SMEM((CHUNKS, LINE, LINE, 1, ROWS), jnp.int32),
             pltpu.SMEM((COARSE, ROWS), jnp.int32),
-            plane, plane, plane,
-            pltpu.VMEM((CHUNKS, LINE * CORES, 2 * PLANE, KV, ROWS), BF16),
+            *([rows] * (LINE * CHUNKS)),
+            pltpu.VMEM((CHUNKS, LINE * CORES, LINE, 2 * LINE, KV, ROWS), BF16),
+            pltpu.VMEM((CHUNKS, CORES, LINE, 2 * LINE, KV, ROWS), BF16),
             dma((CHUNKS,)),
             dma((4,)),
             dma((CHUNKS,)),
@@ -444,15 +501,19 @@
             dma((len(AXES), LINE, CORES)),
             dma((CHUNKS, 2, LINE)),
             dma((CHUNKS, 2, LINE)),
-            dma((CHUNKS, 2, LINE)),
-            dma((CHUNKS, 2, LINE)),
-            dma((CHUNKS, LINE, CORES)),
-            dma((CHUNKS, LINE, CORES)),
-            dma((CHUNKS,)),
+            dma((CHUNKS, LINE)),
+            dma((CHUNKS, LINE)),
+            dma((CHUNKS, 6)),
+            dma((CHUNKS, 6)),
+            dma((CHUNKS, len(PARTS), LINE, CORES)),
+            dma((CHUNKS, len(PARTS), LINE, CORES)),
+            dma((CHUNKS, len(PARTS), CORES)),
+            dma((CHUNKS, len(PARTS), CORES)),
+            dma((CHUNKS, len(PARTS))),
             dma((3,)),
         ],
         compiler_params=pltpu.CompilerParams(
-            collective_id=0, has_side_effects=True, vmem_limit_bytes=48 * 1024 * 1024
+            collective_id=0, has_side_effects=True, vmem_limit_bytes=60 * 1024 * 1024
         ),
         name="smooth",
     )(test_vectors, coef_x, coef_y, coef_z, shift, meta)
@@ -539,13 +600,13 @@
             jax.ShapeDtypeStruct((SLOTS, NX, NY, ROWS), F32),
             jax.ShapeDtypeStruct((VECS, NX, NY, ROWS), F32),
         ),
-        in_specs=[pl.BlockSpec(memory_space=pltpu.SMEM), vmem, vmem, anywhere],
+        in_specs=[pl.BlockSpec(memory_space=pltpu.SMEM), vmem, vmem, vmem],
         out_specs=(vmem, anywhere),
         scratch_shapes=[
             pltpu.VMEM((len(PAIRS), SITES * 8, ROWS), F32),
             pltpu.SemaphoreType.DMA,
         ],
-        compiler_params=pltpu.CompilerParams(vmem_limit_bytes=48 * 1024 * 1024),
+        compiler_params=pltpu.CompilerParams(vmem_limit_bytes=60 * 1024 * 1024),
         name="fit",
     )(target, replies, blk, sm)
 

time: 86.7 us -> 73.7 us (0.85)
  Pallas kernels: 75.3 us -> 68.6 us
  local copies, waits for them, and re-layouts: 7.13 us -> 0.81 us
    pallas_call x1, Pallas kernels: 69.8 us -> 61 us  [smooth(): pl.pallas_call(smooth_kernel, out_shape=(jax.ShapeDtypeStruct((VECS, NX,...]
    unnamed x14 -> x2, local copies, waits for them, and re-layouts: 6.84 us -> 0.52 us
    pallas_call x1, Pallas kernels: 5.54 us -> 7.55 us  [fit(): pl.pallas_call(weights_kernel, out_shape=(jax.ShapeDtypeStruct((SLOTS, NX...]
where the time goes in v5:
time: 73.7 us; the launch traced here: 73.4 us
  Pallas kernels  68.6 us (93%)
  other arithmetic  3.36 us (5%)
  local copies, waits for them, and re-layouts  0.81 us (1%)
    pallas_call x1, Pallas kernels, smooth(): pl.pallas_call(smooth_kernel, out_shape=(jax.ShapeDtypeStruct((VECS, NX,...  61 us
    pallas_call x1, Pallas kernels, fit(): pl.pallas_call(weights_kernel, out_shape=(jax.ShapeDtypeStruct((SLOTS, NX...  7.55 us

profile of v5, /device:TPU:1, one launch (start us, length us, event | category | flops | bytes accessed | tf_op | source)
XLA Modules:
  0.0 73.4 jit_solution(10442710465050819613)
XLA Ops:
  0.6 0.5 broadcast.26
  1.1 1.3 %reduce.3 = s32[4,16]{1,0:T(4,128)S(1)} reduce(s32[4,16,1]{1,2,0:T(1,128)} %param.14, s32[]{:T(128)} %broadcast.26), dimensions={2}, to_apply=%param.14.reduce_sub_computation.3 | reduce | bytes 516 | tf_op args[5]
  2.5 0.1 reshape.32
  2.6 0.7 broadcast_compare_fusion
  3.3 0.7 add_select_fusion
  4.0 0.1 copy.12
  4.1 0.1 reshape.31
  4.2 0.6 pad_add_fusion.meta
  4.8 61.0 %smooth.1 = (f32[48,4,16,128]{3,2,1,0:T(8,128)}, bf16[3,64,16,128]{3,2,1,0:T(8,128)(2,1)}, bf16[3,8,4,8,16,128]{5,4,3,2,1,0:T(8,128)(2,1)}, s32[8,128]{1,0:T(8,128)}) custom-call(f32[48,4,16,128]{3,2,1,0:T(8,128)} %tv.1, f32[4,16,128]{2,1,0:T(8,128)} %cx.1, f32[4,16,128]{2,1,0:T(8,128)} %cy.1, f32[4,16,128]{2,1,0:T(8,128)} %cz.1, f32[4,16,128]{2,1,0:T(8,128)} %sh.1, ...), custom_call_target="tpu_custom_call" | custom-call | tf_op jit(solution)/shard_map/smooth/pallas_call | solution.py:465
  65.9 7.6 %fit.1 = (f32[4,4,16,128]{3,2,1,0:T(8,128)}, f32[48,4,16,128]{3,2,1,0:T(8,128)}) custom-call(s32[8,128]{1,0:T(8,128)} %get-tuple-element.8.target, bf16[3,256,16,128]{3,2,1,0:T(8,128)(2,1)} %bitcast.10, bf16[3,64,16,128]{3,2,1,0:T(8,128)(2,1)} %get-tuple-element.10.blk, f32[48,4,16,128]{3,2,1,0:T(8,128)} %get-tuple-element.11.sm_in), custom_call_target="tpu_custom_call" | custom-call | tf_op jit(solution)/shard_map/fit/pallas_call | solution.py:597
  (1 shorter events, 0.0 us)

commit v6 on v5

--- a/solution.py
+++ b/solution.py
@@ -36,7 +36,7 @@
 PLANE = LINE * LINE
 ROUTES = (("x", "z", "y"), ("y", "x", "z"), ("z", "y", "x"))
 BACKS = (0, 1, 3, 2)
-PARTS = ((0, 1), (1, 2), (3, 1))
+PARTS = ((0, 3), (3, 1))
 
 
 def lists_of(meta, here):
@@ -88,9 +88,9 @@
 def smooth_kernel(
     tv, cx, cy, cz, sh, meta, sm_out, blk, rb, tgt,
     stage, coef, wa, wb, ka, kb, km, kp, fxs, fxr, fys, fyr,
-    want, wants, ranks, idv, want_s, rank_s, id_s, p00, p01, p02, p03, p10, p11, p12, p13, p20, p21, p22, p23, sb, fb,
-    in_sem, coef_sem, out_sem, send_sem, recv_sem, want_send, want_recv, rank_send, rank_recv,
-    near_send, near_recv, cast_send, cast_recv, ans_send, ans_recv, fwd_send, fwd_recv, own_sem, smem_sem,
+    pair, lines, ranks, idv, line_s, rank_s, id_s, p00, p01, p02, p03, p10, p11, p12, p13, p20, p21, p22, p23, sb, fb,
+    in_sem, coef_sem, out_sem, send_sem, recv_sem, pair_sem, table_sem,
+    near_sem, cast_send, cast_recv, ans_send, ans_recv, hop_recv, fwd_send, own_sem, smem_sem,
 ):
     pg = ((p00, p01, p02, p03), (p10, p11, p12, p13), (p20, p21, p22, p23))
     i = lax.axis_index("gx")
@@ -145,6 +145,9 @@
         (j < GY - 1).astype(F32),
     )
 
+    def drain(ref, sem):
+        pltpu.make_async_copy(ref, ref, sem).wait()
+
     def copies(s, c):
         out = []
         for d in range(4):
@@ -152,7 +155,7 @@
             out.append(
                 remote(
                     src.at[s, c, d % 2], dst.at[s, c, 1 - d % 2],
-                    send_sem.at[s, c, d], recv_sem.at[s, c, d], peers[d],
+                    send_sem.at[d // 2], recv_sem.at[s, c, d // 2], peers[d],
                 )
             )
         return out
@@ -168,8 +171,8 @@
             copy.start()
 
     def fill_halo(s, c, w):
-        for copy in copies(s, c):
-            copy.wait_recv()
+        drain(fxr.at[s, c], recv_sem.at[s, c, 0])
+        drain(fyr.at[s, c], recv_sem.at[s, c, 1])
         for side in range(2):
             x = -1 if side == 0 else NX
             w[c, pl.ds(site_row(x, 0), NY * KV)] = fxr[s, c, side].astype(F32) * keep[side]
@@ -205,38 +208,38 @@
 
         lax.fori_loop(0, NX, plane, 0)
 
-    def want_copies():
+    def pair_copy():
+        slot = pair.at[core]
+        return remote(slot, slot, pair_sem.at[0], pair_sem.at[1], device("x", 0, 1))
+
+    def line_copies():
+        return [
+            remote(
+                pair, lines.at[n, at[axis]], table_sem.at[0, 0], table_sem.at[0, 1],
+                device(axis, d, 0),
+            )
+            for n, axis in enumerate(AXES)
+            for d in range(1, LINE)
+        ]
+
+    def rank_copies():
         out = []
-        for n, axis in enumerate(AXES):
-            for d in range(LINE):
-                for e in range(CORES):
-                    if d or e:
-                        out.append(
-                            remote(
-                                want, wants.at[n, at[axis] * CORES + core],
-                                want_send.at[n, d, e], want_recv.at[n, d, e], device(axis, d, e),
-                            )
-                        )
-        return out
-
-    def rank_copies(c, step):
-        a, u, v = ROUTES[c]
-        out = []
-        for d in range(1, LINE):
-            if step == 0:
-                ref, peer = ranks.at[c, at[v], at[u]], device(u, d, 0)
-            else:
-                ref, peer = ranks.at[c, at[v]], device(v, d, 0)
-            out.append(
-                remote(ref, ref, rank_send.at[c, step, d], rank_recv.at[c, step, d], peer)
-            )
+        for c, (a, u, v) in enumerate(ROUTES):
+            src = lines.at[AXES.index(u), :, core, 2]
+            for d in range(1, LINE):
+                out.append(
+                    remote(
+                        src, ranks.at[c, at[v]], table_sem.at[1, 0], table_sem.at[1, 1],
+                        device(v, d, 0),
+                    )
+                )
         return out
 
     def spread_copies(c):
         a, u, v = ROUTES[c]
         ref = pg[c][0].at[at[u]]
         return [
-            remote(ref, ref, near_send.at[c, d], near_recv.at[c, d], device(u, d, 0))
+            remote(ref, ref, near_sem.at[c, 0], near_sem.at[c, 1], device(u, d, 0))
             for d in (2, 1, 3)
         ]
 
@@ -246,7 +249,7 @@
         return [
             remote(
                 pg[c][src].at[pl.ds(half * 2, 2)], pg[c][dst].at[pl.ds(half * 2, 2)],
-                cast_send.at[c, n], cast_recv.at[c, n], device(v, d, 0),
+                cast_send.at[c, n // 2], cast_recv.at[c, min(n, 2 + n // 4)], device(v, d, 0),
             )
             for n, (src, half, dst, d) in enumerate(plan)
         ]
@@ -265,16 +268,15 @@
             return pltpu.make_async_copy(src, dst, own_sem.at[c, part])
         if d == 2:
             dst, peer = piece(fb.at[c, e], part), device(a, 1 + 2 * e, 0)
-        return remote(
-            src, dst, ans_send.at[c, part, d, e], ans_recv.at[c, part, d, e], peer
-        )
+            return remote(src, dst, ans_send.at[c, part], hop_recv.at[c, part, e], peer)
+        return remote(src, dst, ans_send.at[c, part], ans_recv.at[c, part], peer)
 
     def forward(c, part, e):
         a = ROUTES[c][0]
         origin = lax.rem(at[a] + 3 - 2 * e, LINE) * CORES + core
         return remote(
             piece(fb.at[c, e], part), piece(rb.at[c, origin], part),
-            fwd_send.at[c, part, e], fwd_recv.at[c, part, e], device(a, 1 + 2 * e, e),
+            fwd_send.at[c, part], ans_recv.at[c, part], device(a, 1 + 2 * e, e),
         )
 
     order = [(d, e) for d in (2, 1, 3, 0) for e in range(CORES)]
@@ -287,8 +289,7 @@
             copy.start()
 
     def cast(c):
-        for copy in spread_copies(c):
-            copy.wait_recv()
+        drain(pg[c][1].at[pl.ds(0, 3)], near_sem.at[c, 1])
         for copy in cast_copies(c)[:4]:
             copy.start()
 
@@ -301,22 +302,24 @@
     def reply(c, part):
         a, u, v = ROUTES[c]
         n = AXES.index(a)
-        if part:
-            for copy in cast_copies(c)[2:4] if part == 1 else cast_copies(c)[4:]:
-                copy.wait_recv()
+        drain(pg[c][0], cast_recv.at[c, 2 + part])
         first, count = PARTS[part]
         for d, e in order:
-            slot = lax.rem(at[a] + d, LINE) * CORES + lax.rem(core + e, CORES)
+            q, to = lax.rem(at[a] + d, LINE), lax.rem(core + e, CORES)
+            slot = q * CORES + to
             for place in range(first, first + count):
                 back = BACKS[place]
                 vv = lax.rem(at[v] + back, LINE)
+                tiles = []
                 for uu in range(LINE):
                     whose = {a: at[a], u: uu, v: vv}
                     owner = whose["x"] * 32 + whose["z"] * 8 + whose["y"] * 2 + core
                     for p in range(2):
-                        block = want_s[n, slot, p, owner] & (SITES - 1)
+                        block = line_s[n, q, to, p, 0, owner] & (SITES - 1)
                         rank = rank_s[c, vv, uu, 0, block] & (COARSE - 1)
-                        sb[c, slot, place, uu * 2 + p] = pg[c][back][uu, rank]
+                        tiles.append(pg[c][back][uu, rank])
+                for t, tile in enumerate(tiles):
+                    sb[c, slot, place, t] = tile
             answer(c, part, d, e).start()
 
     def reply_on(c, part):
@@ -368,14 +371,11 @@
     idv[...] = ids
     id_copy = pltpu.make_async_copy(idv, id_s, smem_sem.at[0])
     id_copy.start()
-    for p in range(2):
-        want[p : p + 1] = wanted[p]
-        for n, axis in enumerate(AXES):
-            wants[n, at[axis] * CORES + core, p : p + 1] = wanted[p]
+    for n, row in enumerate((*wanted, rank)):
+        pair[core, n] = row
+    pair_copy().start()
     tgt[...] = jnp.zeros_like(tgt)
     for c in range(CHUNKS):
-        a, u, v = ROUTES[c]
-        ranks[c, at[v], at[u]] = rank
         for h in range(2):
             tgt[2 * c + h : 2 * c + h + 1] = targets[c][h]
 
@@ -383,37 +383,33 @@
         fill_halo(0, c, wa)
         sweep(c, wa, wb, False)
         send_faces(1, c, wb)
-    for c in range(CHUNKS):
-        for copy in rank_copies(c, 0):
-            copy.start()
-    for copy in want_copies():
+    pair_copy().wait_recv()
+    for copy in line_copies():
         copy.start()
+    for n, axis in enumerate(AXES):
+        lines[n, at[axis]] = pair[...]
     for c in range(CHUNKS):
         fill_halo(1, c, wb)
         sweep(c, wb, wa, False)
         send_faces(2, c, wa)
-    for c in range(CHUNKS):
-        for copy in rank_copies(c, 0):
-            copy.wait_recv()
-        for copy in rank_copies(c, 1):
-            copy.start()
+    drain(lines.at[:, pl.ds(0, 3)], table_sem.at[0, 1])
+    for copy in rank_copies():
+        copy.start()
+    for c, (a, u, v) in enumerate(ROUTES):
+        ranks[c, at[v]] = lines[AXES.index(u), :, core, 2]
+    line_copy = pltpu.make_async_copy(lines, line_s, smem_sem.at[1])
+    line_copy.start()
     id_copy.wait()
     for c in range(CHUNKS):
         fill_halo(2, c, wa)
         sweep(c, wa, wb, True)
         spread(c)
-    for copy in want_copies():
-        copy.wait_recv()
-    want_copy = pltpu.make_async_copy(wants, want_s, smem_sem.at[1])
-    want_copy.start()
-    for c in range(CHUNKS):
-        for copy in rank_copies(c, 1):
-            copy.wait_recv()
+    drain(ranks.at[:, pl.ds(0, 3)], table_sem.at[1, 1])
     rank_copy = pltpu.make_async_copy(ranks, rank_s, smem_sem.at[2])
     rank_copy.start()
     for c in range(CHUNKS):
         cast(c)
-    want_copy.wait()
+    line_copy.wait()
     rank_copy.wait()
     transpose_out(0, wb)
     for c in range(CHUNKS):
@@ -423,35 +419,27 @@
     for c in range(CHUNKS):
         reply(c, 1)
         reply_on(c, 0)
-    for c in range(CHUNKS):
-        reply(c, 2)
+    transpose_out(1, wb)
+    for c in range(CHUNKS):
         reply_on(c, 1)
-    transpose_out(1, wb)
-    for c in range(CHUNKS):
-        reply_on(c, 2)
     transpose_out(2, wb)
 
-    for s in range(SWEEPS):
-        for c in range(CHUNKS):
-            for copy in copies(s, c):
-                copy.wait_send()
-    for copy in want_copies():
-        copy.wait_send()
-    for c in range(CHUNKS):
-        for copy in rank_copies(c, 0) + rank_copies(c, 1) + spread_copies(c) + cast_copies(c):
-            copy.wait_send()
+    drain(fxs, send_sem.at[0])
+    drain(fys, send_sem.at[1])
+    pair_copy().wait_send()
+    drain(lines.at[:, pl.ds(0, 3)], table_sem.at[0, 0])
+    drain(ranks.at[:, pl.ds(0, 3)], table_sem.at[1, 0])
+    for c in range(CHUNKS):
+        drain(pg[c][0].at[pl.ds(0, 3)], near_sem.at[c, 0])
+        for n in range(3):
+            drain(pg[c][0], cast_send.at[c, n])
         for part in range(len(PARTS)):
-            for d, e in order:
-                copy = answer(c, part, d, e)
-                if d or e:
-                    copy.wait_send()
-                    if d != 2:
-                        copy.wait_recv()
-                else:
-                    copy.wait()
-            for e in range(2):
-                forward(c, part, e).wait_send()
-                forward(c, part, e).wait_recv()
+            answer(c, part, 0, 0).wait()
+            first, count = PARTS[part]
+            seven = sb.at[c, pl.ds(0, 7), pl.ds(first, count)]
+            drain(seven, ans_send.at[c, part])
+            drain(fb.at[c, :, pl.ds(first, count)], fwd_send.at[c, part])
+            drain(seven, ans_recv.at[c, part])
     for store in stores:
         store.wait()
 
@@ -482,11 +470,11 @@
             pltpu.VMEM((SWEEPS, CHUNKS, 2, NY * KV, ROWS), BF16),
             pltpu.VMEM((SWEEPS, CHUNKS, 2, NX * KV, ROWS), BF16),
             pltpu.VMEM((SWEEPS, CHUNKS, 2, NX * KV, ROWS), BF16),
-            pltpu.VMEM((2, ROWS), jnp.int32),
-            pltpu.VMEM((len(AXES), LINE * CORES, 2, ROWS), jnp.int32),
+            pltpu.VMEM((CORES, 3, 1, ROWS), jnp.int32),
+            pltpu.VMEM((len(AXES), LINE, CORES, 3, 1, ROWS), jnp.int32),
             pltpu.VMEM((CHUNKS, LINE, LINE, 1, ROWS), jnp.int32),
             pltpu.VMEM((COARSE, ROWS), jnp.int32),
-            pltpu.SMEM((len(AXES), LINE * CORES, 2, ROWS), jnp.int32),
+            pltpu.SMEM((len(AXES), LINE, CORES, 3, 1, ROWS), jnp.int32),
             pltpu.SMEM((CHUNKS, LINE, LINE, 1, ROWS), jnp.int32),
             pltpu.SMEM((COARSE, ROWS), jnp.int32),
             *([rows] * (LINE * CHUNKS)),
@@ -495,20 +483,17 @@
             dma((CHUNKS,)),
             dma((4,)),
             dma((CHUNKS,)),
-            dma((SWEEPS, CHUNKS, 4)),
-            dma((SWEEPS, CHUNKS, 4)),
-            dma((len(AXES), LINE, CORES)),
-            dma((len(AXES), LINE, CORES)),
-            dma((CHUNKS, 2, LINE)),
-            dma((CHUNKS, 2, LINE)),
-            dma((CHUNKS, LINE)),
-            dma((CHUNKS, LINE)),
-            dma((CHUNKS, 6)),
-            dma((CHUNKS, 6)),
-            dma((CHUNKS, len(PARTS), LINE, CORES)),
-            dma((CHUNKS, len(PARTS), LINE, CORES)),
+            dma((2,)),
+            dma((SWEEPS, CHUNKS, 2)),
+            dma((2,)),
+            dma((2, 2)),
+            dma((CHUNKS, 2)),
+            dma((CHUNKS, 3)),
+            dma((CHUNKS, 4)),
+            dma((CHUNKS, len(PARTS))),
+            dma((CHUNKS, len(PARTS))),
             dma((CHUNKS, len(PARTS), CORES)),
-            dma((CHUNKS, len(PARTS), CORES)),
+            dma((CHUNKS, len(PARTS))),
             dma((CHUNKS, len(PARTS))),
             dma((3,)),
         ],

time: 73.7 us -> 70.1 us (0.951)
  Pallas kernels: 68.6 us -> 65 us
    pallas_call x1, Pallas kernels: 61 us -> 57.5 us  [smooth(): pl.pallas_call(smooth_kernel, out_shape=(jax.ShapeDtypeStruct((VECS, NX,...]
where the time goes in v6:
time: 70.1 us; the launch traced here: 69.9 us
  Pallas kernels  65 us (93%)
  other arithmetic  3.36 us (5%)
  local copies, waits for them, and re-layouts  0.81 us (1%)
    pallas_call x1, Pallas kernels, smooth(): pl.pallas_call(smooth_kernel, out_shape=(jax.ShapeDtypeStruct((VECS, NX,...  57.5 us
    pallas_call x1, Pallas kernels, fit(): pl.pallas_call(weights_kernel, out_shape=(jax.ShapeDtypeStruct((SLOTS, NX...  7.55 us

profile of v6, /device:TPU:1, one launch (start us, length us, event | category | flops | bytes accessed | tf_op | source)
XLA Modules:
  0.0 69.9 jit_solution(1010659806559457289)
XLA Ops:
  0.6 0.5 broadcast.26
  1.1 1.3 %reduce.3 = s32[4,16]{1,0:T(4,128)S(1)} reduce(s32[4,16,1]{1,2,0:T(1,128)} %param.14, s32[]{:T(128)} %broadcast.26), dimensions={2}, to_apply=%param.14.reduce_sub_computation.3 | reduce | bytes 516 | tf_op args[5]
  2.5 0.1 reshape.32
  2.6 0.7 broadcast_compare_fusion
  3.3 0.7 %add_select_fusion = s32[4,16,1,4]{1,3,2,0:T(4,128)S(1)} fusion(s32[4,16,1,4]{1,3,2,0:T(4,128)} %param.17, s32[4,16,1,4]{1,3,2,0:T(4,128)} %param.16, s32[4,16]{1,0:T(4,128)} %bitcast.12, pred[4,16]{1,0:T(4,128)(4,1)S(1)} %bitcast.11), kind=kLoop, calls=%fused_computation | loop fusion | flops 1280 | bytes 3392 | tf_op jit(solution)/shard_map/jit(_where)/select_n | solution.py:604
  4.0 0.1 copy.12
  4.1 0.1 reshape.31
  4.2 0.6 pad_add_fusion.meta
  4.8 57.5 %smooth.1 = (f32[48,4,16,128]{3,2,1,0:T(8,128)}, bf16[3,64,16,128]{3,2,1,0:T(8,128)(2,1)}, bf16[3,8,4,8,16,128]{5,4,3,2,1,0:T(8,128)(2,1)}, s32[8,128]{1,0:T(8,128)}) custom-call(f32[48,4,16,128]{3,2,1,0:T(8,128)} %tv.1, f32[4,16,128]{2,1,0:T(8,128)} %cx.1, f32[4,16,128]{2,1,0:T(8,128)} %cy.1, f32[4,16,128]{2,1,0:T(8,128)} %cz.1, f32[4,16,128]{2,1,0:T(8,128)} %sh.1, ...), custom_call_target="tpu_custom_call" | custom-call | tf_op jit(solution)/shard_map/smooth/pallas_call | solution.py:453
  62.3 7.6 %fit.1 = (f32[4,4,16,128]{3,2,1,0:T(8,128)}, f32[48,4,16,128]{3,2,1,0:T(8,128)}) custom-call(s32[8,128]{1,0:T(8,128)} %get-tuple-element.8.target, bf16[3,256,16,128]{3,2,1,0:T(8,128)(2,1)} %bitcast.10, bf16[3,64,16,128]{3,2,1,0:T(8,128)(2,1)} %get-tuple-element.10.blk, f32[48,4,16,128]{3,2,1,0:T(8,128)} %get-tuple-element.11.sm_in), custom_call_target="tpu_custom_call" | custom-call | tf_op jit(solution)/shard_map/fit/pallas_call | solution.py:582
  (1 shorter events, 0.0 us)

commit v7 on v6

--- a/solution.py
+++ b/solution.py
@@ -29,6 +29,7 @@
     return (x + 1) * XROW + (y + 1) * KV
 
 
+PAIRS = [(s, t) for s in range(SLOTS) for t in range(s + 1)] + [(s, SLOTS) for s in range(SLOTS)]
 AXES = "xyz"
 LINE = 4
 CORES = 2
@@ -36,6 +37,9 @@
 PLANE = LINE * LINE
 ROUTES = (("x", "z", "y"), ("y", "x", "z"), ("z", "y", "x"))
 BACKS = (0, 1, 3, 2)
+EMPTY = LINE * CORES * PLANE * 2
+SPOT = 2 * LINE
+REPLY = PLANE * 2
 PARTS = ((0, 3), (3, 1))
 
 
@@ -75,7 +79,7 @@
             back = (at[v] - here[v]) & 3
             spot = jnp.where(back == 2, 3, jnp.where(back == 3, 2, back))
             slot = ((at[a] * CORES + (own & 1)) * PLANE + spot * LINE + at[u]) * 2 + place
-            targets[c].append(jnp.where(own < 0, -1, slot))
+            targets[c].append(jnp.where(own < 0, EMPTY, slot))
     coarse = meta[2:3]
     rank = jnp.sum(jnp.where(sub < lane, column(coarse), 0), axis=0, keepdims=True)
     hit = (rank == sub[:COARSE]) & (coarse > 0)
@@ -86,12 +90,15 @@
 
 
 def smooth_kernel(
-    tv, cx, cy, cz, sh, meta, sm_out, blk, rb, tgt,
+    tv, cx, cy, cz, sh, split, count, owner, local, sm_out, sums,
+    split_v, count_v, owner_v, local_v, meta, tgt, tgt_s, blk, rb0, rb1, rb2, part_sums,
     stage, coef, wa, wb, ka, kb, km, kp, fxs, fxr, fys, fyr,
     pair, lines, ranks, idv, line_s, rank_s, id_s, p00, p01, p02, p03, p10, p11, p12, p13, p20, p21, p22, p23, sb, fb,
     in_sem, coef_sem, out_sem, send_sem, recv_sem, pair_sem, table_sem,
-    near_sem, cast_send, cast_recv, ans_send, ans_recv, hop_recv, fwd_send, own_sem, smem_sem,
+    near_sem, cast_send, cast_recv, ans_send, ans_recv, hop_recv, fwd_send, own_sem, smem_sem, list_sem,
 ):
+    cells = (split_v, count_v, owner_v, local_v)
+    rb = (rb0, rb1, rb2)
     pg = ((p00, p01, p02, p03), (p10, p11, p12, p13), (p20, p21, p22, p23))
     i = lax.axis_index("gx")
     j = lax.axis_index("gy")
@@ -121,6 +128,11 @@
         load.start()
         loads.append(load)
     coef_loads, loads = loads, []
+    lists = []
+    for n, part in enumerate((split, count, owner, local)):
+        load = pltpu.make_async_copy(part, cells[n], list_sem.at[n])
+        load.start()
+        lists.append(load)
     for c in range(CHUNKS):
         part = pl.ds(c * KV, KV)
         load = pltpu.make_async_copy(tv.at[part], stage.at[part], in_sem.at[c])
@@ -254,20 +266,20 @@
             for n, (src, half, dst, d) in enumerate(plan)
         ]
 
-    def piece(ref, part):
+    def piece(slot, part):
         first, count = PARTS[part]
-        return ref.at[pl.ds(first, count)]
+        return pl.ds(slot * REPLY + first * SPOT, count * SPOT)
 
     def answer(c, part, d, e):
         a = ROUTES[c][0]
         slot = lax.rem(at[a] + d, LINE) * CORES + lax.rem(core + e, CORES)
         here = at[a] * CORES + core
-        src = piece(sb.at[c, slot], part)
-        dst, peer = piece(rb.at[c, here], part), device(a, d, e)
+        src = sb.at[c, piece(slot, part)]
+        dst, peer = rb[c].at[piece(here, part)], device(a, d, e)
         if d == 0 and e == 0:
             return pltpu.make_async_copy(src, dst, own_sem.at[c, part])
         if d == 2:
-            dst, peer = piece(fb.at[c, e], part), device(a, 1 + 2 * e, 0)
+            dst, peer = fb.at[c, e, piece(0, part)], device(a, 1 + 2 * e, 0)
             return remote(src, dst, ans_send.at[c, part], hop_recv.at[c, part, e], peer)
         return remote(src, dst, ans_send.at[c, part], ans_recv.at[c, part], peer)
 
@@ -275,7 +287,7 @@
         a = ROUTES[c][0]
         origin = lax.rem(at[a] + 3 - 2 * e, LINE) * CORES + core
         return remote(
-            piece(fb.at[c, e], part), piece(rb.at[c, origin], part),
+            fb.at[c, e, piece(0, part)], rb[c].at[piece(origin, part)],
             fwd_send.at[c, part], ans_recv.at[c, part], device(a, 1 + 2 * e, e),
         )
 
@@ -319,7 +331,7 @@
                         rank = rank_s[c, vv, uu, 0, block] & (COARSE - 1)
                         tiles.append(pg[c][back][uu, rank])
                 for t, tile in enumerate(tiles):
-                    sb[c, slot, place, t] = tile
+                    sb[c, slot * REPLY + place * SPOT + t] = tile
             answer(c, part, d, e).start()
 
     def reply_on(c, part):
@@ -335,6 +347,27 @@
                     wa[c, pl.ds(site_row(x, half * 8) + k, 8, stride=KV), :] = stage[
                         c * KV + k, x, pl.ds(half * 8, 8), :
                     ]
+
+    def add_products(c):
+        def step(g, carry):
+            for m in range(4):
+                b = g * 4 + m
+                column = ((b >> 4) & 1) * (ROWS // 2) + (b & (NY - 1))
+                values = []
+                for t in range(SLOTS):
+                    found = tgt_s[2 * c + (b >> 5), column + t * NY]
+                    values.append(rb[c][found].astype(F32))
+                values.append(blk[c, b].astype(F32))
+                row = pl.ds(pl.multiple_of(b * 8, 8), 8)
+                for n, (p, q) in enumerate(PAIRS):
+                    product = values[p] * values[q]
+                    product = product[0:8] + product[8:16]
+                    if c:
+                        product = product + part_sums[n, row, :]
+                    part_sums[n, row, :] = product
+            return carry
+
+        lax.fori_loop(0, SITES // 4, step, 0)
 
     stores = []
 
@@ -367,6 +400,17 @@
     km[...] = jnp.where(lane == 0, 0.0, az)
     kp[...] = jnp.where(lane == ROWS - 1, 0.0, az)
 
+    for load in lists:
+        load.wait()
+    meta[...] = jnp.zeros_like(meta)
+    slots = lax.broadcasted_iota(jnp.int32, (SLOTS, NY), 0)
+    for x in range(NX):
+        live = (cells[0][x] == 0) & (slots < cells[1][x])
+        listed = jnp.where(live, cells[2][x] * SITES + cells[3][x], -1)
+        for t in range(SLOTS):
+            where = pl.ds((x % 2) * (ROWS // 2) + t * NY, NY)
+            meta[x // 2 : x // 2 + 1, where] = listed[t : t + 1]
+        meta[2:3, pl.ds(x * NY, NY)] = cells[0][x]
     wanted, targets, rank, ids = lists_of(meta[...], at)
     idv[...] = ids
     id_copy = pltpu.make_async_copy(idv, id_s, smem_sem.at[0])
@@ -378,6 +422,9 @@
     for c in range(CHUNKS):
         for h in range(2):
             tgt[2 * c + h : 2 * c + h + 1] = targets[c][h]
+        rb[c][EMPTY] = jnp.zeros((KV, ROWS), BF16)
+    tgt_copy = pltpu.make_async_copy(tgt, tgt_s, smem_sem.at[3])
+    tgt_copy.start()
 
     for c in range(CHUNKS):
         fill_halo(0, c, wa)
@@ -423,6 +470,18 @@
     for c in range(CHUNKS):
         reply_on(c, 1)
     transpose_out(2, wb)
+    tgt_copy.wait()
+    for c in range(CHUNKS):
+        for part in range(len(PARTS)):
+            answer(c, part, 0, 0).wait()
+            drain(sb.at[c, pl.ds(0, 7 * PARTS[part][1] * SPOT)], ans_recv.at[c, part])
+        add_products(c)
+    for g in range(SITES // 8):
+        for n in range(len(PAIRS)):
+            acc = part_sums[n, pl.ds(g * 64, 8, stride=8), :]
+            for h in range(1, 8):
+                acc = acc + part_sums[n, pl.ds(g * 64 + h, 8, stride=8), :]
+            sums[n, pl.ds(g * 8, 8), :] = acc
 
     drain(fxs, send_sem.at[0])
     drain(fys, send_sem.at[1])
@@ -434,17 +493,14 @@
         for n in range(3):
             drain(pg[c][0], cast_send.at[c, n])
         for part in range(len(PARTS)):
-            answer(c, part, 0, 0).wait()
-            first, count = PARTS[part]
-            seven = sb.at[c, pl.ds(0, 7), pl.ds(first, count)]
-            drain(seven, ans_send.at[c, part])
-            drain(fb.at[c, :, pl.ds(first, count)], fwd_send.at[c, part])
-            drain(seven, ans_recv.at[c, part])
+            count = PARTS[part][1]
+            drain(sb.at[c, pl.ds(0, 7 * count * SPOT)], ans_send.at[c, part])
+            drain(fb.at[c, :, pl.ds(0, count * SPOT)], fwd_send.at[c, part])
     for store in stores:
         store.wait()
 
 
-def smooth(test_vectors, coef_x, coef_y, coef_z, shift, meta):
+def smooth(test_vectors, coef_x, coef_y, coef_z, shift, split, count, owner, local):
     vmem = pl.BlockSpec(memory_space=pltpu.VMEM)
     anywhere = pl.BlockSpec(memory_space=pl.ANY)
     cells = pltpu.VMEM((NX, NY, ROWS), F32)
@@ -454,13 +510,21 @@
         smooth_kernel,
         out_shape=(
             jax.ShapeDtypeStruct((VECS, NX, NY, ROWS), F32),
-            jax.ShapeDtypeStruct((CHUNKS, SITES, KV, ROWS), BF16),
-            jax.ShapeDtypeStruct((CHUNKS, LINE * CORES, LINE, 2 * LINE, KV, ROWS), BF16),
-            jax.ShapeDtypeStruct((8, ROWS), jnp.int32),
+            jax.ShapeDtypeStruct((len(PAIRS), SITES, ROWS), F32),
         ),
-        in_specs=[anywhere] * 5 + [vmem],
-        out_specs=(anywhere, vmem, anywhere, vmem),
+        in_specs=[anywhere] * 9,
+        out_specs=(anywhere, vmem),
         scratch_shapes=[
+            pltpu.VMEM((NX, 1, NY), jnp.int32),
+            pltpu.VMEM((NX, 1, NY), jnp.int32),
+            pltpu.VMEM((NX, SLOTS, NY), jnp.int32),
+            pltpu.VMEM((NX, SLOTS, NY), jnp.int32),
+            pltpu.VMEM((8, ROWS), jnp.int32),
+            pltpu.VMEM((8, ROWS), jnp.int32),
+            pltpu.SMEM((8, ROWS), jnp.int32),
+            pltpu.VMEM((CHUNKS, SITES, KV, ROWS), BF16),
+            *([pltpu.VMEM((EMPTY + 8, KV, ROWS), BF16)] * CHUNKS),
+            pltpu.VMEM((len(PAIRS), SITES * 8, ROWS), F32),
             pltpu.VMEM((VECS, NX, NY, ROWS), F32),
             pltpu.VMEM((4, NX, NY, ROWS), F32),
             pltpu.VMEM((CHUNKS, EXT, ROWS), F32),
@@ -478,8 +542,8 @@
             pltpu.SMEM((CHUNKS, LINE, LINE, 1, ROWS), jnp.int32),
             pltpu.SMEM((COARSE, ROWS), jnp.int32),
             *([rows] * (LINE * CHUNKS)),
-            pltpu.VMEM((CHUNKS, LINE * CORES, LINE, 2 * LINE, KV, ROWS), BF16),
-            pltpu.VMEM((CHUNKS, CORES, LINE, 2 * LINE, KV, ROWS), BF16),
+            pltpu.VMEM((CHUNKS, EMPTY, KV, ROWS), BF16),
+            pltpu.VMEM((CHUNKS, CORES, REPLY, KV, ROWS), BF16),
             dma((CHUNKS,)),
             dma((4,)),
             dma((CHUNKS,)),
@@ -495,13 +559,14 @@
             dma((CHUNKS, len(PARTS), CORES)),
             dma((CHUNKS, len(PARTS))),
             dma((CHUNKS, len(PARTS))),
-            dma((3,)),
+            dma((4,)),
+            dma((4,)),
         ],
         compiler_params=pltpu.CompilerParams(
             collective_id=0, has_side_effects=True, vmem_limit_bytes=60 * 1024 * 1024
         ),
         name="smooth",
-    )(test_vectors, coef_x, coef_y, coef_z, shift, meta)
+    )(test_vectors, coef_x, coef_y, coef_z, shift, split, count, owner, local)
 
 
 def solve_rows(gram, rhs):
@@ -533,80 +598,48 @@
     return out
 
 
-PAIRS = [(s, t) for s in range(SLOTS) for t in range(s + 1)] + [
-    (s, SLOTS) for s in range(SLOTS)
-]
-
-
-def weights_kernel(target, replies, blk, sm_in, w_out, sm_out, sums, copy_sem):
+def solve_kernel(sums, sm_in, w_out, sm_out, copy_sem):
     move = pltpu.make_async_copy(sm_in, sm_out, copy_sem)
     move.start()
-
-    def block(b, carry):
-        accs = [None] * len(PAIRS)
-        for c in range(CHUNKS):
-            values = []
-            for s in range(SLOTS):
-                at = target[2 * c + b // 32, lax.rem(b, 32) * SLOTS + s]
-                found = replies[c, jnp.maximum(at, 0)].astype(F32)
-                values.append(jnp.where(at >= 0, found, 0.0))
-            values.append(blk[c, b].astype(F32))
-            for n, (s, t) in enumerate(PAIRS):
-                prod = values[s] * values[t]
-                part = prod[0:8] + prod[8:16]
-                accs[n] = part if c == 0 else accs[n] + part
-        for n, acc in enumerate(accs):
-            sums[n, pl.ds(pl.multiple_of(b * 8, 8), 8), :] = acc
-        return carry
-
-    lax.fori_loop(0, SITES, block, 0)
     for g in range(SITES // 8):
         total = {}
         for n, pair in enumerate(PAIRS):
-            acc = sums[n, pl.ds(g * 64, 8, stride=8), :]
-            for h in range(1, 8):
-                acc = acc + sums[n, pl.ds(g * 64 + h, 8, stride=8), :]
-            acc = acc * (1.0 / VECS)
+            total[pair] = sums[n, pl.ds(g * 8, 8), :] * (1.0 / VECS)
             if pair[0] == pair[1]:
-                acc = acc + RIDGE
-            total[pair] = acc
+                total[pair] = total[pair] + RIDGE
         out = solve_rows(total, [total[s, SLOTS] for s in range(SLOTS)])
         for s in range(SLOTS):
             w_out[s, g // 2, pl.ds((g % 2) * 8, 8), :] = out[s]
     move.wait()
 
 
-def fit(target, replies, blk, sm):
+def fit(sums, sm):
     vmem = pl.BlockSpec(memory_space=pltpu.VMEM)
-    anywhere = pl.BlockSpec(memory_space=pl.ANY)
     return pl.pallas_call(
-        weights_kernel,
+        solve_kernel,
         out_shape=(
             jax.ShapeDtypeStruct((SLOTS, NX, NY, ROWS), F32),
             jax.ShapeDtypeStruct((VECS, NX, NY, ROWS), F32),
         ),
-        in_specs=[pl.BlockSpec(memory_space=pltpu.SMEM), vmem, vmem, vmem],
-        out_specs=(vmem, anywhere),
-        scratch_shapes=[
-            pltpu.VMEM((len(PAIRS), SITES * 8, ROWS), F32),
-            pltpu.SemaphoreType.DMA,
-        ],
+        in_specs=[vmem, vmem],
+        out_specs=(vmem, pl.BlockSpec(memory_space=pl.ANY)),
+        scratch_shapes=[pltpu.SemaphoreType.DMA],
         compiler_params=pltpu.CompilerParams(vmem_limit_bytes=60 * 1024 * 1024),
         name="fit",
-    )(target, replies, blk, sm)
+    )(sums, sm)
 
 
 def per_device(
     test_vectors, coef_x, coef_y, coef_z, shift, cf_split, nbr_count, nbr_owner, nbr_block
 ):
-    entries = SITES * SLOTS
-    live = (cf_split == 0)[..., None] & (jnp.arange(SLOTS) < nbr_count[..., None])
-    listed = jnp.where(live, nbr_owner * SITES + nbr_block, -1).reshape(entries // ROWS, ROWS)
-    coarse = jnp.pad(cf_split.reshape(1, SITES), ((0, 5), (0, ROWS - SITES)))
-    meta = jnp.concatenate([listed, coarse], axis=0)
-    sm, blk, replies, target = smooth(test_vectors, coef_x, coef_y, coef_z, shift, meta)
-    replies = replies.reshape(CHUNKS, LINE * CORES * 2 * PLANE, KV, ROWS)
-    weights, smoothed = fit(target, replies, blk, sm)
+    sm, sums = smooth(
+        test_vectors, coef_x, coef_y, coef_z, shift,
+        jnp.swapaxes(cf_split, 1, 2),
+        jnp.swapaxes(nbr_count, 1, 2),
+        jnp.transpose(nbr_owner, (0, 2, 3, 1)).reshape(NX, SLOTS, NY),
+        jnp.transpose(nbr_block, (0, 2, 3, 1)).reshape(NX, SLOTS, NY),
+    )
+    weights, smoothed = fit(sums, sm)
     return (smoothed, weights)
 
 

time: 70.1 us -> 64 us (0.913)
  other arithmetic: 3.36 us -> 0 us
  Pallas kernels: 65 us -> 63.2 us
  local copies, waits for them, and re-layouts: 0.81 us -> 0 us
    pallas_call x1, Pallas kernels: 7.55 us -> 3.37 us  [fit(): pl.pallas_call(solve_kernel, out_shape=(jax.ShapeDtypeStruct((SLOTS, NX,...]
    pallas_call x1, Pallas kernels: 57.5 us -> 59.8 us  [smooth(): pl.pallas_call(smooth_kernel, out_shape=(jax.ShapeDtypeStruct((VECS, NX,...]
    unnamed x1 -> x0, other arithmetic: 1.34 us -> none
    select_n x1 -> x0, other arithmetic: 0.72 us -> none  [per_device(): jnp.where(live, nbr_owner * SITES + nbr_block, -1)]
where the time goes in v7:
time: 64 us; the launch traced here: 63.8 us
  Pallas kernels  63.2 us (99%)
  between operations  0.64 us (1%)
    pallas_call x1, Pallas kernels, smooth(): pl.pallas_call(smooth_kernel, out_shape=(jax.ShapeDtypeStruct((VECS, NX,...  59.8 us
    pallas_call x1, Pallas kernels, fit(): pl.pallas_call(solve_kernel, out_shape=(jax.ShapeDtypeStruct((SLOTS, NX,...  3.37 us

profile of v7, /device:TPU:1, one launch (start us, length us, event | category | flops | bytes accessed | tf_op | source)
XLA Modules:
  0.0 63.8 jit_solution(1639391687952970860)
XLA Ops:
  0.6 59.8 %smooth.1 = (f32[48,4,16,128]{3,2,1,0:T(8,128)}, f32[14,64,128]{2,1,0:T(8,128)}) custom-call(f32[48,4,16,128]{3,2,1,0:T(8,128)} %tv.1, f32[4,16,128]{2,1,0:T(8,128)} %cx.1, f32[4,16,128]{2,1,0:T(8,128)} %cy.1, f32[4,16,128]{2,1,0:T(8,128)} %cz.1, f32[4,16,128]{2,1,0:T(8,128)} %sh.1, s32[4,1,16]{2,1,0:T(1,128)} %bitcast.18, s32[4,1,16]{2,1,0:T(1,128)} %bitcast.19, ...), custom_call_target="tpu_custom_call" | custom-call | tf_op jit(solution)/shard_map/smooth/pallas_call | solution.py:509
  60.4 3.4 %fit.1 = (f32[4,4,16,128]{3,2,1,0:T(8,128)}, f32[48,4,16,128]{3,2,1,0:T(8,128)}) custom-call(f32[14,64,128]{2,1,0:T(8,128)} %get-tuple-element.6.sums, f32[48,4,16,128]{3,2,1,0:T(8,128)} %get-tuple-element.7.sm_in), custom_call_target="tpu_custom_call" | custom-call | tf_op jit(solution)/shard_map/fit/pallas_call | solution.py:618

commit v8 on v7

--- a/solution.py
+++ b/solution.py
@@ -27,6 +27,35 @@
 
 def site_row(x, y):
     return (x + 1) * XROW + (y + 1) * KV
+
+
+def solve_rows(gram, rhs):
+    low = [[None] * SLOTS for _ in range(SLOTS)]
+    inv = []
+    for r in range(SLOTS):
+        scaled = []
+        diag = gram[r, r]
+        for c in range(r):
+            rest = gram[r, c]
+            for m in range(c):
+                rest = rest - scaled[m] * low[c][m]
+            scaled.append(rest)
+            low[r][c] = rest * inv[c]
+            diag = diag - rest * low[r][c]
+        inv.append(1.0 / diag)
+    fwd = []
+    for r in range(SLOTS):
+        rest = rhs[r]
+        for m in range(r):
+            rest = rest - low[r][m] * fwd[m]
+        fwd.append(rest)
+    out = [None] * SLOTS
+    for r in reversed(range(SLOTS)):
+        rest = fwd[r] * inv[r]
+        for m in range(r + 1, SLOTS):
+            rest = rest - low[m][r] * out[m]
+        out[r] = rest
+    return out
 
 
 PAIRS = [(s, t) for s in range(SLOTS) for t in range(s + 1)] + [(s, SLOTS) for s in range(SLOTS)]
@@ -90,7 +119,7 @@
 
 
 def smooth_kernel(
-    tv, cx, cy, cz, sh, split, count, owner, local, sm_out, sums,
+    tv, cx, cy, cz, sh, split, count, owner, local, sm_out, w_out,
     split_v, count_v, owner_v, local_v, meta, tgt, tgt_s, blk, rb0, rb1, rb2, part_sums,
     stage, coef, wa, wb, ka, kb, km, kp, fxs, fxr, fys, fyr,
     pair, lines, ranks, idv, line_s, rank_s, id_s, p00, p01, p02, p03, p10, p11, p12, p13, p20, p21, p22, p23, sb, fb,
@@ -123,21 +152,10 @@
         )
 
     loads = []
-    for n, part in enumerate((cx, cy, cz, sh)):
-        load = pltpu.make_async_copy(part, coef.at[n], coef_sem.at[n])
-        load.start()
-        loads.append(load)
-    coef_loads, loads = loads, []
-    lists = []
-    for n, part in enumerate((split, count, owner, local)):
-        load = pltpu.make_async_copy(part, cells[n], list_sem.at[n])
-        load.start()
-        lists.append(load)
     for c in range(CHUNKS):
         part = pl.ds(c * KV, KV)
-        load = pltpu.make_async_copy(tv.at[part], stage.at[part], in_sem.at[c])
-        load.start()
-        loads.append(load)
+        loads.append(pltpu.make_async_copy(tv.at[part], stage.at[part], in_sem.at[c]))
+    loads[0].start()
     barrier = pltpu.get_barrier_semaphore()
     for peer in peers[:2]:
         pl.semaphore_signal(barrier, inc=1, device_id=peer, device_id_type=MESH)
@@ -149,6 +167,18 @@
                     barrier, inc=1, device_id=device(axis, d, e), device_id_type=MESH
                 )
     greeted = 3 + len(AXES) * (LINE - 1) * CORES
+    for load in loads[1:]:
+        load.start()
+    coef_loads = []
+    for n, part in enumerate((cx, cy, cz, sh)):
+        load = pltpu.make_async_copy(part, coef.at[n], coef_sem.at[n])
+        load.start()
+        coef_loads.append(load)
+    lists = []
+    for n, part in enumerate((split, count, owner, local)):
+        load = pltpu.make_async_copy(part, cells[n], list_sem.at[n])
+        load.start()
+        lists.append(load)
 
     keep = (
         (i > 0).astype(F32),
@@ -278,9 +308,9 @@
         dst, peer = rb[c].at[piece(here, part)], device(a, d, e)
         if d == 0 and e == 0:
             return pltpu.make_async_copy(src, dst, own_sem.at[c, part])
-        if d == 2:
+        if d == 2 and part == 0:
             dst, peer = fb.at[c, e, piece(0, part)], device(a, 1 + 2 * e, 0)
-            return remote(src, dst, ans_send.at[c, part], hop_recv.at[c, part, e], peer)
+            return remote(src, dst, ans_send.at[c, part], hop_recv.at[c, e], peer)
         return remote(src, dst, ans_send.at[c, part], ans_recv.at[c, part], peer)
 
     def forward(c, part, e):
@@ -288,7 +318,7 @@
         origin = lax.rem(at[a] + 3 - 2 * e, LINE) * CORES + core
         return remote(
             fb.at[c, e, piece(0, part)], rb[c].at[piece(origin, part)],
-            fwd_send.at[c, part], ans_recv.at[c, part], device(a, 1 + 2 * e, e),
+            fwd_send.at[c], ans_recv.at[c, part], device(a, 1 + 2 * e, e),
         )
 
     order = [(d, e) for d in (2, 1, 3, 0) for e in range(CORES)]
@@ -348,26 +378,60 @@
                         c * KV + k, x, pl.ds(half * 8, 8), :
                     ]
 
+    def products(c, b):
+        column = ((b >> 4) & 1) * (ROWS // 2) + (b & (NY - 1))
+        values = []
+        for t in range(SLOTS):
+            found = tgt_s[2 * c + (b >> 5), column + t * NY]
+            values.append(rb[c][found].astype(F32))
+        values.append(blk[c, b].astype(F32))
+        for n, (p, q) in enumerate(PAIRS):
+            product = values[p] * values[q]
+            product = product[0:8] + product[8:16]
+            row = pl.ds(pl.multiple_of(b * 8, 8), 8)
+            if c:
+                product = product + part_sums[n, row, :]
+            part_sums[n, row, :] = product
+
     def add_products(c):
         def step(g, carry):
             for m in range(4):
-                b = g * 4 + m
-                column = ((b >> 4) & 1) * (ROWS // 2) + (b & (NY - 1))
-                values = []
-                for t in range(SLOTS):
-                    found = tgt_s[2 * c + (b >> 5), column + t * NY]
-                    values.append(rb[c][found].astype(F32))
-                values.append(blk[c, b].astype(F32))
-                row = pl.ds(pl.multiple_of(b * 8, 8), 8)
-                for n, (p, q) in enumerate(PAIRS):
-                    product = values[p] * values[q]
-                    product = product[0:8] + product[8:16]
-                    if c:
-                        product = product + part_sums[n, row, :]
-                    part_sums[n, row, :] = product
+                products(c, g * 4 + m)
             return carry
 
         lax.fori_loop(0, SITES // 4, step, 0)
+
+    def finish():
+        sub = lax.broadcasted_iota(jnp.int32, (8, ROWS), 0)
+        low4, low2, low1 = sub < 4, (sub & 2) == 0, (sub & 1) == 0
+
+        def merge(first, second, keep_first, shift):
+            first = first + pltpu.roll(first, 8 - shift, 0)
+            second = second + pltpu.roll(second, shift, 0)
+            return jnp.where(keep_first, first, second)
+
+        def group(g, carry):
+            total = {}
+            for n, pair in enumerate(PAIRS):
+                rows = [
+                    part_sums[n, pl.ds(pl.multiple_of(g * 64, 64) + 8 * m, 8), :]
+                    for m in range(8)
+                ]
+                rows = [
+                    jnp.where(low4, rows[m], rows[m + 4])
+                    + pltpu.roll(jnp.where(low4, rows[m + 4], rows[m]), 4, 0)
+                    for m in range(4)
+                ]
+                rows = [merge(rows[m], rows[m + 2], low2, 2) for m in range(2)]
+                total[pair] = merge(rows[0], rows[1], low1, 1) * (1.0 / VECS)
+                if pair[0] == pair[1]:
+                    total[pair] = total[pair] + RIDGE
+            out = solve_rows(total, [total[s, SLOTS] for s in range(SLOTS)])
+            for s in range(SLOTS):
+                w_out[s, pl.ds(pl.multiple_of(g * 8, 8), 8), :] = out[s]
+            return carry
+
+        lax.fori_loop(0, SITES // 8, group, 0)
 
     stores = []
 
@@ -464,11 +528,9 @@
     for c in range(CHUNKS):
         reply(c, 0)
     for c in range(CHUNKS):
+        reply_on(c, 0)
         reply(c, 1)
-        reply_on(c, 0)
     transpose_out(1, wb)
-    for c in range(CHUNKS):
-        reply_on(c, 1)
     transpose_out(2, wb)
     tgt_copy.wait()
     for c in range(CHUNKS):
@@ -476,12 +538,7 @@
             answer(c, part, 0, 0).wait()
             drain(sb.at[c, pl.ds(0, 7 * PARTS[part][1] * SPOT)], ans_recv.at[c, part])
         add_products(c)
-    for g in range(SITES // 8):
-        for n in range(len(PAIRS)):
-            acc = part_sums[n, pl.ds(g * 64, 8, stride=8), :]
-            for h in range(1, 8):
-                acc = acc + part_sums[n, pl.ds(g * 64 + h, 8, stride=8), :]
-            sums[n, pl.ds(g * 8, 8), :] = acc
+    finish()
 
     drain(fxs, send_sem.at[0])
     drain(fys, send_sem.at[1])
@@ -495,7 +552,7 @@
         for part in range(len(PARTS)):
             count = PARTS[part][1]
             drain(sb.at[c, pl.ds(0, 7 * count * SPOT)], ans_send.at[c, part])
-            drain(fb.at[c, :, pl.ds(0, count * SPOT)], fwd_send.at[c, part])
+        drain(fb.at[c, :, pl.ds(0, PARTS[0][1] * SPOT)], fwd_send.at[c])
     for store in stores:
         store.wait()
 
@@ -510,7 +567,7 @@
         smooth_kernel,
         out_shape=(
             jax.ShapeDtypeStruct((VECS, NX, NY, ROWS), F32),
-            jax.ShapeDtypeStruct((len(PAIRS), SITES, ROWS), F32),
+            jax.ShapeDtypeStruct((SLOTS, SITES, ROWS), F32),
         ),
         in_specs=[anywhere] * 9,
         out_specs=(anywhere, vmem),
@@ -556,8 +613,8 @@
             dma((CHUNKS, 4)),
             dma((CHUNKS, len(PARTS))),
             dma((CHUNKS, len(PARTS))),
-            dma((CHUNKS, len(PARTS), CORES)),
-            dma((CHUNKS, len(PARTS))),
+            dma((CHUNKS, CORES)),
+            dma((CHUNKS,)),
             dma((CHUNKS, len(PARTS))),
             dma((4,)),
             dma((4,)),
@@ -569,77 +626,55 @@
     )(test_vectors, coef_x, coef_y, coef_z, shift, split, count, owner, local)
 
 
-def solve_rows(gram, rhs):
-    low = [[None] * SLOTS for _ in range(SLOTS)]
-    inv = []
-    for r in range(SLOTS):
-        scaled = []
-        diag = gram[r, r]
-        for c in range(r):
-            rest = gram[r, c]
-            for m in range(c):
-                rest = rest - scaled[m] * low[c][m]
-            scaled.append(rest)
-            low[r][c] = rest * inv[c]
-            diag = diag - rest * low[r][c]
-        inv.append(1.0 / diag)
-    fwd = []
-    for r in range(SLOTS):
-        rest = rhs[r]
-        for m in range(r):
-            rest = rest - low[r][m] * fwd[m]
-        fwd.append(rest)
-    out = [None] * SLOTS
-    for r in reversed(range(SLOTS)):
-        rest = fwd[r] * inv[r]
-        for m in range(r + 1, SLOTS):
-            rest = rest - low[m][r] * out[m]
-        out[r] = rest
-    return out
-
-
-def solve_kernel(sums, sm_in, w_out, sm_out, copy_sem):
-    move = pltpu.make_async_copy(sm_in, sm_out, copy_sem)
-    move.start()
-    for g in range(SITES // 8):
-        total = {}
-        for n, pair in enumerate(PAIRS):
-            total[pair] = sums[n, pl.ds(g * 8, 8), :] * (1.0 / VECS)
-            if pair[0] == pair[1]:
-                total[pair] = total[pair] + RIDGE
-        out = solve_rows(total, [total[s, SLOTS] for s in range(SLOTS)])
-        for s in range(SLOTS):
-            w_out[s, g // 2, pl.ds((g % 2) * 8, 8), :] = out[s]
-    move.wait()
-
-
-def fit(sums, sm):
-    vmem = pl.BlockSpec(memory_space=pltpu.VMEM)
+def pass_kernel(w_in, sm_in, w_out, sm_out, w_hold, sm_hold, in_sem, out_sem):
+    parts = [(w_in, w_hold, w_out)]
+    for c in range(CHUNKS):
+        part = pl.ds(c * KV, KV)
+        parts.append((sm_in.at[part], sm_hold.at[part], sm_out.at[part]))
+    ins = [pltpu.make_async_copy(a, b, in_sem.at[n]) for n, (a, b, _) in enumerate(parts)]
+    outs = [pltpu.make_async_copy(b, d, out_sem.at[n]) for n, (_, b, d) in enumerate(parts)]
+    for copy in ins:
+        copy.start()
+    for load, store in zip(ins, outs):
+        load.wait()
+        store.start()
+    for store in outs:
+        store.wait()
+
+
+def pass_on_results(weights, sm):
+    anywhere = pl.BlockSpec(memory_space=pl.ANY)
+    dma = pltpu.SemaphoreType.DMA
     return pl.pallas_call(
-        solve_kernel,
+        pass_kernel,
         out_shape=(
-            jax.ShapeDtypeStruct((SLOTS, NX, NY, ROWS), F32),
-            jax.ShapeDtypeStruct((VECS, NX, NY, ROWS), F32),
+            jax.ShapeDtypeStruct(weights.shape, F32),
+            jax.ShapeDtypeStruct(sm.shape, F32),
         ),
-        in_specs=[vmem, vmem],
-        out_specs=(vmem, pl.BlockSpec(memory_space=pl.ANY)),
-        scratch_shapes=[pltpu.SemaphoreType.DMA],
+        in_specs=[anywhere, anywhere],
+        out_specs=(anywhere, anywhere),
+        scratch_shapes=[
+            pltpu.VMEM(weights.shape, F32),
+            pltpu.VMEM(sm.shape, F32),
+            dma((CHUNKS + 1,)),
+            dma((CHUNKS + 1,)),
+        ],
         compiler_params=pltpu.CompilerParams(vmem_limit_bytes=60 * 1024 * 1024),
         name="fit",
-    )(sums, sm)
+    )(weights, sm)
 
 
 def per_device(
     test_vectors, coef_x, coef_y, coef_z, shift, cf_split, nbr_count, nbr_owner, nbr_block
 ):
-    sm, sums = smooth(
+    sm, weights = smooth(
         test_vectors, coef_x, coef_y, coef_z, shift,
         jnp.swapaxes(cf_split, 1, 2),
         jnp.swapaxes(nbr_count, 1, 2),
         jnp.transpose(nbr_owner, (0, 2, 3, 1)).reshape(NX, SLOTS, NY),
         jnp.transpose(nbr_block, (0, 2, 3, 1)).reshape(NX, SLOTS, NY),
     )
-    weights, smoothed = fit(sums, sm)
+    weights, smoothed = pass_on_results(weights.reshape(SLOTS, NX, NY, ROWS), sm)
     return (smoothed, weights)
 
 

time: 64 us -> 60.8 us (0.950)
  Pallas kernels: 63.2 us -> 60 us
    pallas_call x1, Pallas kernels: 59.8 us -> 57.7 us  [smooth(): pl.pallas_call(smooth_kernel, out_shape=(jax.ShapeDtypeStruct((VECS, NX,...]
    pallas_call x1, Pallas kernels: 3.37 us -> 2.32 us  [pass_on_results(): pl.pallas_call(pass_kernel, out_shape=(jax.ShapeDtypeStruct(weights.shape...]
where the time goes in v8:
time: 60.8 us; the launch traced here: 60.6 us
  Pallas kernels  60 us (99%)
  between operations  0.64 us (1%)
    pallas_call x1, Pallas kernels, smooth(): pl.pallas_call(smooth_kernel, out_shape=(jax.ShapeDtypeStruct((VECS, NX,...  57.7 us
    pallas_call x1, Pallas kernels, pass_on_results(): pl.pallas_call(pass_kernel, out_shape=(jax.ShapeDtypeStruct(weights.shape...  2.32 us

profile of v8, /device:TPU:1, one launch (start us, length us, event | category | flops | bytes accessed | tf_op | source)
XLA Modules:
  0.0 60.6 jit_solution(14262913847741571275)
XLA Ops:
  0.6 57.7 %smooth.1 = (f32[48,4,16,128]{3,2,1,0:T(8,128)}, f32[4,64,128]{2,1,0:T(8,128)}) custom-call(f32[48,4,16,128]{3,2,1,0:T(8,128)} %tv.1, f32[4,16,128]{2,1,0:T(8,128)} %cx.1, f32[4,16,128]{2,1,0:T(8,128)} %cy.1, f32[4,16,128]{2,1,0:T(8,128)} %cz.1, f32[4,16,128]{2,1,0:T(8,128)} %sh.1, s32[4,1,16]{2,1,0:T(1,128)} %bitcast.20, s32[4,1,16]{2,1,0:T(1,128)} %bitcast.21, ...), custom_call_target="tpu_custom_call" | custom-call | tf_op jit(solution)/shard_map/smooth/pallas_call | solution.py:566
  58.3 2.3 %fit.1 = (f32[4,4,16,128]{3,2,1,0:T(8,128)}, f32[48,4,16,128]{3,2,1,0:T(8,128)}) custom-call(f32[4,4,16,128]{3,2,1,0:T(8,128)} %bitcast.17, f32[48,4,16,128]{3,2,1,0:T(8,128)} %get-tuple-element.7.sm_in), custom_call_target="tpu_custom_call" | custom-call | tf_op jit(solution)/shard_map/fit/pallas_call | solution.py:648

commit v9 on v8

--- a/solution.py
+++ b/solution.py
@@ -68,6 +68,7 @@
 BACKS = (0, 1, 3, 2)
 EMPTY = LINE * CORES * PLANE * 2
 SPOT = 2 * LINE
+GRAM_ORDER = (1, 2, 0)
 REPLY = PLANE * 2
 PARTS = ((0, 3), (3, 1))
 
@@ -107,7 +108,7 @@
         for c, (a, u, v) in enumerate(ROUTES):
             back = (at[v] - here[v]) & 3
             spot = jnp.where(back == 2, 3, jnp.where(back == 3, 2, back))
-            slot = ((at[a] * CORES + (own & 1)) * PLANE + spot * LINE + at[u]) * 2 + place
+            slot = ((at[a] * CORES + (own & 1)) * PLANE + spot * LINE + ((at[u] - here[u]) & 3)) * 2 + place
             targets[c].append(jnp.where(own < 0, EMPTY, slot))
     coarse = meta[2:3]
     rank = jnp.sum(jnp.where(sub < lane, column(coarse), 0), axis=0, keepdims=True)
@@ -122,7 +123,7 @@
     tv, cx, cy, cz, sh, split, count, owner, local, sm_out, w_out,
     split_v, count_v, owner_v, local_v, meta, tgt, tgt_s, blk, rb0, rb1, rb2, part_sums,
     stage, coef, wa, wb, ka, kb, km, kp, fxs, fxr, fys, fyr,
-    pair, lines, ranks, idv, line_s, rank_s, id_s, p00, p01, p02, p03, p10, p11, p12, p13, p20, p21, p22, p23, sb, fb,
+    pair, lines, ranks, idv, line_s, rank_s, id_s, tile_s, p00, p01, p02, p03, p10, p11, p12, p13, p20, p21, p22, p23, sb, fb,
     in_sem, coef_sem, out_sem, send_sem, recv_sem, pair_sem, table_sem,
     near_sem, cast_send, cast_recv, ans_send, ans_recv, hop_recv, fwd_send, own_sem, smem_sem, list_sem,
 ):
@@ -279,21 +280,32 @@
 
     def spread_copies(c):
         a, u, v = ROUTES[c]
-        ref = pg[c][0].at[at[u]]
         return [
-            remote(ref, ref, near_sem.at[c, 0], near_sem.at[c, 1], device(u, d, 0))
+            remote(
+                pg[c][0].at[0], pg[c][0].at[LINE - d],
+                near_sem.at[c, 0], near_sem.at[c, 1], device(u, d, 0),
+            )
             for d in (2, 1, 3)
         ]
 
     def cast_copies(c):
         a, u, v = ROUTES[c]
-        plan = ((0, 0, 3, 1), (0, 1, 1, 3), (0, 1, 3, 1), (0, 0, 1, 3), (3, 0, 2, 1), (1, 1, 2, 3))
+        plan = (
+            (0, 0, 1, 3, 1, 0, 0),
+            (0, 0, 1, 1, 3, 1, 2),
+            (0, 1, 1, 3, 1, 0, 0),
+            (0, 2, 2, 1, 3, 1, 1),
+            (0, 2, 2, 3, 1, 0, 2),
+            (0, 1, 1, 1, 3, 1, 2),
+            (3, 0, 2, 2, 1, 2, 3),
+            (1, 2, 2, 2, 3, 2, 3),
+        )
         return [
             remote(
-                pg[c][src].at[pl.ds(half * 2, 2)], pg[c][dst].at[pl.ds(half * 2, 2)],
-                cast_send.at[c, n // 2], cast_recv.at[c, min(n, 2 + n // 4)], device(v, d, 0),
+                pg[c][src].at[pl.ds(first, size)], pg[c][dst].at[pl.ds(first, size)],
+                cast_send.at[c, out], cast_recv.at[c, into], device(v, d, 0),
             )
-            for n, (src, half, dst, d) in enumerate(plan)
+            for src, first, size, dst, d, out, into in plan
         ]
 
     def piece(slot, part):
@@ -326,40 +338,51 @@
     def spread(c):
         a, u, v = ROUTES[c]
         for r in range(COARSE):
-            pg[c][0][at[u], r] = blk[c, id_s[r, 0] & (SITES - 1)]
-        for copy in spread_copies(c):
+            pg[c][0][0, r] = blk[c, id_s[r, 0] & (SITES - 1)]
+        for copy in spread_copies(c) + cast_copies(c)[:2]:
             copy.start()
 
     def cast(c):
         drain(pg[c][1].at[pl.ds(0, 3)], near_sem.at[c, 1])
-        for copy in cast_copies(c)[:4]:
+        for copy in cast_copies(c)[2:6]:
             copy.start()
 
     def pass_on(c):
-        all_copies = cast_copies(c)
         for n in range(2):
-            all_copies[n].wait_recv()
-            all_copies[4 + n].start()
-
-    def reply(c, part):
+            drain(pg[c][0].at[pl.ds(0, 2)], cast_recv.at[c, n])
+            cast_copies(c)[6 + n].start()
+
+    def find_tiles(c):
         a, u, v = ROUTES[c]
         n = AXES.index(a)
-        drain(pg[c][0], cast_recv.at[c, 2 + part])
-        first, count = PARTS[part]
-        for d, e in order:
-            q, to = lax.rem(at[a] + d, LINE), lax.rem(core + e, CORES)
-            slot = q * CORES + to
-            for place in range(first, first + count):
-                back = BACKS[place]
+
+        def one(slot, carry):
+            q, to = slot // CORES, lax.rem(slot, CORES)
+            for place, back in enumerate(BACKS):
                 vv = lax.rem(at[v] + back, LINE)
-                tiles = []
-                for uu in range(LINE):
+                for ahead in range(LINE):
+                    uu = lax.rem(at[u] + ahead, LINE)
                     whose = {a: at[a], u: uu, v: vv}
                     owner = whose["x"] * 32 + whose["z"] * 8 + whose["y"] * 2 + core
                     for p in range(2):
                         block = line_s[n, q, to, p, 0, owner] & (SITES - 1)
                         rank = rank_s[c, vv, uu, 0, block] & (COARSE - 1)
-                        tiles.append(pg[c][back][uu, rank])
+                        tile_s[c, slot, place * SPOT + ahead * 2 + p] = rank
+            return carry
+
+        lax.fori_loop(0, LINE * CORES, one, 0)
+
+    def reply(c, part):
+        a, u, v = ROUTES[c]
+        drain(pg[c][0], cast_recv.at[c, 2 + part])
+        first, count = PARTS[part]
+        for d, e in order:
+            slot = lax.rem(at[a] + d, LINE) * CORES + lax.rem(core + e, CORES)
+            for place in range(first, first + count):
+                tiles = []
+                for t in range(SPOT):
+                    rank = tile_s[c, slot, place * SPOT + t] & (COARSE - 1)
+                    tiles.append(pg[c][BACKS[place]][t // 2, rank])
                 for t, tile in enumerate(tiles):
                     sb[c, slot * REPLY + place * SPOT + t] = tile
             answer(c, part, d, e).start()
@@ -389,7 +412,7 @@
             product = values[p] * values[q]
             product = product[0:8] + product[8:16]
             row = pl.ds(pl.multiple_of(b * 8, 8), 8)
-            if c:
+            if c != GRAM_ORDER[0]:
                 product = product + part_sums[n, row, :]
             part_sums[n, row, :] = product
 
@@ -518,22 +541,25 @@
     drain(ranks.at[:, pl.ds(0, 3)], table_sem.at[1, 1])
     rank_copy = pltpu.make_async_copy(ranks, rank_s, smem_sem.at[2])
     rank_copy.start()
-    for c in range(CHUNKS):
-        cast(c)
+    cast(0)
+    cast(1)
     line_copy.wait()
     rank_copy.wait()
-    transpose_out(0, wb)
+    find_tiles(1)
+    cast(2)
+    find_tiles(0)
+    find_tiles(2)
     for c in range(CHUNKS):
         pass_on(c)
-    for c in range(CHUNKS):
+    for c in (1, 2, 0):
         reply(c, 0)
-    for c in range(CHUNKS):
+    for c in (1, 0, 2):
         reply_on(c, 0)
         reply(c, 1)
-    transpose_out(1, wb)
-    transpose_out(2, wb)
+    for c in range(CHUNKS):
+        transpose_out(c, wb)
     tgt_copy.wait()
-    for c in range(CHUNKS):
+    for c in GRAM_ORDER:
         for part in range(len(PARTS)):
             answer(c, part, 0, 0).wait()
             drain(sb.at[c, pl.ds(0, 7 * PARTS[part][1] * SPOT)], ans_recv.at[c, part])
@@ -598,6 +624,7 @@
             pltpu.SMEM((len(AXES), LINE, CORES, 3, 1, ROWS), jnp.int32),
             pltpu.SMEM((CHUNKS, LINE, LINE, 1, ROWS), jnp.int32),
             pltpu.SMEM((COARSE, ROWS), jnp.int32),
+            pltpu.SMEM((CHUNKS, LINE * CORES, REPLY), jnp.int32),
             *([rows] * (LINE * CHUNKS)),
             pltpu.VMEM((CHUNKS, EMPTY, KV, ROWS), BF16),
             pltpu.VMEM((CHUNKS, CORES, REPLY, KV, ROWS), BF16),

time: 60.8 us -> 59.8 us (0.984)
  Pallas kernels: 60 us -> 59 us
    pallas_call x1, Pallas kernels: 57.7 us -> 56.7 us  [smooth(): pl.pallas_call(smooth_kernel, out_shape=(jax.ShapeDtypeStruct((VECS, NX,...]
where the time goes in v9:
time: 59.8 us; the launch traced here: 59.7 us
  Pallas kernels  59 us (99%)
  between operations  0.64 us (1%)
    pallas_call x1, Pallas kernels, smooth(): pl.pallas_call(smooth_kernel, out_shape=(jax.ShapeDtypeStruct((VECS, NX,...  56.7 us
    pallas_call x1, Pallas kernels, pass_on_results(): pl.pallas_call(pass_kernel, out_shape=(jax.ShapeDtypeStruct(weights.shape...  2.32 us

profile of v9, /device:TPU:1, one launch (start us, length us, event | category | flops | bytes accessed | tf_op | source)
XLA Modules:
  0.0 59.7 jit_solution(2957002858079078471)
XLA Ops:
  0.6 56.7 %smooth.1 = (f32[48,4,16,128]{3,2,1,0:T(8,128)}, f32[4,64,128]{2,1,0:T(8,128)}) custom-call(f32[48,4,16,128]{3,2,1,0:T(8,128)} %tv.1, f32[4,16,128]{2,1,0:T(8,128)} %cx.1, f32[4,16,128]{2,1,0:T(8,128)} %cy.1, f32[4,16,128]{2,1,0:T(8,128)} %cz.1, f32[4,16,128]{2,1,0:T(8,128)} %sh.1, s32[4,1,16]{2,1,0:T(1,128)} %bitcast.20, s32[4,1,16]{2,1,0:T(1,128)} %bitcast.21, ...), custom_call_target="tpu_custom_call" | custom-call | tf_op jit(solution)/shard_map/smooth/pallas_call | solution.py:592
  57.4 2.3 %fit.1 = (f32[4,4,16,128]{3,2,1,0:T(8,128)}, f32[48,4,16,128]{3,2,1,0:T(8,128)}) custom-call(f32[4,4,16,128]{3,2,1,0:T(8,128)} %bitcast.17, f32[48,4,16,128]{3,2,1,0:T(8,128)} %get-tuple-element.7.sm_in), custom_call_target="tpu_custom_call" | custom-call | tf_op jit(solution)/shard_map/fit/pallas_call | solution.py:675

commit v10 on v9

--- a/solution.py
+++ b/solution.py
@@ -64,11 +64,11 @@
 CORES = 2
 COARSE = 16
 PLANE = LINE * LINE
-ROUTES = (("x", "z", "y"), ("y", "x", "z"), ("z", "y", "x"))
+ROUTES = (("z", "x", "y"), ("y", "z", "x"), ("x", "y", "z"))
 BACKS = (0, 1, 3, 2)
 EMPTY = LINE * CORES * PLANE * 2
 SPOT = 2 * LINE
-GRAM_ORDER = (1, 2, 0)
+GRAM_ORDER = (1, 0, 2)
 REPLY = PLANE * 2
 PARTS = ((0, 3), (3, 1))
 
@@ -551,9 +551,9 @@
     find_tiles(2)
     for c in range(CHUNKS):
         pass_on(c)
-    for c in (1, 2, 0):
+    for c in GRAM_ORDER:
         reply(c, 0)
-    for c in (1, 0, 2):
+    for c in (0, 1, 2):
         reply_on(c, 0)
         reply(c, 1)
     for c in range(CHUNKS):

time: 59.8 us -> 61.4 us (1.027)
  Pallas kernels: 59 us -> 60.6 us
    pallas_call x1, Pallas kernels: 56.7 us -> 58.3 us  [smooth(): pl.pallas_call(smooth_kernel, out_shape=(jax.ShapeDtypeStruct((VECS, NX,...]
where the time goes in v10:
time: 61.4 us; the launch traced here: 61.3 us
  Pallas kernels  60.6 us (99%)
  between operations  0.64 us (1%)
    pallas_call x1, Pallas kernels, smooth(): pl.pallas_call(smooth_kernel, out_shape=(jax.ShapeDtypeStruct((VECS, NX,...  58.3 us
    pallas_call x1, Pallas kernels, pass_on_results(): pl.pallas_call(pass_kernel, out_shape=(jax.ShapeDtypeStruct(weights.shape...  2.32 us

profile of v10, /device:TPU:1, one launch (start us, length us, event | category | flops | bytes accessed | tf_op | source)
XLA Modules:
  0.0 61.3 jit_solution(13607801737667930268)
XLA Ops:
  0.6 58.3 %smooth.1 = (f32[48,4,16,128]{3,2,1,0:T(8,128)}, f32[4,64,128]{2,1,0:T(8,128)}) custom-call(f32[48,4,16,128]{3,2,1,0:T(8,128)} %tv.1, f32[4,16,128]{2,1,0:T(8,128)} %cx.1, f32[4,16,128]{2,1,0:T(8,128)} %cy.1, f32[4,16,128]{2,1,0:T(8,128)} %cz.1, f32[4,16,128]{2,1,0:T(8,128)} %sh.1, s32[4,1,16]{2,1,0:T(1,128)} %bitcast.20, s32[4,1,16]{2,1,0:T(1,128)} %bitcast.21, ...), custom_call_target="tpu_custom_call" | custom-call | tf_op jit(solution)/shard_map/smooth/pallas_call | solution.py:592
  58.9 2.3 %fit.1 = (f32[4,4,16,128]{3,2,1,0:T(8,128)}, f32[48,4,16,128]{3,2,1,0:T(8,128)}) custom-call(f32[4,4,16,128]{3,2,1,0:T(8,128)} %bitcast.17, f32[48,4,16,128]{3,2,1,0:T(8,128)} %get-tuple-element.7.sm_in), custom_call_target="tpu_custom_call" | custom-call | tf_op jit(solution)/shard_map/fit/pallas_call | solution.py:675

commit v11 on v9

--- a/solution.py
+++ b/solution.py
@@ -63,6 +63,7 @@
 LINE = 4
 CORES = 2
 COARSE = 16
+FINE = 48
 PLANE = LINE * LINE
 ROUTES = (("x", "z", "y"), ("y", "x", "z"), ("z", "y", "x"))
 BACKS = (0, 1, 3, 2)
@@ -81,9 +82,6 @@
 
     def column(row):
         return jnp.sum(jnp.where(diag, row, 0), axis=1, keepdims=True)
-
-    def line(col):
-        return jnp.sum(jnp.where(diag, col, 0), axis=0, keepdims=True)
 
     members, keys, owners = [], [], []
     for h in range(2):
@@ -98,7 +96,6 @@
     first = jnp.where(first >= none, 0, first)
     second = jnp.maximum(*[jnp.where(m, k, 0) for m, k in zip(members, keys)])
     second = jnp.max(second, axis=1, keepdims=True)
-    wanted = [line(v) & (SITES - 1) for v in (first, second)]
     targets = [[] for _ in ROUTES]
     for h in range(2):
         own = owners[h]
@@ -112,19 +109,34 @@
             targets[c].append(jnp.where(own < 0, EMPTY, slot))
     coarse = meta[2:3]
     rank = jnp.sum(jnp.where(sub < lane, column(coarse), 0), axis=0, keepdims=True)
-    hit = (rank == sub[:COARSE]) & (coarse > 0)
-    ids = jnp.sum(jnp.where(hit, lane[:COARSE], 0), axis=1, keepdims=True)
-    ids = jnp.broadcast_to(ids, (COARSE, ROWS))
+    fine_rank = jnp.minimum(lane[:1] - rank, FINE)
+    fine_rank = jnp.where(coarse > 0, FINE, fine_rank)
+
+    def numbers(hit):
+        found = jnp.sum(jnp.where(hit, lane[: hit.shape[0]], 0), axis=1, keepdims=True)
+        return jnp.broadcast_to(found, hit.shape)
+
+    ids = numbers((rank == sub[:COARSE]) & (coarse > 0))
+    fine_ids = numbers((fine_rank == sub[:FINE]) & (lane[:1] < SITES))
     rank = jnp.minimum(rank, COARSE - 1)
-    return wanted, targets, rank, ids
+    return (first, second), targets, rank, ids, fine_ids, fine_rank
+
+
+def ranks_wanted(blocks, table):
+    lane = lax.broadcasted_iota(jnp.int32, (ROWS, ROWS), 1)
+    sub = lax.broadcasted_iota(jnp.int32, (ROWS, ROWS), 0)
+    found = jnp.sum(
+        jnp.where(lane == (blocks & (SITES - 1)), table, 0), axis=1, keepdims=True
+    )
+    return jnp.sum(jnp.where(lane == sub, found, 0), axis=0, keepdims=True)
 
 
 def smooth_kernel(
     tv, cx, cy, cz, sh, split, count, owner, local, sm_out, w_out,
     split_v, count_v, owner_v, local_v, meta, tgt, tgt_s, blk, rb0, rb1, rb2, part_sums,
     stage, coef, wa, wb, ka, kb, km, kp, fxs, fxr, fys, fyr,
-    pair, lines, ranks, idv, line_s, rank_s, id_s, tile_s, p00, p01, p02, p03, p10, p11, p12, p13, p20, p21, p22, p23, sb, fb,
-    in_sem, coef_sem, out_sem, send_sem, recv_sem, pair_sem, table_sem,
+    pair, lines, near, far, block_cols, idv, line_s, id_s, fine_s, spot_s, p00, p01, p02, p03, p10, p11, p12, p13, p20, p21, p22, p23, sb, fb,
+    in_sem, coef_sem, out_sem, send_sem, recv_sem, pair_sem, table_sem, gather_sem,
     near_sem, cast_send, cast_recv, ans_send, ans_recv, hop_recv, fwd_send, own_sem, smem_sem, list_sem,
 ):
     cells = (split_v, count_v, owner_v, local_v)
@@ -258,25 +270,61 @@
     def line_copies():
         return [
             remote(
-                pair, lines.at[n, at[axis]], table_sem.at[0, 0], table_sem.at[0, 1],
+                pair, lines.at[n, at[axis]], table_sem.at[0], table_sem.at[1],
                 device(axis, d, 0),
             )
             for n, axis in enumerate(AXES)
             for d in range(1, LINE)
         ]
 
-    def rank_copies():
-        out = []
-        for c, (a, u, v) in enumerate(ROUTES):
-            src = lines.at[AXES.index(u), :, core, 2]
-            for d in range(1, LINE):
-                out.append(
-                    remote(
-                        src, ranks.at[c, at[v]], table_sem.at[1, 0], table_sem.at[1, 1],
-                        device(v, d, 0),
-                    )
-                )
-        return out
+    def gather_copies(step):
+        send, recv = gather_sem.at[step, 0], gather_sem.at[step, 1]
+        if step == 0:
+            slot = near.at[at["y"] * CORES + core]
+            return [
+                remote(slot, slot, send, recv, device("y", d, e))
+                for d in range(LINE)
+                for e in range(CORES)
+                if d or e
+            ]
+        slot = far.at[at["x"], at["z"]] if step == 1 else far.at[at["x"]]
+        return [
+            remote(slot, slot, send, recv, device("zx"[step - 1], d, 0)) for d in range(1, LINE)
+        ]
+
+    def gathered(step):
+        if step == 0:
+            return near.at[pl.ds(0, 7)]
+        return far.at[0, pl.ds(0, 3)] if step == 1 else far.at[pl.ds(0, 3)]
+
+    def gather_step(step):
+        drain(gathered(step), gather_sem.at[step, 1])
+        if step == 0:
+            for n in range(LINE * CORES):
+                far[at["x"], at["z"], n : n + 1] = near[n, 0:1]
+        for copy in gather_copies(step + 1):
+            copy.start()
+
+    def ask():
+        drain(gathered(2), gather_sem.at[2, 1])
+        table = far[...].reshape(ROWS, ROWS)
+        for p in range(2):
+            pair[core, p] = ranks_wanted(block_cols[p], table)
+        pair_copy().start()
+
+    def ask_lines():
+        pair_copy().wait_recv()
+        for copy in line_copies():
+            copy.start()
+        for n, axis in enumerate(AXES):
+            lines[n, at[axis]] = pair[...]
+
+    steps = {
+        (0, 1): lambda: gather_step(0),
+        (1, 0): lambda: gather_step(1),
+        (1, 2): ask,
+        (2, 1): ask_lines,
+    }
 
     def spread_copies(c):
         a, u, v = ROUTES[c]
@@ -352,37 +400,27 @@
             drain(pg[c][0].at[pl.ds(0, 2)], cast_recv.at[c, n])
             cast_copies(c)[6 + n].start()
 
-    def find_tiles(c):
+    def reply(c, part):
         a, u, v = ROUTES[c]
         n = AXES.index(a)
-
-        def one(slot, carry):
-            q, to = slot // CORES, lax.rem(slot, CORES)
-            for place, back in enumerate(BACKS):
-                vv = lax.rem(at[v] + back, LINE)
-                for ahead in range(LINE):
-                    uu = lax.rem(at[u] + ahead, LINE)
-                    whose = {a: at[a], u: uu, v: vv}
-                    owner = whose["x"] * 32 + whose["z"] * 8 + whose["y"] * 2 + core
-                    for p in range(2):
-                        block = line_s[n, q, to, p, 0, owner] & (SITES - 1)
-                        rank = rank_s[c, vv, uu, 0, block] & (COARSE - 1)
-                        tile_s[c, slot, place * SPOT + ahead * 2 + p] = rank
-            return carry
-
-        lax.fori_loop(0, LINE * CORES, one, 0)
-
-    def reply(c, part):
-        a, u, v = ROUTES[c]
         drain(pg[c][0], cast_recv.at[c, 2 + part])
         first, count = PARTS[part]
         for d, e in order:
-            slot = lax.rem(at[a] + d, LINE) * CORES + lax.rem(core + e, CORES)
+            q, to = lax.rem(at[a] + d, LINE), lax.rem(core + e, CORES)
+            slot = q * CORES + to
             for place in range(first, first + count):
+                back = BACKS[place]
                 tiles = []
-                for t in range(SPOT):
-                    rank = tile_s[c, slot, place * SPOT + t] & (COARSE - 1)
-                    tiles.append(pg[c][BACKS[place]][t // 2, rank])
+                for ahead in range(LINE):
+                    whose = {
+                        a: at[a],
+                        u: lax.rem(at[u] + ahead, LINE),
+                        v: lax.rem(at[v] + back, LINE),
+                    }
+                    owner = whose["x"] * 32 + whose["z"] * 8 + whose["y"] * 2 + core
+                    for p in range(2):
+                        rank = line_s[n, q, to, p, 0, owner] & (COARSE - 1)
+                        tiles.append(pg[c][back][ahead, rank])
                 for t, tile in enumerate(tiles):
                     sb[c, slot * REPLY + place * SPOT + t] = tile
             answer(c, part, d, e).start()
@@ -401,7 +439,8 @@
                         c * KV + k, x, pl.ds(half * 8, 8), :
                     ]
 
-    def products(c, b):
+    def products(c, place):
+        b = fine_s[place, 0] & (SITES - 1)
         column = ((b >> 4) & 1) * (ROWS // 2) + (b & (NY - 1))
         values = []
         for t in range(SLOTS):
@@ -411,10 +450,9 @@
         for n, (p, q) in enumerate(PAIRS):
             product = values[p] * values[q]
             product = product[0:8] + product[8:16]
-            row = pl.ds(pl.multiple_of(b * 8, 8), 8)
             if c != GRAM_ORDER[0]:
-                product = product + part_sums[n, row, :]
-            part_sums[n, row, :] = product
+                product = product + part_sums[n, place]
+            part_sums[n, place] = product
 
     def add_products(c):
         def step(g, carry):
@@ -422,7 +460,7 @@
                 products(c, g * 4 + m)
             return carry
 
-        lax.fori_loop(0, SITES // 4, step, 0)
+        lax.fori_loop(0, FINE // 4, step, 0)
 
     def finish():
         sub = lax.broadcasted_iota(jnp.int32, (8, ROWS), 0)
@@ -435,20 +473,18 @@
 
         def group(g, carry):
             total = {}
-            for n, pair in enumerate(PAIRS):
-                rows = [
-                    part_sums[n, pl.ds(pl.multiple_of(g * 64, 64) + 8 * m, 8), :]
-                    for m in range(8)
-                ]
+            spots = [spot_s[0, g * 8 + m] & (SITES - 1) for m in range(8)]
+            for n, couple in enumerate(PAIRS):
+                rows = [part_sums[n, spot] for spot in spots]
                 rows = [
                     jnp.where(low4, rows[m], rows[m + 4])
                     + pltpu.roll(jnp.where(low4, rows[m + 4], rows[m]), 4, 0)
                     for m in range(4)
                 ]
                 rows = [merge(rows[m], rows[m + 2], low2, 2) for m in range(2)]
-                total[pair] = merge(rows[0], rows[1], low1, 1) * (1.0 / VECS)
-                if pair[0] == pair[1]:
-                    total[pair] = total[pair] + RIDGE
+                total[couple] = merge(rows[0], rows[1], low1, 1) * (1.0 / VECS)
+                if couple[0] == couple[1]:
+                    total[couple] = total[couple] + RIDGE
             out = solve_rows(total, [total[s, SLOTS] for s in range(SLOTS)])
             for s in range(SLOTS):
                 w_out[s, pl.ds(pl.multiple_of(g * 8, 8), 8), :] = out[s]
@@ -498,13 +534,23 @@
             where = pl.ds((x % 2) * (ROWS // 2) + t * NY, NY)
             meta[x // 2 : x // 2 + 1, where] = listed[t : t + 1]
         meta[2:3, pl.ds(x * NY, NY)] = cells[0][x]
-    wanted, targets, rank, ids = lists_of(meta[...], at)
-    idv[...] = ids
-    id_copy = pltpu.make_async_copy(idv, id_s, smem_sem.at[0])
-    id_copy.start()
-    for n, row in enumerate((*wanted, rank)):
-        pair[core, n] = row
-    pair_copy().start()
+    blocks, targets, rank, ids, fine_ids, fine_rank = lists_of(meta[...], at)
+    near[at["y"] * CORES + core] = jnp.broadcast_to(rank, (8, ROWS))
+    for copy in gather_copies(0):
+        copy.start()
+    for p in range(2):
+        block_cols[p] = jnp.broadcast_to(blocks[p], (ROWS, ROWS))
+    idv[:COARSE] = ids
+    idv[COARSE : COARSE + FINE] = fine_ids
+    idv[COARSE + FINE :] = jnp.broadcast_to(fine_rank, (8, ROWS))
+    part_sums[:, FINE] = jnp.zeros((len(PAIRS), 8, ROWS), F32)
+    id_copies = [
+        pltpu.make_async_copy(idv.at[pl.ds(0, COARSE)], id_s, smem_sem.at[0]),
+        pltpu.make_async_copy(idv.at[pl.ds(COARSE, FINE)], fine_s, smem_sem.at[2]),
+        pltpu.make_async_copy(idv.at[pl.ds(COARSE + FINE, 8)], spot_s, smem_sem.at[4]),
+    ]
+    for copy in id_copies:
+        copy.start()
     tgt[...] = jnp.zeros_like(tgt)
     for c in range(CHUNKS):
         for h in range(2):
@@ -513,42 +559,27 @@
     tgt_copy = pltpu.make_async_copy(tgt, tgt_s, smem_sem.at[3])
     tgt_copy.start()
 
-    for c in range(CHUNKS):
-        fill_halo(0, c, wa)
-        sweep(c, wa, wb, False)
-        send_faces(1, c, wb)
-    pair_copy().wait_recv()
-    for copy in line_copies():
-        copy.start()
-    for n, axis in enumerate(AXES):
-        lines[n, at[axis]] = pair[...]
-    for c in range(CHUNKS):
-        fill_halo(1, c, wb)
-        sweep(c, wb, wa, False)
-        send_faces(2, c, wa)
-    drain(lines.at[:, pl.ds(0, 3)], table_sem.at[0, 1])
-    for copy in rank_copies():
-        copy.start()
-    for c, (a, u, v) in enumerate(ROUTES):
-        ranks[c, at[v]] = lines[AXES.index(u), :, core, 2]
+    for s in range(SWEEPS):
+        src, dst = (wb, wa) if s % 2 else (wa, wb)
+        for c in range(CHUNKS):
+            fill_halo(s, c, src)
+            sweep(c, src, dst, s == SWEEPS - 1)
+            if s < SWEEPS - 1:
+                send_faces(s + 1, c, dst)
+            else:
+                if c == 0:
+                    for copy in id_copies:
+                        copy.wait()
+                spread(c)
+            if (s, c) in steps:
+                steps[s, c]()
+    drain(lines.at[:, pl.ds(0, 3)], table_sem.at[1])
     line_copy = pltpu.make_async_copy(lines, line_s, smem_sem.at[1])
     line_copy.start()
-    id_copy.wait()
-    for c in range(CHUNKS):
-        fill_halo(2, c, wa)
-        sweep(c, wa, wb, True)
-        spread(c)
-    drain(ranks.at[:, pl.ds(0, 3)], table_sem.at[1, 1])
-    rank_copy = pltpu.make_async_copy(ranks, rank_s, smem_sem.at[2])
-    rank_copy.start()
     cast(0)
     cast(1)
+    cast(2)
     line_copy.wait()
-    rank_copy.wait()
-    find_tiles(1)
-    cast(2)
-    find_tiles(0)
-    find_tiles(2)
     for c in range(CHUNKS):
         pass_on(c)
     for c in (1, 2, 0):
@@ -569,8 +600,9 @@
     drain(fxs, send_sem.at[0])
     drain(fys, send_sem.at[1])
     pair_copy().wait_send()
-    drain(lines.at[:, pl.ds(0, 3)], table_sem.at[0, 0])
-    drain(ranks.at[:, pl.ds(0, 3)], table_sem.at[1, 0])
+    drain(lines.at[:, pl.ds(0, 3)], table_sem.at[0])
+    for step in range(3):
+        drain(gathered(step), gather_sem.at[step, 0])
     for c in range(CHUNKS):
         drain(pg[c][0].at[pl.ds(0, 3)], near_sem.at[c, 0])
         for n in range(3):
@@ -607,7 +639,7 @@
             pltpu.SMEM((8, ROWS), jnp.int32),
             pltpu.VMEM((CHUNKS, SITES, KV, ROWS), BF16),
             *([pltpu.VMEM((EMPTY + 8, KV, ROWS), BF16)] * CHUNKS),
-            pltpu.VMEM((len(PAIRS), SITES * 8, ROWS), F32),
+            pltpu.VMEM((len(PAIRS), SITES, 8, ROWS), F32),
             pltpu.VMEM((VECS, NX, NY, ROWS), F32),
             pltpu.VMEM((4, NX, NY, ROWS), F32),
             pltpu.VMEM((CHUNKS, EXT, ROWS), F32),
@@ -617,14 +649,16 @@
             pltpu.VMEM((SWEEPS, CHUNKS, 2, NY * KV, ROWS), BF16),
             pltpu.VMEM((SWEEPS, CHUNKS, 2, NX * KV, ROWS), BF16),
             pltpu.VMEM((SWEEPS, CHUNKS, 2, NX * KV, ROWS), BF16),
-            pltpu.VMEM((CORES, 3, 1, ROWS), jnp.int32),
-            pltpu.VMEM((len(AXES), LINE, CORES, 3, 1, ROWS), jnp.int32),
-            pltpu.VMEM((CHUNKS, LINE, LINE, 1, ROWS), jnp.int32),
-            pltpu.VMEM((COARSE, ROWS), jnp.int32),
-            pltpu.SMEM((len(AXES), LINE, CORES, 3, 1, ROWS), jnp.int32),
-            pltpu.SMEM((CHUNKS, LINE, LINE, 1, ROWS), jnp.int32),
+            pltpu.VMEM((CORES, 2, 1, ROWS), jnp.int32),
+            pltpu.VMEM((len(AXES), LINE, CORES, 2, 1, ROWS), jnp.int32),
+            pltpu.VMEM((LINE * CORES, 8, ROWS), jnp.int32),
+            pltpu.VMEM((LINE, LINE, LINE * CORES, ROWS), jnp.int32),
+            pltpu.VMEM((2, ROWS, ROWS), jnp.int32),
+            pltpu.VMEM((COARSE + FINE + 8, ROWS), jnp.int32),
+            pltpu.SMEM((len(AXES), LINE, CORES, 2, 1, ROWS), jnp.int32),
             pltpu.SMEM((COARSE, ROWS), jnp.int32),
-            pltpu.SMEM((CHUNKS, LINE * CORES, REPLY), jnp.int32),
+            pltpu.SMEM((FINE, ROWS), jnp.int32),
+            pltpu.SMEM((8, ROWS), jnp.int32),
             *([rows] * (LINE * CHUNKS)),
             pltpu.VMEM((CHUNKS, EMPTY, KV, ROWS), BF16),
             pltpu.VMEM((CHUNKS, CORES, REPLY, KV, ROWS), BF16),
@@ -634,7 +668,8 @@
             dma((2,)),
             dma((SWEEPS, CHUNKS, 2)),
             dma((2,)),
-            dma((2, 2)),
+            dma((2,)),
+            dma((3, 2)),
             dma((CHUNKS, 2)),
             dma((CHUNKS, 3)),
             dma((CHUNKS, 4)),
@@ -643,7 +678,7 @@
             dma((CHUNKS, CORES)),
             dma((CHUNKS,)),
             dma((CHUNKS, len(PARTS))),
-            dma((4,)),
+            dma((5,)),
             dma((4,)),
         ],
         compiler_params=pltpu.CompilerParams(

time: 59.8 us -> 59.6 us (level)
  no operation moved by 1% of the time
where the time goes in v11:
time: 59.6 us; the launch traced here: 59.4 us
  Pallas kernels  58.8 us (99%)
  between operations  0.64 us (1%)
    pallas_call x1, Pallas kernels, smooth(): pl.pallas_call(smooth_kernel, out_shape=(jax.ShapeDtypeStruct((VECS, NX,...  56.5 us
    pallas_call x1, Pallas kernels, pass_on_results(): pl.pallas_call(pass_kernel, out_shape=(jax.ShapeDtypeStruct(weights.shape...  2.32 us

profile of v11, /device:TPU:1, one launch (start us, length us, event | category | flops | bytes accessed | tf_op | source)
XLA Modules:
  0.0 59.4 jit_solution(12683365022008949838)
XLA Ops:
  0.6 56.5 %smooth.1 = (f32[48,4,16,128]{3,2,1,0:T(8,128)}, f32[4,64,128]{2,1,0:T(8,128)}) custom-call(f32[48,4,16,128]{3,2,1,0:T(8,128)} %tv.1, f32[4,16,128]{2,1,0:T(8,128)} %cx.1, f32[4,16,128]{2,1,0:T(8,128)} %cy.1, f32[4,16,128]{2,1,0:T(8,128)} %cz.1, f32[4,16,128]{2,1,0:T(8,128)} %sh.1, s32[4,1,16]{2,1,0:T(1,128)} %bitcast.20, s32[4,1,16]{2,1,0:T(1,128)} %bitcast.21, ...), custom_call_target="tpu_custom_call" | custom-call | tf_op jit(solution)/shard_map/smooth/pallas_call | solution.py:624
  57.1 2.3 %fit.1 = (f32[4,4,16,128]{3,2,1,0:T(8,128)}, f32[48,4,16,128]{3,2,1,0:T(8,128)}) custom-call(f32[4,4,16,128]{3,2,1,0:T(8,128)} %bitcast.17, f32[48,4,16,128]{3,2,1,0:T(8,128)} %get-tuple-element.7.sm_in), custom_call_target="tpu_custom_call" | custom-call | tf_op jit(solution)/shard_map/fit/pallas_call | solution.py:710

commit v12 on v11

--- a/solution.py
+++ b/solution.py
@@ -64,6 +64,7 @@
 CORES = 2
 COARSE = 16
 FINE = 48
+PIECES = 6
 PLANE = LINE * LINE
 ROUTES = (("x", "z", "y"), ("y", "x", "z"), ("z", "y", "x"))
 BACKS = (0, 1, 3, 2)
@@ -328,12 +329,14 @@
 
     def spread_copies(c):
         a, u, v = ROUTES[c]
+        half = COARSE // 2
+        plan = ((0, 0, COARSE, 3, 1, 0), (0, 0, COARSE, 1, 3, 1), (3, 0, half, 2, 1, 2), (1, half, half, 2, 3, 2))
         return [
             remote(
-                pg[c][0].at[0], pg[c][0].at[LINE - d],
-                near_sem.at[c, 0], near_sem.at[c, 1], device(u, d, 0),
+                pg[c][0].at[src, pl.ds(first, size)], pg[c][0].at[dst, pl.ds(first, size)],
+                near_sem.at[c, 3], near_sem.at[c, into], device(u, d, 0),
             )
-            for d in (2, 1, 3)
+            for src, first, size, dst, d, into in plan
         ]
 
     def cast_copies(c):
@@ -368,9 +371,9 @@
         dst, peer = rb[c].at[piece(here, part)], device(a, d, e)
         if d == 0 and e == 0:
             return pltpu.make_async_copy(src, dst, own_sem.at[c, part])
-        if d == 2 and part == 0:
+        if d == 2:
             dst, peer = fb.at[c, e, piece(0, part)], device(a, 1 + 2 * e, 0)
-            return remote(src, dst, ans_send.at[c, part], hop_recv.at[c, e], peer)
+            return remote(src, dst, ans_send.at[c, part], hop_recv.at[c, part, e], peer)
         return remote(src, dst, ans_send.at[c, part], ans_recv.at[c, part], peer)
 
     def forward(c, part, e):
@@ -378,7 +381,7 @@
         origin = lax.rem(at[a] + 3 - 2 * e, LINE) * CORES + core
         return remote(
             fb.at[c, e, piece(0, part)], rb[c].at[piece(origin, part)],
-            fwd_send.at[c], ans_recv.at[c, part], device(a, 1 + 2 * e, e),
+            fwd_send.at[c, part], ans_recv.at[c, part], device(a, 1 + 2 * e, e),
         )
 
     order = [(d, e) for d in (2, 1, 3, 0) for e in range(CORES)]
@@ -387,11 +390,16 @@
         a, u, v = ROUTES[c]
         for r in range(COARSE):
             pg[c][0][0, r] = blk[c, id_s[r, 0] & (SITES - 1)]
-        for copy in spread_copies(c) + cast_copies(c)[:2]:
+        for copy in spread_copies(c)[:2] + cast_copies(c)[:2]:
             copy.start()
 
+    def spread_on(c):
+        for n in range(2):
+            drain(pg[c][0].at[0], near_sem.at[c, n])
+            spread_copies(c)[2 + n].start()
+
     def cast(c):
-        drain(pg[c][1].at[pl.ds(0, 3)], near_sem.at[c, 1])
+        drain(pg[c][0].at[0], near_sem.at[c, 2])
         for copy in cast_copies(c)[2:6]:
             copy.start()
 
@@ -571,12 +579,15 @@
                     for copy in id_copies:
                         copy.wait()
                 spread(c)
+                if c > 0:
+                    spread_on(c - 1)
             if (s, c) in steps:
                 steps[s, c]()
     drain(lines.at[:, pl.ds(0, 3)], table_sem.at[1])
     line_copy = pltpu.make_async_copy(lines, line_s, smem_sem.at[1])
     line_copy.start()
     cast(0)
+    spread_on(2)
     cast(1)
     cast(2)
     line_copy.wait()
@@ -587,8 +598,11 @@
     for c in (1, 0, 2):
         reply_on(c, 0)
         reply(c, 1)
-    for c in range(CHUNKS):
-        transpose_out(c, wb)
+    transpose_out(0, wb)
+    for c in (1, 0, 2):
+        reply_on(c, 1)
+    transpose_out(1, wb)
+    transpose_out(2, wb)
     tgt_copy.wait()
     for c in GRAM_ORDER:
         for part in range(len(PARTS)):
@@ -604,13 +618,13 @@
     for step in range(3):
         drain(gathered(step), gather_sem.at[step, 0])
     for c in range(CHUNKS):
-        drain(pg[c][0].at[pl.ds(0, 3)], near_sem.at[c, 0])
+        drain(pg[c][0].at[pl.ds(0, 3)], near_sem.at[c, 3])
         for n in range(3):
             drain(pg[c][0], cast_send.at[c, n])
         for part in range(len(PARTS)):
             count = PARTS[part][1]
             drain(sb.at[c, pl.ds(0, 7 * count * SPOT)], ans_send.at[c, part])
-        drain(fb.at[c, :, pl.ds(0, PARTS[0][1] * SPOT)], fwd_send.at[c])
+            drain(fb.at[c, :, pl.ds(0, count * SPOT)], fwd_send.at[c, part])
     for store in stores:
         store.wait()
 
@@ -670,13 +684,13 @@
             dma((2,)),
             dma((2,)),
             dma((3, 2)),
-            dma((CHUNKS, 2)),
+            dma((CHUNKS, 4)),
             dma((CHUNKS, 3)),
             dma((CHUNKS, 4)),
             dma((CHUNKS, len(PARTS))),
             dma((CHUNKS, len(PARTS))),
-            dma((CHUNKS, CORES)),
-            dma((CHUNKS,)),
+            dma((CHUNKS, len(PARTS), CORES)),
+            dma((CHUNKS, len(PARTS))),
             dma((CHUNKS, len(PARTS))),
             dma((5,)),
             dma((4,)),
@@ -690,8 +704,8 @@
 
 def pass_kernel(w_in, sm_in, w_out, sm_out, w_hold, sm_hold, in_sem, out_sem):
     parts = [(w_in, w_hold, w_out)]
-    for c in range(CHUNKS):
-        part = pl.ds(c * KV, KV)
+    for c in range(PIECES):
+        part = pl.ds(c * (VECS // PIECES), VECS // PIECES)
         parts.append((sm_in.at[part], sm_hold.at[part], sm_out.at[part]))
     ins = [pltpu.make_async_copy(a, b, in_sem.at[n]) for n, (a, b, _) in enumerate(parts)]
     outs = [pltpu.make_async_copy(b, d, out_sem.at[n]) for n, (_, b, d) in enumerate(parts)]
@@ -718,8 +732,8 @@
         scratch_shapes=[
             pltpu.VMEM(weights.shape, F32),
             pltpu.VMEM(sm.shape, F32),
-            dma((CHUNKS + 1,)),
-            dma((CHUNKS + 1,)),
+            dma((PIECES + 1,)),
+            dma((PIECES + 1,)),
         ],
         compiler_params=pltpu.CompilerParams(vmem_limit_bytes=60 * 1024 * 1024),
         name="fit",

time: 59.6 us -> 67.9 us (1.14)
  Pallas kernels: 58.8 us -> 67.1 us
    pallas_call x1, Pallas kernels: 56.5 us -> 64.8 us  [smooth(): pl.pallas_call(smooth_kernel, out_shape=(jax.ShapeDtypeStruct((VECS, NX,...]
where the time goes in v12:
time: 67.9 us; the launch traced here: 67.7 us
  Pallas kernels  67.1 us (99%)
    pallas_call x1, Pallas kernels, smooth(): pl.pallas_call(smooth_kernel, out_shape=(jax.ShapeDtypeStruct((VECS, NX,...  64.8 us
    pallas_call x1, Pallas kernels, pass_on_results(): pl.pallas_call(pass_kernel, out_shape=(jax.ShapeDtypeStruct(weights.shape...  2.28 us

profile of v12, /device:TPU:1, one launch (start us, length us, event | category | flops | bytes accessed | tf_op | source)
XLA Modules:
  0.0 67.7 jit_solution(579589190804110695)
XLA Ops:
  0.6 64.8 %smooth.1 = (f32[48,4,16,128]{3,2,1,0:T(8,128)}, f32[4,64,128]{2,1,0:T(8,128)}) custom-call(f32[48,4,16,128]{3,2,1,0:T(8,128)} %tv.1, f32[4,16,128]{2,1,0:T(8,128)} %cx.1, f32[4,16,128]{2,1,0:T(8,128)} %cy.1, f32[4,16,128]{2,1,0:T(8,128)} %cz.1, f32[4,16,128]{2,1,0:T(8,128)} %sh.1, s32[4,1,16]{2,1,0:T(1,128)} %bitcast.20, s32[4,1,16]{2,1,0:T(1,128)} %bitcast.21, ...), custom_call_target="tpu_custom_call" | custom-call | tf_op jit(solution)/shard_map/smooth/pallas_call | solution.py:638
  65.4 2.3 %fit.1 = (f32[4,4,16,128]{3,2,1,0:T(8,128)}, f32[48,4,16,128]{3,2,1,0:T(8,128)}) custom-call(f32[4,4,16,128]{3,2,1,0:T(8,128)} %bitcast.17, f32[48,4,16,128]{3,2,1,0:T(8,128)} %get-tuple-element.7.sm_in), custom_call_target="tpu_custom_call" | custom-call | tf_op jit(solution)/shard_map/fit/pallas_call | solution.py:724

commit v13 on v11

--- a/solution.py
+++ b/solution.py
@@ -135,9 +135,9 @@
     tv, cx, cy, cz, sh, split, count, owner, local, sm_out, w_out,
     split_v, count_v, owner_v, local_v, meta, tgt, tgt_s, blk, rb0, rb1, rb2, part_sums,
     stage, coef, wa, wb, ka, kb, km, kp, fxs, fxr, fys, fyr,
-    pair, lines, near, far, block_cols, idv, line_s, id_s, fine_s, spot_s, p00, p01, p02, p03, p10, p11, p12, p13, p20, p21, p22, p23, sb, fb,
+    pair, lines, near, far, block_cols, idv, line_s, id_s, fine_s, spot_s, p00, p01, p02, p03, p10, p11, p12, p13, p20, p21, p22, p23, sb,
     in_sem, coef_sem, out_sem, send_sem, recv_sem, pair_sem, table_sem, gather_sem,
-    near_sem, cast_send, cast_recv, ans_send, ans_recv, hop_recv, fwd_send, own_sem, smem_sem, list_sem,
+    near_sem, cast_send, cast_recv, ans_send, ans_recv, own_sem, smem_sem, list_sem,
 ):
     cells = (split_v, count_v, owner_v, local_v)
     rb = (rb0, rb1, rb2)
@@ -368,18 +368,7 @@
         dst, peer = rb[c].at[piece(here, part)], device(a, d, e)
         if d == 0 and e == 0:
             return pltpu.make_async_copy(src, dst, own_sem.at[c, part])
-        if d == 2 and part == 0:
-            dst, peer = fb.at[c, e, piece(0, part)], device(a, 1 + 2 * e, 0)
-            return remote(src, dst, ans_send.at[c, part], hop_recv.at[c, e], peer)
         return remote(src, dst, ans_send.at[c, part], ans_recv.at[c, part], peer)
-
-    def forward(c, part, e):
-        a = ROUTES[c][0]
-        origin = lax.rem(at[a] + 3 - 2 * e, LINE) * CORES + core
-        return remote(
-            fb.at[c, e, piece(0, part)], rb[c].at[piece(origin, part)],
-            fwd_send.at[c], ans_recv.at[c, part], device(a, 1 + 2 * e, e),
-        )
 
     order = [(d, e) for d in (2, 1, 3, 0) for e in range(CORES)]
 
@@ -424,11 +413,6 @@
                 for t, tile in enumerate(tiles):
                     sb[c, slot * REPLY + place * SPOT + t] = tile
             answer(c, part, d, e).start()
-
-    def reply_on(c, part):
-        for e in range(2):
-            answer(c, part, 2, e).wait_recv()
-            forward(c, part, e).start()
 
     def transpose_in(c):
         loads[c].wait()
@@ -585,7 +569,6 @@
     for c in (1, 2, 0):
         reply(c, 0)
     for c in (1, 0, 2):
-        reply_on(c, 0)
         reply(c, 1)
     for c in range(CHUNKS):
         transpose_out(c, wb)
@@ -610,7 +593,6 @@
         for part in range(len(PARTS)):
             count = PARTS[part][1]
             drain(sb.at[c, pl.ds(0, 7 * count * SPOT)], ans_send.at[c, part])
-        drain(fb.at[c, :, pl.ds(0, PARTS[0][1] * SPOT)], fwd_send.at[c])
     for store in stores:
         store.wait()
 
@@ -661,7 +643,6 @@
             pltpu.SMEM((8, ROWS), jnp.int32),
             *([rows] * (LINE * CHUNKS)),
             pltpu.VMEM((CHUNKS, EMPTY, KV, ROWS), BF16),
-            pltpu.VMEM((CHUNKS, CORES, REPLY, KV, ROWS), BF16),
             dma((CHUNKS,)),
             dma((4,)),
             dma((CHUNKS,)),
@@ -675,8 +656,6 @@
             dma((CHUNKS, 4)),
             dma((CHUNKS, len(PARTS))),
             dma((CHUNKS, len(PARTS))),
-            dma((CHUNKS, CORES)),
-            dma((CHUNKS,)),
             dma((CHUNKS, len(PARTS))),
             dma((5,)),
             dma((4,)),

time: 59.6 us -> 59.5 us (level)
  no operation moved by 1% of the time
where the time goes in v13:
time: 59.5 us; the launch traced here: 59.4 us
  Pallas kernels  58.7 us (99%)
  between operations  0.64 us (1%)
    pallas_call x1, Pallas kernels, smooth(): pl.pallas_call(smooth_kernel, out_shape=(jax.ShapeDtypeStruct((VECS, NX,...  56.4 us
    pallas_call x1, Pallas kernels, pass_on_results(): pl.pallas_call(pass_kernel, out_shape=(jax.ShapeDtypeStruct(weights.shape...  2.32 us

profile of v13, /device:TPU:1, one launch (start us, length us, event | category | flops | bytes accessed | tf_op | source)
XLA Modules:
  0.0 59.4 jit_solution(255535428126788832)
XLA Ops:
  0.6 56.4 %smooth.1 = (f32[48,4,16,128]{3,2,1,0:T(8,128)}, f32[4,64,128]{2,1,0:T(8,128)}) custom-call(f32[48,4,16,128]{3,2,1,0:T(8,128)} %tv.1, f32[4,16,128]{2,1,0:T(8,128)} %cx.1, f32[4,16,128]{2,1,0:T(8,128)} %cy.1, f32[4,16,128]{2,1,0:T(8,128)} %cz.1, f32[4,16,128]{2,1,0:T(8,128)} %sh.1, s32[4,1,16]{2,1,0:T(1,128)} %bitcast.20, s32[4,1,16]{2,1,0:T(1,128)} %bitcast.21, ...), custom_call_target="tpu_custom_call" | custom-call | tf_op jit(solution)/shard_map/smooth/pallas_call | solution.py:606
  57.1 2.3 %fit.1 = (f32[4,4,16,128]{3,2,1,0:T(8,128)}, f32[48,4,16,128]{3,2,1,0:T(8,128)}) custom-call(f32[4,4,16,128]{3,2,1,0:T(8,128)} %bitcast.17, f32[48,4,16,128]{3,2,1,0:T(8,128)} %get-tuple-element.7.sm_in), custom_call_target="tpu_custom_call" | custom-call | tf_op jit(solution)/shard_map/fit/pallas_call | solution.py:689

commit v14 on v13

--- a/solution.py
+++ b/solution.py
@@ -336,24 +336,15 @@
             for d in (2, 1, 3)
         ]
 
-    def cast_copies(c):
+    def cast_copies(c, first, size):
         a, u, v = ROUTES[c]
-        plan = (
-            (0, 0, 1, 3, 1, 0, 0),
-            (0, 0, 1, 1, 3, 1, 2),
-            (0, 1, 1, 3, 1, 0, 0),
-            (0, 2, 2, 1, 3, 1, 1),
-            (0, 2, 2, 3, 1, 0, 2),
-            (0, 1, 1, 1, 3, 1, 2),
-            (3, 0, 2, 2, 1, 2, 3),
-            (1, 2, 2, 2, 3, 2, 3),
-        )
+        shards = pl.ds(first, size)
         return [
             remote(
-                pg[c][src].at[pl.ds(first, size)], pg[c][dst].at[pl.ds(first, size)],
-                cast_send.at[c, out], cast_recv.at[c, into], device(v, d, 0),
+                pg[c][0].at[shards], pg[c][LINE - d].at[shards],
+                cast_send.at[c, d - 1], cast_recv.at[c, LINE - d], device(v, d, 0),
             )
-            for src, first, size, dst, d, out, into in plan
+            for d in (2, 1, 3)
         ]
 
     def piece(slot, part):
@@ -376,23 +367,19 @@
         a, u, v = ROUTES[c]
         for r in range(COARSE):
             pg[c][0][0, r] = blk[c, id_s[r, 0] & (SITES - 1)]
-        for copy in spread_copies(c) + cast_copies(c)[:2]:
+        for copy in spread_copies(c) + cast_copies(c, 0, 1):
             copy.start()
 
     def cast(c):
         drain(pg[c][1].at[pl.ds(0, 3)], near_sem.at[c, 1])
-        for copy in cast_copies(c)[2:6]:
+        for copy in cast_copies(c, 1, LINE - 1):
             copy.start()
-
-    def pass_on(c):
-        for n in range(2):
-            drain(pg[c][0].at[pl.ds(0, 2)], cast_recv.at[c, n])
-            cast_copies(c)[6 + n].start()
 
     def reply(c, part):
         a, u, v = ROUTES[c]
         n = AXES.index(a)
-        drain(pg[c][0], cast_recv.at[c, 2 + part])
+        for back in ((1, 3), (2,))[part]:
+            drain(pg[c][0], cast_recv.at[c, back])
         first, count = PARTS[part]
         for d, e in order:
             q, to = lax.rem(at[a] + d, LINE), lax.rem(core + e, CORES)
@@ -564,8 +551,6 @@
     cast(1)
     cast(2)
     line_copy.wait()
-    for c in range(CHUNKS):
-        pass_on(c)
     for c in (1, 2, 0):
         reply(c, 0)
     for c in (1, 0, 2):
@@ -653,7 +638,7 @@
             dma((3, 2)),
             dma((CHUNKS, 2)),
             dma((CHUNKS, 3)),
-            dma((CHUNKS, 4)),
+            dma((CHUNKS, LINE)),
             dma((CHUNKS, len(PARTS))),
             dma((CHUNKS, len(PARTS))),
             dma((CHUNKS, len(PARTS))),

time: 59.5 us -> 65.4 us (1.099)
  Pallas kernels: 58.7 us -> 64.6 us
    pallas_call x1, Pallas kernels: 56.4 us -> 62.3 us  [smooth(): pl.pallas_call(smooth_kernel, out_shape=(jax.ShapeDtypeStruct((VECS, NX,...]
where the time goes in v14:
time: 65.4 us; the launch traced here: 65.2 us
  Pallas kernels  64.6 us (99%)
    pallas_call x1, Pallas kernels, smooth(): pl.pallas_call(smooth_kernel, out_shape=(jax.ShapeDtypeStruct((VECS, NX,...  62.3 us
    pallas_call x1, Pallas kernels, pass_on_results(): pl.pallas_call(pass_kernel, out_shape=(jax.ShapeDtypeStruct(weights.shape...  2.32 us

profile of v14, /device:TPU:1, one launch (start us, length us, event | category | flops | bytes accessed | tf_op | source)
XLA Modules:
  0.0 65.2 jit_solution(10630659032781539711)
XLA Ops:
  0.6 62.3 %smooth.1 = (f32[48,4,16,128]{3,2,1,0:T(8,128)}, f32[4,64,128]{2,1,0:T(8,128)}) custom-call(f32[48,4,16,128]{3,2,1,0:T(8,128)} %tv.1, f32[4,16,128]{2,1,0:T(8,128)} %cx.1, f32[4,16,128]{2,1,0:T(8,128)} %cy.1, f32[4,16,128]{2,1,0:T(8,128)} %cz.1, f32[4,16,128]{2,1,0:T(8,128)} %sh.1, s32[4,1,16]{2,1,0:T(1,128)} %bitcast.20, s32[4,1,16]{2,1,0:T(1,128)} %bitcast.21, ...), custom_call_target="tpu_custom_call" | custom-call | tf_op jit(solution)/shard_map/smooth/pallas_call | solution.py:591
  62.9 2.3 %fit.1 = (f32[4,4,16,128]{3,2,1,0:T(8,128)}, f32[48,4,16,128]{3,2,1,0:T(8,128)}) custom-call(f32[4,4,16,128]{3,2,1,0:T(8,128)} %bitcast.17, f32[48,4,16,128]{3,2,1,0:T(8,128)} %get-tuple-element.7.sm_in), custom_call_target="tpu_custom_call" | custom-call | tf_op jit(solution)/shard_map/fit/pallas_call | solution.py:674

commit v15 on v11

--- a/solution.py
+++ b/solution.py
@@ -400,30 +400,43 @@
             drain(pg[c][0].at[pl.ds(0, 2)], cast_recv.at[c, n])
             cast_copies(c)[6 + n].start()
 
-    def reply(c, part):
+    def pack(c, d, e, places):
         a, u, v = ROUTES[c]
         n = AXES.index(a)
-        drain(pg[c][0], cast_recv.at[c, 2 + part])
-        first, count = PARTS[part]
+        q, to = lax.rem(at[a] + d, LINE), lax.rem(core + e, CORES)
+        slot = q * CORES + to
+        for place in places:
+            back = BACKS[place]
+            tiles = []
+            for ahead in range(LINE):
+                whose = {
+                    a: at[a],
+                    u: lax.rem(at[u] + ahead, LINE),
+                    v: lax.rem(at[v] + back, LINE),
+                }
+                owner = whose["x"] * 32 + whose["z"] * 8 + whose["y"] * 2 + core
+                for p in range(2):
+                    rank = line_s[n, q, to, p, 0, owner] & (COARSE - 1)
+                    tiles.append(pg[c][back][ahead, rank])
+            for t, tile in enumerate(tiles):
+                sb[c, slot * REPLY + place * SPOT + t] = tile
+
+    def pack_own(c):
         for d, e in order:
-            q, to = lax.rem(at[a] + d, LINE), lax.rem(core + e, CORES)
-            slot = q * CORES + to
-            for place in range(first, first + count):
-                back = BACKS[place]
-                tiles = []
-                for ahead in range(LINE):
-                    whose = {
-                        a: at[a],
-                        u: lax.rem(at[u] + ahead, LINE),
-                        v: lax.rem(at[v] + back, LINE),
-                    }
-                    owner = whose["x"] * 32 + whose["z"] * 8 + whose["y"] * 2 + core
-                    for p in range(2):
-                        rank = line_s[n, q, to, p, 0, owner] & (COARSE - 1)
-                        tiles.append(pg[c][back][ahead, rank])
-                for t, tile in enumerate(tiles):
-                    sb[c, slot * REPLY + place * SPOT + t] = tile
-            answer(c, part, d, e).start()
+            pack(c, d, e, (0,))
+
+    def reply(part):
+        for n, group in enumerate(((2,), (1, 3), (0,))):
+            for c in GRAM_ORDER:
+                if n == 0:
+                    drain(pg[c][0], cast_recv.at[c, 2 + part])
+                for d in group:
+                    for e in range(CORES):
+                        pack(c, d, e, (3,) if part else (1, 2))
+                        answer(c, part, d, e).start()
+            if part == 0 and n == 1:
+                for c in GRAM_ORDER:
+                    reply_on(c, 0)
 
     def reply_on(c, part):
         for e in range(2):
@@ -581,12 +594,11 @@
     cast(2)
     line_copy.wait()
     for c in range(CHUNKS):
+        pack_own(c)
+    for c in range(CHUNKS):
         pass_on(c)
-    for c in (1, 2, 0):
-        reply(c, 0)
-    for c in (1, 0, 2):
-        reply_on(c, 0)
-        reply(c, 1)
+    reply(0)
+    reply(1)
     for c in range(CHUNKS):
         transpose_out(c, wb)
     tgt_copy.wait()

time: 59.6 us -> 60.5 us (1.015)
  Pallas kernels: 58.8 us -> 59.7 us
    pallas_call x1, Pallas kernels: 56.5 us -> 57.4 us  [smooth(): pl.pallas_call(smooth_kernel, out_shape=(jax.ShapeDtypeStruct((VECS, NX,...]
where the time goes in v15:
time: 60.5 us; the launch traced here: 60.4 us
  Pallas kernels  59.7 us (99%)
  between operations  0.64 us (1%)
    pallas_call x1, Pallas kernels, smooth(): pl.pallas_call(smooth_kernel, out_shape=(jax.ShapeDtypeStruct((VECS, NX,...  57.4 us
    pallas_call x1, Pallas kernels, pass_on_results(): pl.pallas_call(pass_kernel, out_shape=(jax.ShapeDtypeStruct(weights.shape...  2.32 us

profile of v15, /device:TPU:1, one launch (start us, length us, event | category | flops | bytes accessed | tf_op | source)
XLA Modules:
  0.0 60.4 jit_solution(778964826033676640)
XLA Ops:
  0.6 57.4 %smooth.1 = (f32[48,4,16,128]{3,2,1,0:T(8,128)}, f32[4,64,128]{2,1,0:T(8,128)}) custom-call(f32[48,4,16,128]{3,2,1,0:T(8,128)} %tv.1, f32[4,16,128]{2,1,0:T(8,128)} %cx.1, f32[4,16,128]{2,1,0:T(8,128)} %cy.1, f32[4,16,128]{2,1,0:T(8,128)} %cz.1, f32[4,16,128]{2,1,0:T(8,128)} %sh.1, s32[4,1,16]{2,1,0:T(1,128)} %bitcast.20, s32[4,1,16]{2,1,0:T(1,128)} %bitcast.21, ...), custom_call_target="tpu_custom_call" | custom-call | tf_op jit(solution)/shard_map/smooth/pallas_call | solution.py:636
  58.0 2.3 %fit.1 = (f32[4,4,16,128]{3,2,1,0:T(8,128)}, f32[48,4,16,128]{3,2,1,0:T(8,128)}) custom-call(f32[4,4,16,128]{3,2,1,0:T(8,128)} %bitcast.17, f32[48,4,16,128]{3,2,1,0:T(8,128)} %get-tuple-element.7.sm_in), custom_call_target="tpu_custom_call" | custom-call | tf_op jit(solution)/shard_map/fit/pallas_call | solution.py:722

commit v16 on v15

--- a/solution.py
+++ b/solution.py
@@ -331,9 +331,9 @@
         return [
             remote(
                 pg[c][0].at[0], pg[c][0].at[LINE - d],
-                near_sem.at[c, 0], near_sem.at[c, 1], device(u, d, 0),
+                near_sem.at[c, 2], near_sem.at[c, into], device(u, d, 0),
             )
-            for d in (2, 1, 3)
+            for d, into in ((1, 0), (3, 0), (2, 1))
         ]
 
     def cast_copies(c):
@@ -342,9 +342,11 @@
             (0, 0, 1, 3, 1, 0, 0),
             (0, 0, 1, 1, 3, 1, 2),
             (0, 1, 1, 3, 1, 0, 0),
-            (0, 2, 2, 1, 3, 1, 1),
-            (0, 2, 2, 3, 1, 0, 2),
+            (0, 3, 1, 1, 3, 1, 1),
+            (0, 3, 1, 3, 1, 0, 2),
             (0, 1, 1, 1, 3, 1, 2),
+            (0, 2, 1, 1, 3, 1, 1),
+            (0, 2, 1, 3, 1, 0, 2),
             (3, 0, 2, 2, 1, 2, 3),
             (1, 2, 2, 2, 3, 2, 3),
         )
@@ -390,15 +392,14 @@
         for copy in spread_copies(c) + cast_copies(c)[:2]:
             copy.start()
 
-    def cast(c):
-        drain(pg[c][1].at[pl.ds(0, 3)], near_sem.at[c, 1])
-        for copy in cast_copies(c)[2:6]:
+    def cast(c, late):
+        drain(pg[c][0].at[pl.ds(0, 2 - late)], near_sem.at[c, late])
+        for copy in cast_copies(c)[6:8] if late else cast_copies(c)[2:6]:
             copy.start()
 
-    def pass_on(c):
-        for n in range(2):
-            drain(pg[c][0].at[pl.ds(0, 2)], cast_recv.at[c, n])
-            cast_copies(c)[6 + n].start()
+    def pass_on(c, n):
+        drain(pg[c][0].at[pl.ds(0, 2)], cast_recv.at[c, n])
+        cast_copies(c)[8 + n].start()
 
     def pack(c, d, e, places):
         a, u, v = ROUTES[c]
@@ -589,14 +590,22 @@
     drain(lines.at[:, pl.ds(0, 3)], table_sem.at[1])
     line_copy = pltpu.make_async_copy(lines, line_s, smem_sem.at[1])
     line_copy.start()
-    cast(0)
-    cast(1)
-    cast(2)
+    cast(0, 0)
+    cast(1, 0)
+    cast(0, 1)
+    cast(2, 0)
+    pass_on(0, 0)
+    cast(1, 1)
+    pass_on(1, 0)
+    cast(2, 1)
     line_copy.wait()
-    for c in range(CHUNKS):
-        pack_own(c)
-    for c in range(CHUNKS):
-        pass_on(c)
+    pack_own(0)
+    pass_on(0, 1)
+    pass_on(2, 0)
+    pack_own(1)
+    pass_on(1, 1)
+    pack_own(2)
+    pass_on(2, 1)
     reply(0)
     reply(1)
     for c in range(CHUNKS):
@@ -616,7 +625,7 @@
     for step in range(3):
         drain(gathered(step), gather_sem.at[step, 0])
     for c in range(CHUNKS):
-        drain(pg[c][0].at[pl.ds(0, 3)], near_sem.at[c, 0])
+        drain(pg[c][0].at[pl.ds(0, 3)], near_sem.at[c, 2])
         for n in range(3):
             drain(pg[c][0], cast_send.at[c, n])
         for part in range(len(PARTS)):
@@ -682,7 +691,7 @@
             dma((2,)),
             dma((2,)),
             dma((3, 2)),
-            dma((CHUNKS, 2)),
+            dma((CHUNKS, 3)),
             dma((CHUNKS, 3)),
             dma((CHUNKS, 4)),
             dma((CHUNKS, len(PARTS))),

time: 60.5 us -> 60.8 us (level)
  no operation moved by 1% of the time
where the time goes in v16:
time: 60.8 us; the launch traced here: 60.6 us
  Pallas kernels  60 us (99%)
  between operations  0.64 us (1%)
    pallas_call x1, Pallas kernels, smooth(): pl.pallas_call(smooth_kernel, out_shape=(jax.ShapeDtypeStruct((VECS, NX,...  57.7 us
    pallas_call x1, Pallas kernels, pass_on_results(): pl.pallas_call(pass_kernel, out_shape=(jax.ShapeDtypeStruct(weights.shape...  2.32 us

profile of v16, /device:TPU:1, one launch (start us, length us, event | category | flops | bytes accessed | tf_op | source)
XLA Modules:
  0.0 60.6 jit_solution(1799636969642836995)
XLA Ops:
  0.6 57.7 %smooth.1 = (f32[48,4,16,128]{3,2,1,0:T(8,128)}, f32[4,64,128]{2,1,0:T(8,128)}) custom-call(f32[48,4,16,128]{3,2,1,0:T(8,128)} %tv.1, f32[4,16,128]{2,1,0:T(8,128)} %cx.1, f32[4,16,128]{2,1,0:T(8,128)} %cy.1, f32[4,16,128]{2,1,0:T(8,128)} %cz.1, f32[4,16,128]{2,1,0:T(8,128)} %sh.1, s32[4,1,16]{2,1,0:T(1,128)} %bitcast.20, s32[4,1,16]{2,1,0:T(1,128)} %bitcast.21, ...), custom_call_target="tpu_custom_call" | custom-call | tf_op jit(solution)/shard_map/smooth/pallas_call | solution.py:645
  58.3 2.3 %fit.1 = (f32[4,4,16,128]{3,2,1,0:T(8,128)}, f32[48,4,16,128]{3,2,1,0:T(8,128)}) custom-call(f32[4,4,16,128]{3,2,1,0:T(8,128)} %bitcast.17, f32[48,4,16,128]{3,2,1,0:T(8,128)} %get-tuple-element.7.sm_in), custom_call_target="tpu_custom_call" | custom-call | tf_op jit(solution)/shard_map/fit/pallas_call | solution.py:731

commit v17 on v15

--- a/solution.py
+++ b/solution.py
@@ -69,9 +69,9 @@
 BACKS = (0, 1, 3, 2)
 EMPTY = LINE * CORES * PLANE * 2
 SPOT = 2 * LINE
-GRAM_ORDER = (1, 2, 0)
+GRAM_ORDER = (0, 1, 2)
 REPLY = PLANE * 2
-PARTS = ((0, 3), (3, 1))
+PARTS = ((0, 4),)
 
 
 def lists_of(meta, here):
@@ -135,9 +135,9 @@
     tv, cx, cy, cz, sh, split, count, owner, local, sm_out, w_out,
     split_v, count_v, owner_v, local_v, meta, tgt, tgt_s, blk, rb0, rb1, rb2, part_sums,
     stage, coef, wa, wb, ka, kb, km, kp, fxs, fxr, fys, fyr,
-    pair, lines, near, far, block_cols, idv, line_s, id_s, fine_s, spot_s, p00, p01, p02, p03, p10, p11, p12, p13, p20, p21, p22, p23, sb, fb,
+    pair, lines, near, far, block_cols, idv, line_s, id_s, fine_s, spot_s, p00, p01, p02, p03, p10, p11, p12, p13, p20, p21, p22, p23, sb,
     in_sem, coef_sem, out_sem, send_sem, recv_sem, pair_sem, table_sem, gather_sem,
-    near_sem, cast_send, cast_recv, ans_send, ans_recv, hop_recv, fwd_send, own_sem, smem_sem, list_sem,
+    near_sem, cast_send, cast_recv, ans_send, ans_recv, own_sem, smem_sem, list_sem,
 ):
     cells = (split_v, count_v, owner_v, local_v)
     rb = (rb0, rb1, rb2)
@@ -368,18 +368,7 @@
         dst, peer = rb[c].at[piece(here, part)], device(a, d, e)
         if d == 0 and e == 0:
             return pltpu.make_async_copy(src, dst, own_sem.at[c, part])
-        if d == 2 and part == 0:
-            dst, peer = fb.at[c, e, piece(0, part)], device(a, 1 + 2 * e, 0)
-            return remote(src, dst, ans_send.at[c, part], hop_recv.at[c, e], peer)
         return remote(src, dst, ans_send.at[c, part], ans_recv.at[c, part], peer)
-
-    def forward(c, part, e):
-        a = ROUTES[c][0]
-        origin = lax.rem(at[a] + 3 - 2 * e, LINE) * CORES + core
-        return remote(
-            fb.at[c, e, piece(0, part)], rb[c].at[piece(origin, part)],
-            fwd_send.at[c], ans_recv.at[c, part], device(a, 1 + 2 * e, e),
-        )
 
     order = [(d, e) for d in (2, 1, 3, 0) for e in range(CORES)]
 
@@ -421,27 +410,15 @@
             for t, tile in enumerate(tiles):
                 sb[c, slot * REPLY + place * SPOT + t] = tile
 
-    def pack_own(c):
+    def pack_rows(c, places):
         for d, e in order:
-            pack(c, d, e, (0,))
-
-    def reply(part):
-        for n, group in enumerate(((2,), (1, 3), (0,))):
-            for c in GRAM_ORDER:
-                if n == 0:
-                    drain(pg[c][0], cast_recv.at[c, 2 + part])
-                for d in group:
-                    for e in range(CORES):
-                        pack(c, d, e, (3,) if part else (1, 2))
-                        answer(c, part, d, e).start()
-            if part == 0 and n == 1:
-                for c in GRAM_ORDER:
-                    reply_on(c, 0)
-
-    def reply_on(c, part):
-        for e in range(2):
-            answer(c, part, 2, e).wait_recv()
-            forward(c, part, e).start()
+            pack(c, d, e, places)
+
+    def reply(c):
+        drain(pg[c][0], cast_recv.at[c, 3])
+        for d, e in order:
+            pack(c, d, e, (3,))
+            answer(c, 0, d, e).start()
 
     def transpose_in(c):
         loads[c].wait()
@@ -594,11 +571,14 @@
     cast(2)
     line_copy.wait()
     for c in range(CHUNKS):
-        pack_own(c)
+        pack_rows(c, (0,))
     for c in range(CHUNKS):
         pass_on(c)
-    reply(0)
-    reply(1)
+    for c in GRAM_ORDER:
+        drain(pg[c][0], cast_recv.at[c, 2])
+        pack_rows(c, (1, 2))
+    for c in GRAM_ORDER:
+        reply(c)
     for c in range(CHUNKS):
         transpose_out(c, wb)
     tgt_copy.wait()
@@ -622,7 +602,6 @@
         for part in range(len(PARTS)):
             count = PARTS[part][1]
             drain(sb.at[c, pl.ds(0, 7 * count * SPOT)], ans_send.at[c, part])
-        drain(fb.at[c, :, pl.ds(0, PARTS[0][1] * SPOT)], fwd_send.at[c])
     for store in stores:
         store.wait()
 
@@ -673,7 +652,6 @@
             pltpu.SMEM((8, ROWS), jnp.int32),
             *([rows] * (LINE * CHUNKS)),
             pltpu.VMEM((CHUNKS, EMPTY, KV, ROWS), BF16),
-            pltpu.VMEM((CHUNKS, CORES, REPLY, KV, ROWS), BF16),
             dma((CHUNKS,)),
             dma((4,)),
             dma((CHUNKS,)),
@@ -687,8 +665,6 @@
             dma((CHUNKS, 4)),
             dma((CHUNKS, len(PARTS))),
             dma((CHUNKS, len(PARTS))),
-            dma((CHUNKS, CORES)),
-            dma((CHUNKS,)),
             dma((CHUNKS, len(PARTS))),
             dma((5,)),
             dma((4,)),

time: 60.5 us -> 62 us (1.025)
  Pallas kernels: 59.7 us -> 61.2 us
    pallas_call x1, Pallas kernels: 57.4 us -> 58.8 us  [smooth(): pl.pallas_call(smooth_kernel, out_shape=(jax.ShapeDtypeStruct((VECS, NX,...]
where the time goes in v17:
time: 62 us; the launch traced here: 61.8 us
  Pallas kernels  61.2 us (99%)
  between operations  0.64 us (1%)
    pallas_call x1, Pallas kernels, smooth(): pl.pallas_call(smooth_kernel, out_shape=(jax.ShapeDtypeStruct((VECS, NX,...  58.8 us
    pallas_call x1, Pallas kernels, pass_on_results(): pl.pallas_call(pass_kernel, out_shape=(jax.ShapeDtypeStruct(weights.shape...  2.32 us

profile of v17, /device:TPU:1, one launch (start us, length us, event | category | flops | bytes accessed | tf_op | source)
XLA Modules:
  0.0 61.8 jit_solution(5252758444687143122)
XLA Ops:
  0.6 58.8 %smooth.1 = (f32[48,4,16,128]{3,2,1,0:T(8,128)}, f32[4,64,128]{2,1,0:T(8,128)}) custom-call(f32[48,4,16,128]{3,2,1,0:T(8,128)} %tv.1, f32[4,16,128]{2,1,0:T(8,128)} %cx.1, f32[4,16,128]{2,1,0:T(8,128)} %cy.1, f32[4,16,128]{2,1,0:T(8,128)} %cz.1, f32[4,16,128]{2,1,0:T(8,128)} %sh.1, s32[4,1,16]{2,1,0:T(1,128)} %bitcast.20, s32[4,1,16]{2,1,0:T(1,128)} %bitcast.21, ...), custom_call_target="tpu_custom_call" | custom-call | tf_op jit(solution)/shard_map/smooth/pallas_call | solution.py:615
  59.5 2.3 %fit.1 = (f32[4,4,16,128]{3,2,1,0:T(8,128)}, f32[48,4,16,128]{3,2,1,0:T(8,128)}) custom-call(f32[4,4,16,128]{3,2,1,0:T(8,128)} %bitcast.17, f32[48,4,16,128]{3,2,1,0:T(8,128)} %get-tuple-element.7.sm_in), custom_call_target="tpu_custom_call" | custom-call | tf_op jit(solution)/shard_map/fit/pallas_call | solution.py:698

commit v18 on v17

--- a/solution.py
+++ b/solution.py
@@ -69,9 +69,9 @@
 BACKS = (0, 1, 3, 2)
 EMPTY = LINE * CORES * PLANE * 2
 SPOT = 2 * LINE
-GRAM_ORDER = (0, 1, 2)
+GRAM_ORDER = (1, 2, 0)
 REPLY = PLANE * 2
-PARTS = ((0, 4),)
+PARTS = ((0, 3), (3, 1))
 
 
 def lists_of(meta, here):
@@ -366,7 +366,7 @@
         here = at[a] * CORES + core
         src = sb.at[c, piece(slot, part)]
         dst, peer = rb[c].at[piece(here, part)], device(a, d, e)
-        if d == 0 and e == 0:
+        if isinstance(d, int) and d == 0 and e == 0:
             return pltpu.make_async_copy(src, dst, own_sem.at[c, part])
         return remote(src, dst, ans_send.at[c, part], ans_recv.at[c, part], peer)
 
@@ -410,24 +410,35 @@
             for t, tile in enumerate(tiles):
                 sb[c, slot * REPLY + place * SPOT + t] = tile
 
-    def pack_rows(c, places):
-        for d, e in order:
+    def reply(c, part):
+        drain(pg[c][0], cast_recv.at[c, 2 + part])
+        first, count = PARTS[part]
+        places = range(first, first + count)
+
+        def to_other_chip(n, carry):
+            k, e = n // CORES, lax.rem(n, CORES)
+            d = 2 - k + 3 * (k // 2)
             pack(c, d, e, places)
-
-    def reply(c):
-        drain(pg[c][0], cast_recv.at[c, 3])
-        for d, e in order:
-            pack(c, d, e, (3,))
-            answer(c, 0, d, e).start()
+            answer(c, part, d, e).start()
+            return carry
+
+        lax.fori_loop(0, (LINE - 1) * CORES, to_other_chip, 0)
+        for e in (1, 0):
+            pack(c, 0, e, places)
+            answer(c, part, 0, e).start()
 
     def transpose_in(c):
         loads[c].wait()
-        for x in range(NX):
-            for half in range(NY // 8):
-                for k in range(KV):
+
+        def one(k, carry):
+            for x in range(NX):
+                for half in range(NY // 8):
                     wa[c, pl.ds(site_row(x, half * 8) + k, 8, stride=KV), :] = stage[
                         c * KV + k, x, pl.ds(half * 8, 8), :
                     ]
+            return carry
+
+        lax.fori_loop(0, KV, one, 0)
 
     def products(c, place):
         b = fine_s[place, 0] & (SITES - 1)
@@ -485,12 +496,16 @@
     stores = []
 
     def transpose_out(c, w):
-        for x in range(NX):
-            for half in range(NY // 8):
-                for k in range(KV):
+
+        def one(k, carry):
+            for x in range(NX):
+                for half in range(NY // 8):
                     stage[c * KV + k, x, pl.ds(half * 8, 8), :] = w[
                         c, pl.ds(site_row(x, half * 8) + k, 8, stride=KV), :
                     ]
+            return carry
+
+        lax.fori_loop(0, KV, one, 0)
         part = pl.ds(c * KV, KV)
         store = pltpu.make_async_copy(stage.at[part], sm_out.at[part], out_sem.at[c])
         store.start()
@@ -571,14 +586,11 @@
     cast(2)
     line_copy.wait()
     for c in range(CHUNKS):
-        pack_rows(c, (0,))
-    for c in range(CHUNKS):
         pass_on(c)
-    for c in GRAM_ORDER:
-        drain(pg[c][0], cast_recv.at[c, 2])
-        pack_rows(c, (1, 2))
-    for c in GRAM_ORDER:
-        reply(c)
+    for c in (1, 2, 0):
+        reply(c, 0)
+    for c in (1, 0, 2):
+        reply(c, 1)
     for c in range(CHUNKS):
         transpose_out(c, wb)
     tgt_copy.wait()

time: 62 us -> 59.7 us (0.963)
  Pallas kernels: 61.2 us -> 58.9 us
    pallas_call x1, Pallas kernels: 58.8 us -> 56.6 us  [smooth(): pl.pallas_call(smooth_kernel, out_shape=(jax.ShapeDtypeStruct((VECS, NX,...]
where the time goes in v18:
time: 59.7 us; the launch traced here: 59.5 us
  Pallas kernels  58.9 us (99%)
  between operations  0.64 us (1%)
    pallas_call x1, Pallas kernels, smooth(): pl.pallas_call(smooth_kernel, out_shape=(jax.ShapeDtypeStruct((VECS, NX,...  56.6 us
    pallas_call x1, Pallas kernels, pass_on_results(): pl.pallas_call(pass_kernel, out_shape=(jax.ShapeDtypeStruct(weights.shape...  2.32 us

profile of v18, /device:TPU:1, one launch (start us, length us, event | category | flops | bytes accessed | tf_op | source)
XLA Modules:
  0.0 59.5 jit_solution(4883066121723957441)
XLA Ops:
  0.6 56.6 %smooth.1 = (f32[48,4,16,128]{3,2,1,0:T(8,128)}, f32[4,64,128]{2,1,0:T(8,128)}) custom-call(f32[48,4,16,128]{3,2,1,0:T(8,128)} %tv.1, f32[4,16,128]{2,1,0:T(8,128)} %cx.1, f32[4,16,128]{2,1,0:T(8,128)} %cy.1, f32[4,16,128]{2,1,0:T(8,128)} %cz.1, f32[4,16,128]{2,1,0:T(8,128)} %sh.1, s32[4,1,16]{2,1,0:T(1,128)} %bitcast.20, s32[4,1,16]{2,1,0:T(1,128)} %bitcast.21, ...), custom_call_target="tpu_custom_call" | custom-call | tf_op jit(solution)/shard_map/smooth/pallas_call | solution.py:627
  57.2 2.3 %fit.1 = (f32[4,4,16,128]{3,2,1,0:T(8,128)}, f32[48,4,16,128]{3,2,1,0:T(8,128)}) custom-call(f32[4,4,16,128]{3,2,1,0:T(8,128)} %bitcast.17, f32[48,4,16,128]{3,2,1,0:T(8,128)} %get-tuple-element.7.sm_in), custom_call_target="tpu_custom_call" | custom-call | tf_op jit(solution)/shard_map/fit/pallas_call | solution.py:710

commit v19 on v18

--- a/solution.py
+++ b/solution.py
@@ -237,31 +237,52 @@
                     fyr[s, c, side, pl.ds(x * KV, KV)].astype(F32) * keep[2 + side]
                 )
 
-    def sweep(c, src, dst, last):
-        def plane(x, carry):
+    def sweep(s, c, src, dst):
+        last = s == SWEEPS - 1
+
+        def plane(x, side):
             base = pl.multiple_of(x * XROW, 16)
 
             def cell(dx, y):
-                return src[c, pl.ds(base + site_row(dx, y), KV)]
+                return src[c, pl.ds(base + site_row(dx, y), KV)].reshape(2, 8, ROWS)
 
             below, here = cell(0, -1), cell(0, 0)
             for y in range(NY):
                 above = cell(0, y + 1)
-                row = slice(y, y + 1)
                 new = (
-                    ka[x, row] * (cell(-1, y) + cell(1, y))
-                    + kb[x, row] * (below + above)
-                    + km[x, row] * pltpu.roll(here, 1, 1)
-                    + kp[x, row] * pltpu.roll(here, ROWS - 1, 1)
+                    ka[x, y] * (cell(-1, y) + cell(1, y))
+                    + kb[x, y] * (below + above)
+                    + km[x, y] * pltpu.roll(here, 1, 2)
+                    + kp[x, y] * pltpu.roll(here, ROWS - 1, 2)
                     + (1.0 - OMEGA) * here
-                )
+                ).reshape(KV, ROWS)
                 dst[c, pl.ds(base + site_row(0, y), KV)] = new
                 if last:
                     blk[c, x * NY + y] = new.astype(BF16)
+                else:
+                    if side is not None:
+                        fxs[s + 1, c, side, pl.ds(y * KV, KV)] = new.astype(BF16)
+                    if y in (0, NY - 1):
+                        rows = pl.ds(pl.multiple_of(x * KV, KV), KV)
+                        fys[s + 1, c, y // (NY - 1), rows] = new.astype(BF16)
                 below, here = here, above
+
+        def outer(n, carry):
+            plane(n * (NX - 1), n)
             return carry
 
-        lax.fori_loop(0, NX, plane, 0)
+        def inner(n, carry):
+            plane(n, None)
+            return carry
+
+        lax.fori_loop(0, 2, outer, 0)
+        if not last:
+            for copy in copies(s + 1, c)[:2]:
+                copy.start()
+        lax.fori_loop(1, NX - 1, inner, 0)
+        if not last:
+            for copy in copies(s + 1, c)[2:]:
+                copy.start()
 
     def pair_copy():
         slot = pair.at[core]
@@ -521,12 +542,14 @@
         load.wait()
     ax, ay, az = coef[0], coef[1], coef[2]
     scale = OMEGA / (2.0 * (ax + ay + az) + coef[3])
-    ka[...] = ax * scale
-    kb[...] = ay * scale
-    az = az * scale
+    ax, ay, az = ax * scale, ay * scale, az * scale
     lane = lax.broadcasted_iota(jnp.int32, az.shape, 2)
-    km[...] = jnp.where(lane == 0, 0.0, az)
-    kp[...] = jnp.where(lane == ROWS - 1, 0.0, az)
+    before = jnp.where(lane == 0, 0.0, az)
+    after = jnp.where(lane == ROWS - 1, 0.0, az)
+    for x in range(NX):
+        for y in range(NY):
+            for held, value in ((ka, ax), (kb, ay), (km, before), (kp, after)):
+                held[x, y] = jnp.broadcast_to(value[x, y : y + 1], (8, ROWS))
 
     for load in lists:
         load.wait()
@@ -568,10 +591,8 @@
         src, dst = (wb, wa) if s % 2 else (wa, wb)
         for c in range(CHUNKS):
             fill_halo(s, c, src)
-            sweep(c, src, dst, s == SWEEPS - 1)
-            if s < SWEEPS - 1:
-                send_faces(s + 1, c, dst)
-            else:
+            sweep(s, c, src, dst)
+            if s == SWEEPS - 1:
                 if c == 0:
                     for copy in id_copies:
                         copy.wait()
@@ -621,7 +642,7 @@
 def smooth(test_vectors, coef_x, coef_y, coef_z, shift, split, count, owner, local):
     vmem = pl.BlockSpec(memory_space=pltpu.VMEM)
     anywhere = pl.BlockSpec(memory_space=pl.ANY)
-    cells = pltpu.VMEM((NX, NY, ROWS), F32)
+    cells = pltpu.VMEM((NX, NY, 8, ROWS), F32)
     rows = pltpu.VMEM((LINE, COARSE, KV, ROWS), BF16)
     dma = pltpu.SemaphoreType.DMA
     return pl.pallas_call(

time: 59.7 us -> 59 us (0.988)
  Pallas kernels: 58.9 us -> 58.2 us
    pallas_call x1, Pallas kernels: 56.6 us -> 55.9 us  [smooth(): pl.pallas_call(smooth_kernel, out_shape=(jax.ShapeDtypeStruct((VECS, NX,...]
where the time goes in v19:
time: 59 us; the launch traced here: 58.8 us
  Pallas kernels  58.2 us (99%)
  between operations  0.64 us (1%)
    pallas_call x1, Pallas kernels, smooth(): pl.pallas_call(smooth_kernel, out_shape=(jax.ShapeDtypeStruct((VECS, NX,...  55.9 us
    pallas_call x1, Pallas kernels, pass_on_results(): pl.pallas_call(pass_kernel, out_shape=(jax.ShapeDtypeStruct(weights.shape...  2.32 us

profile of v19, /device:TPU:1, one launch (start us, length us, event | category | flops | bytes accessed | tf_op | source)
XLA Modules:
  0.0 58.8 jit_solution(18308652008757393546)
XLA Ops:
  0.6 55.9 %smooth.1 = (f32[48,4,16,128]{3,2,1,0:T(8,128)}, f32[4,64,128]{2,1,0:T(8,128)}) custom-call(f32[48,4,16,128]{3,2,1,0:T(8,128)} %tv.1, f32[4,16,128]{2,1,0:T(8,128)} %cx.1, f32[4,16,128]{2,1,0:T(8,128)} %cy.1, f32[4,16,128]{2,1,0:T(8,128)} %cz.1, f32[4,16,128]{2,1,0:T(8,128)} %sh.1, s32[4,1,16]{2,1,0:T(1,128)} %bitcast.20, s32[4,1,16]{2,1,0:T(1,128)} %bitcast.21, ...), custom_call_target="tpu_custom_call" | custom-call | tf_op jit(solution)/shard_map/smooth/pallas_call | solution.py:648
  56.5 2.3 %fit.1 = (f32[4,4,16,128]{3,2,1,0:T(8,128)}, f32[48,4,16,128]{3,2,1,0:T(8,128)}) custom-call(f32[4,4,16,128]{3,2,1,0:T(8,128)} %bitcast.17, f32[48,4,16,128]{3,2,1,0:T(8,128)} %get-tuple-element.7.sm_in), custom_call_target="tpu_custom_call" | custom-call | tf_op jit(solution)/shard_map/fit/pallas_call | solution.py:731

commit v20 on v19

--- a/solution.py
+++ b/solution.py
@@ -133,11 +133,11 @@
 
 def smooth_kernel(
     tv, cx, cy, cz, sh, split, count, owner, local, sm_out, w_out,
-    split_v, count_v, owner_v, local_v, meta, tgt, tgt_s, blk, rb0, rb1, rb2, part_sums,
+    split_v, count_v, owner_v, local_v, meta, tgt, tgt_s, blk, rb0, rb1, rb2, part_sums, w_hold,
     stage, coef, wa, wb, ka, kb, km, kp, fxs, fxr, fys, fyr,
     pair, lines, near, far, block_cols, idv, line_s, id_s, fine_s, spot_s, p00, p01, p02, p03, p10, p11, p12, p13, p20, p21, p22, p23, sb,
     in_sem, coef_sem, out_sem, send_sem, recv_sem, pair_sem, table_sem, gather_sem,
-    near_sem, cast_send, cast_recv, ans_send, ans_recv, own_sem, smem_sem, list_sem,
+    near_sem, cast_send, cast_recv, ans_send, ans_recv, own_sem, smem_sem, list_sem, w_sem,
 ):
     cells = (split_v, count_v, owner_v, local_v)
     rb = (rb0, rb1, rb2)
@@ -484,6 +484,10 @@
 
         lax.fori_loop(0, FINE // 4, step, 0)
 
+    def w_copy(g):
+        rows = pl.ds(pl.multiple_of(g * 8, 8), 8)
+        return pltpu.make_async_copy(w_hold.at[:, rows], w_out.at[:, rows], w_sem.at[g])
+
     def finish():
         sub = lax.broadcasted_iota(jnp.int32, (8, ROWS), 0)
         low4, low2, low1 = sub < 4, (sub & 2) == 0, (sub & 1) == 0
@@ -509,10 +513,13 @@
                     total[couple] = total[couple] + RIDGE
             out = solve_rows(total, [total[s, SLOTS] for s in range(SLOTS)])
             for s in range(SLOTS):
-                w_out[s, pl.ds(pl.multiple_of(g * 8, 8), 8), :] = out[s]
+                w_hold[s, pl.ds(pl.multiple_of(g * 8, 8), 8), :] = out[s]
+            w_copy(g).start()
             return carry
 
         lax.fori_loop(0, SITES // 8, group, 0)
+        for g in range(SITES // 8):
+            w_copy(g).wait()
 
     stores = []
 
@@ -610,18 +617,10 @@
         pass_on(c)
     for c in (1, 2, 0):
         reply(c, 0)
-    for c in (1, 0, 2):
+    for c in GRAM_ORDER:
         reply(c, 1)
     for c in range(CHUNKS):
         transpose_out(c, wb)
-    tgt_copy.wait()
-    for c in GRAM_ORDER:
-        for part in range(len(PARTS)):
-            answer(c, part, 0, 0).wait()
-            drain(sb.at[c, pl.ds(0, 7 * PARTS[part][1] * SPOT)], ans_recv.at[c, part])
-        add_products(c)
-    finish()
-
     drain(fxs, send_sem.at[0])
     drain(fys, send_sem.at[1])
     pair_copy().wait_send()
@@ -632,11 +631,18 @@
         drain(pg[c][0].at[pl.ds(0, 3)], near_sem.at[c, 0])
         for n in range(3):
             drain(pg[c][0], cast_send.at[c, n])
+    tgt_copy.wait()
+    for c in GRAM_ORDER:
+        for part in range(len(PARTS)):
+            answer(c, part, 0, 0).wait()
+            drain(sb.at[c, pl.ds(0, 7 * PARTS[part][1] * SPOT)], ans_recv.at[c, part])
+        add_products(c)
         for part in range(len(PARTS)):
             count = PARTS[part][1]
             drain(sb.at[c, pl.ds(0, 7 * count * SPOT)], ans_send.at[c, part])
     for store in stores:
         store.wait()
+    finish()
 
 
 def smooth(test_vectors, coef_x, coef_y, coef_z, shift, split, count, owner, local):
@@ -652,7 +658,7 @@
             jax.ShapeDtypeStruct((SLOTS, SITES, ROWS), F32),
         ),
         in_specs=[anywhere] * 9,
-        out_specs=(anywhere, vmem),
+        out_specs=(anywhere, anywhere),
         scratch_shapes=[
             pltpu.VMEM((NX, 1, NY), jnp.int32),
             pltpu.VMEM((NX, 1, NY), jnp.int32),
@@ -664,6 +670,7 @@
             pltpu.VMEM((CHUNKS, SITES, KV, ROWS), BF16),
             *([pltpu.VMEM((EMPTY + 8, KV, ROWS), BF16)] * CHUNKS),
             pltpu.VMEM((len(PAIRS), SITES, 8, ROWS), F32),
+            pltpu.VMEM((SLOTS, SITES, ROWS), F32),
             pltpu.VMEM((VECS, NX, NY, ROWS), F32),
             pltpu.VMEM((4, NX, NY, ROWS), F32),
             pltpu.VMEM((CHUNKS, EXT, ROWS), F32),
@@ -701,6 +708,7 @@
             dma((CHUNKS, len(PARTS))),
             dma((5,)),
             dma((4,)),
+            dma((SITES // 8,)),
         ],
         compiler_params=pltpu.CompilerParams(
             collective_id=0, has_side_effects=True, vmem_limit_bytes=60 * 1024 * 1024

time: 59 us -> 59 us (level)
  no operation moved by 1% of the time
where the time goes in v20:
time: 59 us; the launch traced here: 58.8 us
  Pallas kernels  58.2 us (99%)
  between operations  0.64 us (1%)
    pallas_call x1, Pallas kernels, smooth(): pl.pallas_call(smooth_kernel, out_shape=(jax.ShapeDtypeStruct((VECS, NX,...  55.9 us
    pallas_call x1, Pallas kernels, pass_on_results(): pl.pallas_call(pass_kernel, out_shape=(jax.ShapeDtypeStruct(weights.shape...  2.32 us

profile of v20, /device:TPU:1, one launch (start us, length us, event | category | flops | bytes accessed | tf_op | source)
XLA Modules:
  0.0 58.8 jit_solution(16878770327916514639)
XLA Ops:
  0.6 55.9 %smooth.1 = (f32[48,4,16,128]{3,2,1,0:T(8,128)}, f32[4,64,128]{2,1,0:T(8,128)}) custom-call(f32[48,4,16,128]{3,2,1,0:T(8,128)} %tv.1, f32[4,16,128]{2,1,0:T(8,128)} %cx.1, f32[4,16,128]{2,1,0:T(8,128)} %cy.1, f32[4,16,128]{2,1,0:T(8,128)} %cz.1, f32[4,16,128]{2,1,0:T(8,128)} %sh.1, s32[4,1,16]{2,1,0:T(1,128)} %bitcast.20, s32[4,1,16]{2,1,0:T(1,128)} %bitcast.21, ...), custom_call_target="tpu_custom_call" | custom-call | tf_op jit(solution)/shard_map/smooth/pallas_call | solution.py:654
  56.5 2.3 %fit.1 = (f32[4,4,16,128]{3,2,1,0:T(8,128)}, f32[48,4,16,128]{3,2,1,0:T(8,128)}) custom-call(f32[4,4,16,128]{3,2,1,0:T(8,128)} %bitcast.17, f32[48,4,16,128]{3,2,1,0:T(8,128)} %get-tuple-element.7.sm_in), custom_call_target="tpu_custom_call" | custom-call | tf_op jit(solution)/shard_map/fit/pallas_call | solution.py:739

commit v21 on v20

--- a/solution.py
+++ b/solution.py
@@ -431,10 +431,17 @@
             for t, tile in enumerate(tiles):
                 sb[c, slot * REPLY + place * SPOT + t] = tile
 
+    def pack_own(c):
+        def one(n, carry):
+            pack(c, n // CORES, lax.rem(n, CORES), (0,))
+            return carry
+
+        lax.fori_loop(0, LINE * CORES, one, 0)
+
     def reply(c, part):
         drain(pg[c][0], cast_recv.at[c, 2 + part])
         first, count = PARTS[part]
-        places = range(first, first + count)
+        places = range(max(first, 1), first + count)
 
         def to_other_chip(n, carry):
             k, e = n // CORES, lax.rem(n, CORES)
@@ -613,6 +620,8 @@
     cast(1)
     cast(2)
     line_copy.wait()
+    for c in range(CHUNKS):
+        pack_own(c)
     for c in range(CHUNKS):
         pass_on(c)
     for c in (1, 2, 0):

time: 59 us -> 59.3 us (level)
  no operation moved by 1% of the time
where the time goes in v21:
time: 59.3 us; the launch traced here: 59.1 us
  Pallas kernels  58.5 us (99%)
  between operations  0.64 us (1%)
    pallas_call x1, Pallas kernels, smooth(): pl.pallas_call(smooth_kernel, out_shape=(jax.ShapeDtypeStruct((VECS, NX,...  56.2 us
    pallas_call x1, Pallas kernels, pass_on_results(): pl.pallas_call(pass_kernel, out_shape=(jax.ShapeDtypeStruct(weights.shape...  2.32 us

profile of v21, /device:TPU:1, one launch (start us, length us, event | category | flops | bytes accessed | tf_op | source)
XLA Modules:
  0.0 59.1 jit_solution(16789717170798500382)
XLA Ops:
  0.6 56.2 %smooth.1 = (f32[48,4,16,128]{3,2,1,0:T(8,128)}, f32[4,64,128]{2,1,0:T(8,128)}) custom-call(f32[48,4,16,128]{3,2,1,0:T(8,128)} %tv.1, f32[4,16,128]{2,1,0:T(8,128)} %cx.1, f32[4,16,128]{2,1,0:T(8,128)} %cy.1, f32[4,16,128]{2,1,0:T(8,128)} %cz.1, f32[4,16,128]{2,1,0:T(8,128)} %sh.1, s32[4,1,16]{2,1,0:T(1,128)} %bitcast.20, s32[4,1,16]{2,1,0:T(1,128)} %bitcast.21, ...), custom_call_target="tpu_custom_call" | custom-call | tf_op jit(solution)/shard_map/smooth/pallas_call | solution.py:663
  56.8 2.3 %fit.1 = (f32[4,4,16,128]{3,2,1,0:T(8,128)}, f32[48,4,16,128]{3,2,1,0:T(8,128)}) custom-call(f32[4,4,16,128]{3,2,1,0:T(8,128)} %bitcast.17, f32[48,4,16,128]{3,2,1,0:T(8,128)} %get-tuple-element.7.sm_in), custom_call_target="tpu_custom_call" | custom-call | tf_op jit(solution)/shard_map/fit/pallas_call | solution.py:748

commit v22 on v20

--- a/solution.py
+++ b/solution.py
@@ -182,17 +182,6 @@
     greeted = 3 + len(AXES) * (LINE - 1) * CORES
     for load in loads[1:]:
         load.start()
-    coef_loads = []
-    for n, part in enumerate((cx, cy, cz, sh)):
-        load = pltpu.make_async_copy(part, coef.at[n], coef_sem.at[n])
-        load.start()
-        coef_loads.append(load)
-    lists = []
-    for n, part in enumerate((split, count, owner, local)):
-        load = pltpu.make_async_copy(part, cells[n], list_sem.at[n])
-        load.start()
-        lists.append(load)
-
     keep = (
         (i > 0).astype(F32),
         (i < GX - 1).astype(F32),
@@ -215,14 +204,19 @@
             )
         return out
 
-    def send_faces(s, c, w):
+    def send_x_faces(c, w):
         for side in range(2):
             x = side * (NX - 1)
-            fxs[s, c, side] = w[c, pl.ds(site_row(x, 0), NY * KV)].astype(BF16)
+            fxs[0, c, side] = w[c, pl.ds(site_row(x, 0), NY * KV)].astype(BF16)
+        for copy in copies(0, c)[:2]:
+            copy.start()
+
+    def send_y_faces(c, w):
+        for side in range(2):
             y = side * (NY - 1)
             for x in range(NX):
-                fys[s, c, side, pl.ds(x * KV, KV)] = w[c, pl.ds(site_row(x, y), KV)].astype(BF16)
-        for copy in copies(s, c):
+                fys[0, c, side, pl.ds(x * KV, KV)] = w[c, pl.ds(site_row(x, y), KV)].astype(BF16)
+        for copy in copies(0, c)[2:]:
             copy.start()
 
     def fill_halo(s, c, w):
@@ -448,11 +442,10 @@
             pack(c, 0, e, places)
             answer(c, part, 0, e).start()
 
-    def transpose_in(c):
-        loads[c].wait()
+    def transpose_in(c, planes):
 
         def one(k, carry):
-            for x in range(NX):
+            for x in planes:
                 for half in range(NY // 8):
                     wa[c, pl.ds(site_row(x, half * 8) + k, 8, stride=KV), :] = stage[
                         c * KV + k, x, pl.ds(half * 8, 8), :
@@ -539,11 +532,28 @@
         store.start()
         stores.append(store)
 
-    for c in range(CHUNKS):
-        transpose_in(c)
-        if c == 0:
-            pl.semaphore_wait(barrier, greeted)
-        send_faces(0, c, wa)
+    loads[0].wait()
+    transpose_in(0, (0, NX - 1))
+    pl.semaphore_wait(barrier, greeted)
+    send_x_faces(0, wa)
+    coef_loads = []
+    for n, part in enumerate((cx, cy, cz, sh)):
+        load = pltpu.make_async_copy(part, coef.at[n], coef_sem.at[n])
+        load.start()
+        coef_loads.append(load)
+    lists = []
+    for n, part in enumerate((split, count, owner, local)):
+        load = pltpu.make_async_copy(part, cells[n], list_sem.at[n])
+        load.start()
+        lists.append(load)
+
+    transpose_in(0, range(1, NX - 1))
+    send_y_faces(0, wa)
+    for c in range(1, CHUNKS):
+        loads[c].wait()
+        transpose_in(c, range(NX))
+        send_x_faces(c, wa)
+        send_y_faces(c, wa)
 
     for load in coef_loads:
         load.wait()

time: 59 us -> 59.1 us (level)
  no operation moved by 1% of the time
where the time goes in v22:
time: 59.1 us; the launch traced here: 58.8 us
  Pallas kernels  58.2 us (98%)
  between operations  0.64 us (1%)
    pallas_call x1, Pallas kernels, smooth(): pl.pallas_call(smooth_kernel, out_shape=(jax.ShapeDtypeStruct((VECS, NX,...  55.9 us
    pallas_call x1, Pallas kernels, pass_on_results(): pl.pallas_call(pass_kernel, out_shape=(jax.ShapeDtypeStruct(weights.shape...  2.32 us

profile of v22, /device:TPU:1, one launch (start us, length us, event | category | flops | bytes accessed | tf_op | source)
XLA Modules:
  0.0 58.8 jit_solution(2076913901439981115)
XLA Ops:
  0.6 55.9 %smooth.1 = (f32[48,4,16,128]{3,2,1,0:T(8,128)}, f32[4,64,128]{2,1,0:T(8,128)}) custom-call(f32[48,4,16,128]{3,2,1,0:T(8,128)} %tv.1, f32[4,16,128]{2,1,0:T(8,128)} %cx.1, f32[4,16,128]{2,1,0:T(8,128)} %cy.1, f32[4,16,128]{2,1,0:T(8,128)} %cz.1, f32[4,16,128]{2,1,0:T(8,128)} %sh.1, s32[4,1,16]{2,1,0:T(1,128)} %bitcast.20, s32[4,1,16]{2,1,0:T(1,128)} %bitcast.21, ...), custom_call_target="tpu_custom_call" | custom-call | tf_op jit(solution)/shard_map/smooth/pallas_call | solution.py:664
  56.5 2.3 %fit.1 = (f32[4,4,16,128]{3,2,1,0:T(8,128)}, f32[48,4,16,128]{3,2,1,0:T(8,128)}) custom-call(f32[4,4,16,128]{3,2,1,0:T(8,128)} %bitcast.17, f32[48,4,16,128]{3,2,1,0:T(8,128)} %get-tuple-element.7.sm_in), custom_call_target="tpu_custom_call" | custom-call | tf_op jit(solution)/shard_map/fit/pallas_call | solution.py:749

commit v23 on v20

--- a/solution.py
+++ b/solution.py
@@ -360,12 +360,10 @@
     def cast_copies(c):
         a, u, v = ROUTES[c]
         plan = (
-            (0, 0, 1, 3, 1, 0, 0),
-            (0, 0, 1, 1, 3, 1, 2),
-            (0, 1, 1, 3, 1, 0, 0),
+            (0, 0, 2, 3, 1, 0, 0),
             (0, 2, 2, 1, 3, 1, 1),
             (0, 2, 2, 3, 1, 0, 2),
-            (0, 1, 1, 1, 3, 1, 2),
+            (0, 0, 2, 1, 3, 1, 2),
             (3, 0, 2, 2, 1, 2, 3),
             (1, 2, 2, 2, 3, 2, 3),
         )
@@ -397,18 +395,18 @@
         a, u, v = ROUTES[c]
         for r in range(COARSE):
             pg[c][0][0, r] = blk[c, id_s[r, 0] & (SITES - 1)]
-        for copy in spread_copies(c) + cast_copies(c)[:2]:
+        for copy in spread_copies(c):
             copy.start()
 
     def cast(c):
         drain(pg[c][1].at[pl.ds(0, 3)], near_sem.at[c, 1])
-        for copy in cast_copies(c)[2:6]:
+        for copy in cast_copies(c)[:4]:
             copy.start()
 
     def pass_on(c):
         for n in range(2):
             drain(pg[c][0].at[pl.ds(0, 2)], cast_recv.at[c, n])
-            cast_copies(c)[6 + n].start()
+            cast_copies(c)[4 + n].start()
 
     def pack(c, d, e, places):
         a, u, v = ROUTES[c]

time: 59 us -> 60.8 us (1.031)
  Pallas kernels: 58.2 us -> 60 us
    pallas_call x1, Pallas kernels: 55.9 us -> 57.7 us  [smooth(): pl.pallas_call(smooth_kernel, out_shape=(jax.ShapeDtypeStruct((VECS, NX,...]
where the time goes in v23:
time: 60.8 us; the launch traced here: 60.6 us
  Pallas kernels  60 us (99%)
  between operations  0.64 us (1%)
    pallas_call x1, Pallas kernels, smooth(): pl.pallas_call(smooth_kernel, out_shape=(jax.ShapeDtypeStruct((VECS, NX,...  57.7 us
    pallas_call x1, Pallas kernels, pass_on_results(): pl.pallas_call(pass_kernel, out_shape=(jax.ShapeDtypeStruct(weights.shape...  2.32 us

profile of v23, /device:TPU:1, one launch (start us, length us, event | category | flops | bytes accessed | tf_op | source)
XLA Modules:
  0.0 60.6 jit_solution(5791357468133945435)
XLA Ops:
  0.6 57.7 %smooth.1 = (f32[48,4,16,128]{3,2,1,0:T(8,128)}, f32[4,64,128]{2,1,0:T(8,128)}) custom-call(f32[48,4,16,128]{3,2,1,0:T(8,128)} %tv.1, f32[4,16,128]{2,1,0:T(8,128)} %cx.1, f32[4,16,128]{2,1,0:T(8,128)} %cy.1, f32[4,16,128]{2,1,0:T(8,128)} %cz.1, f32[4,16,128]{2,1,0:T(8,128)} %sh.1, s32[4,1,16]{2,1,0:T(1,128)} %bitcast.20, s32[4,1,16]{2,1,0:T(1,128)} %bitcast.21, ...), custom_call_target="tpu_custom_call" | custom-call | tf_op jit(solution)/shard_map/smooth/pallas_call | solution.py:652
  58.3 2.3 %fit.1 = (f32[4,4,16,128]{3,2,1,0:T(8,128)}, f32[48,4,16,128]{3,2,1,0:T(8,128)}) custom-call(f32[4,4,16,128]{3,2,1,0:T(8,128)} %bitcast.17, f32[48,4,16,128]{3,2,1,0:T(8,128)} %get-tuple-element.7.sm_in), custom_call_target="tpu_custom_call" | custom-call | tf_op jit(solution)/shard_map/fit/pallas_call | solution.py:737
